TPU v7x, 32 devices: a whole 2x2x4 slice. The times are simulated.
32 devices in a mesh: dp: 4 (over y, x), section: 4 (over z), group: 2 (over core).
Axes of the slice: x: 2, y: 2, z: 4, core: 2. Of those that a mesh axis runs over, the one named last changes fastest.
Arguments:
- tokens_in: bfloat16 [1024, 4096], P(('dp', 'group')), may hold values from -6 to 6
- cotangent: bfloat16 [1024, 4096], P(('dp', 'group')), may hold values from -6 to 6
- gains: float32 [4, 4096], P('section'), may hold values from 0.5 to 1.5
- w_qkv: bfloat16 [4, 4096, 384], P('section'), may hold values from -0.09375 to 0.09375
- w_out: bfloat16 [4, 128, 4096], P('section'), may hold values from -0.5 to 0.5
- segments: int32 [64, 16], P(('dp', 'group')), may hold values from 0 to 3, never falling along the last dimension, each value on 1 to 8 neighbouring positions
- plan: int32 [8, 8], P(('dp', 'group')), may hold values from 0 to 7, each once within a row
Outputs:
- input_grads: bfloat16 [4, 1024, 4096], P('section', ('dp', 'group'))
- gain_grads: float32 [4, 4096], P('section')
Inputs may be any that keep to these rules, and one draw needn't show every extreme that they name: Each row of plan names every one of 0 .. 7 once. `segments`: segment numbers never fall along a row and every episode lies within one row.
All inputs are finite; a program needn't handle non-finite values.
Results may differ from a plain program's by a relative error of at most 0.029.
Values may be sent and summed in bfloat16 or wider, within the bound.
No kernel may reach another device: no remote copies, remote signals or barrier semaphores. Data moves between devices by JAX's collectives and lax.ppermute only.
A program may use at most 64 MiB of HBM per device.

v0:
```python
import math

import jax
import jax.numpy as jnp
from jax import lax
from jax.experimental import pallas as pl
from jax.experimental.pallas import tpu as pltpu
from jax.sharding import PartitionSpec as P

EPS = 1e-05
VMEM_BYTES = 24 * 1024 * 1024
SMALL = 16 * 1024 * 1024
F32 = jnp.float32
BF16 = jnp.bfloat16


def dot_nn(a, b):
    return lax.dot_general(a, b, (((1,), (0,)), ((), ())), preferred_element_type=F32)


def dot_nt(a, b):
    return lax.dot_general(a, b, (((1,), (1,)), ((), ())), preferred_element_type=F32)


def dot_tn(a, b):
    return lax.dot_general(a, b, (((0,), (0,)), ((), ())), preferred_element_type=F32)


IN_HBM = pl.BlockSpec(memory_space=pltpu.HBM)
ANYWHERE = pl.BlockSpec(memory_space=pl.ANY)
IN_VMEM = pl.BlockSpec(memory_space=pltpu.VMEM)
IN_SMEM = pl.BlockSpec(memory_space=pltpu.SMEM)


def in_hbm(array):
    return pltpu.with_memory_space_constraint(array, pltpu.HBM)


def in_vmem(array):
    return pltpu.with_memory_space_constraint(array, pltpu.VMEM)


def mover(sems):
    used = []

    def start(source, target):
        copy = pltpu.make_async_copy(source, target, sems.at[len(used)])
        copy.start()
        used.append(copy)
        return copy

    return start


def steps(width):
    step = min(width, 1024)
    return [slice(at, at + step) for at in range(0, width, step)]


def params(limit=VMEM_BYTES):
    return pltpu.CompilerParams(vmem_limit_bytes=limit)


def pick(tokens, plan, place, groups, out_layer, mine, slice_rows):
    rows, length, width = tokens.shape
    share = rows // groups

    def kernel(plan_ref, place_ref, mine_ref, tokens_ref, o_ref, *rest):
        slice_ref, parts = rest[0], rest[1 : 1 + groups]
        slice_in, rows_in, sems = rest[1 + groups :]
        start = mover(sems)
        at = pl.ds(pl.multiple_of(mine_ref[0] * slice_rows, slice_rows), slice_rows)
        loads = [(start(o_ref.at[at], slice_in), slice_in, slice_ref)]
        for r in range(groups):
            target = lax.rem(place_ref[0] + r, groups)
            for c in range(share):
                here = rows_in.at[r * share + c]
                row = plan_ref[0, target * share + c]
                loads.append((start(tokens_ref.at[row], here), here, parts[r].at[c]))
        stores = []
        for load, here, there in loads:
            load.wait()
            stores.append(start(here, there))
        for store in stores:
            store.wait()

    return pl.pallas_call(
        kernel,
        out_shape=[pltpu.HBM((slice_rows, width), BF16)]
        + [pltpu.HBM((share, length, width), BF16)] * groups,
        in_specs=[IN_SMEM, IN_SMEM, IN_SMEM, IN_HBM, IN_HBM],
        out_specs=[IN_HBM] * (1 + groups),
        scratch_shapes=[
            pltpu.VMEM((slice_rows, width), BF16),
            pltpu.VMEM((rows, length, width), BF16),
            pltpu.SemaphoreType.DMA((2 * rows + 2,)),
        ],
        compiler_params=params(),
        name="pick",
    )(plan, place, mine, in_hbm(tokens), in_hbm(out_layer))


def project(parts, cotangent, gain, w_layer, out_layer, place, after):
    groups = len(parts)
    tokens, width = cotangent.shape
    head = out_layer.shape[0]
    wide = w_layer.shape[1]
    block = tokens // groups
    cuts = steps(width)
    copies = len(cuts) * (groups + 4)

    def kernel(place_ref, *refs):
        part_refs = refs[:groups]
        cot_ref, g_ref, w_ref, o_ref = refs[groups : groups + 4]
        x_ref, xz_ref, n_ref = refs[groups + 4 + len(after) : groups + 7 + len(after)]
        x_in, c_in, w_in, o_in, sems = refs[groups + 7 + len(after) :]
        start = mover(sems)
        loads = []
        for cut in cuts:
            mine = [start(w_ref.at[cut], w_in.at[cut])]
            mine.append(start(o_ref.at[:, cut], o_in.at[:, cut]))
            for r in range(groups):
                source = lax.rem(place_ref[0] + groups - r, groups)
                rows = pl.ds(pl.multiple_of(source * block, block), block)
                mine.append(start(part_refs[r].at[:, cut], x_in.at[rows, cut]))
            mine.append(start(cot_ref.at[:, cut], c_in.at[:, cut]))
            loads.append(mine)
        through = jnp.zeros((tokens, wide), F32)
        across = jnp.zeros((tokens, head), F32)
        back = jnp.zeros((tokens, head), F32)
        square = jnp.zeros((tokens, 1), F32)
        stores = []
        for cut, mine in zip(cuts, loads):
            for load in mine:
                load.wait()
            stores.append(start(x_in.at[:, cut], x_ref.at[:, cut]))
            x = x_in[:, cut]
            xf = x.astype(F32)
            through += dot_nn((xf * g_ref[:, cut]).astype(BF16), w_in[cut, :])
            across += dot_nt(x, o_in[:, cut])
            back += dot_nt(c_in[:, cut], o_in[:, cut])
            square += jnp.sum(xf * xf, axis=1, keepdims=True)
        xz_ref[:, :wide] = through.astype(BF16)
        xz_ref[:, wide : wide + head] = across.astype(BF16)
        xz_ref[:, wide + head :] = back.astype(BF16)
        n_ref[...] = square
        for store in stores:
            store.wait()

    return pl.pallas_call(
        kernel,
        out_shape=[
            pltpu.HBM((tokens, width), BF16),
            jax.ShapeDtypeStruct((tokens, wide + 2 * head), BF16),
            jax.ShapeDtypeStruct((tokens, 1), F32),
        ],
        in_specs=[IN_SMEM]
        + [ANYWHERE] * groups
        + [IN_HBM, IN_VMEM, IN_HBM, IN_HBM]
        + [ANYWHERE] * len(after),
        out_specs=[IN_HBM, IN_VMEM, IN_VMEM],
        scratch_shapes=[
            pltpu.VMEM((tokens, width), BF16),
            pltpu.VMEM((tokens, width), BF16),
            pltpu.VMEM((width, wide), BF16),
            pltpu.VMEM((head, width), BF16),
            pltpu.SemaphoreType.DMA((copies,)),
        ],
        compiler_params=params(),
        name="project",
    )(
        place,
        *parts,
        in_hbm(cotangent),
        gain,
        in_hbm(w_layer),
        in_hbm(out_layer),
        *after,
    )


def couple(slices, gain, w_layer, out_layer, last, after):
    sections = len(slices)
    count, width = slices[0].shape
    head = out_layer.shape[0]
    wide = w_layer.shape[1]
    below = (sections - 2) * wide
    packed = below + max(wide, (sections - 1) * head)
    cuts = steps(width)
    copies = len(cuts) * (sections + 2) + sections - 1

    def kernel(last_ref, *refs):
        s_refs = refs[:sections][::-1]
        g_ref, w_ref, o_ref = refs[sections : sections + 3]
        out_ref, stack_ref, r_in, w_in, o_in, sems = refs[sections + 3 + len(after) :]
        rows = [slice(r * count, (r + 1) * count) for r in range(sections)]
        start = mover(sems)
        loads = []
        for cut in cuts:
            mine = [start(w_ref.at[cut], w_in.at[cut])]
            mine.append(start(o_ref.at[:, cut], o_in.at[:, cut]))
            for r in range(sections):
                mine.append(start(s_refs[r].at[:, cut], r_in.at[rows[r], cut]))
            loads.append(mine)
        through = jnp.zeros((sections * count, wide), F32)
        across = jnp.zeros((sections * count, head), F32)
        for cut, mine in zip(cuts, loads):
            for load in mine:
                load.wait()
            r = r_in[:, cut]
            through += dot_nn((r.astype(F32) * g_ref[:, cut]).astype(BF16), w_in[cut, :])
            across += dot_nt(r, o_in[:, cut])
        stores = [start(r_in.at[rows[r]], stack_ref.at[r - 1]) for r in range(1, sections)]
        through = through.astype(BF16)
        across = across.astype(BF16)
        out_ref[...] = jnp.zeros_like(out_ref)
        for r in range(1, sections - 1):
            out_ref[:, (r - 1) * wide : r * wide] = through[rows[r]]

        @pl.when(last_ref[0] == 1)
        def _():
            out_ref[:, below : below + wide] = through[rows[-1]]

        @pl.when(last_ref[0] == 0)
        def _():
            for r in range(sections - 1):
                out_ref[:, below + r * head : below + (r + 1) * head] = across[rows[r]]

        for store in stores:
            store.wait()

    return pl.pallas_call(
        kernel,
        out_shape=[
            jax.ShapeDtypeStruct((count, packed), BF16),
            pltpu.HBM((sections - 1, count, width), BF16),
        ],
        in_specs=[IN_SMEM]
        + [ANYWHERE] * sections
        + [IN_VMEM, IN_HBM, IN_HBM]
        + [ANYWHERE] * len(after),
        out_specs=[IN_VMEM, IN_HBM],
        scratch_shapes=[
            pltpu.VMEM((sections * count, width), BF16),
            pltpu.VMEM((width, wide), BF16),
            pltpu.VMEM((head, width), BF16),
            pltpu.SemaphoreType.DMA((copies,)),
        ],
        compiler_params=params(),
        name="couple",
    )(last, *slices[::-1], gain, in_hbm(w_layer), in_hbm(out_layer), *after)


def layout(sections, wide, head):
    through, across, at = {}, {}, 0
    for k in range(sections):
        for j in range(k):
            through[j, k] = slice(at, at + wide)
            at += wide
        for j in range(k + 1 if k < sections - 1 else 0):
            across[j, k] = slice(at, at + head)
            at += head
    return through, across, at


def compact(parts, section, wide, head, after):
    sections = len(parts)
    count = parts[0].shape[0]
    below = (sections - 2) * wide
    through, across, total = layout(sections, wide, head)

    def kernel(s_ref, *refs):
        part_refs, out_ref = refs[:sections], refs[-1]
        mine = s_ref[0]

        def fill(k, r):
            for j in range(k):
                at = (k - j - 1) * wide
                out_ref[0, :, through[j, k]] = part_refs[r][:, at : at + wide]
            for j in range(k + 1 if k < sections - 1 else 0):
                at = below + (k - j) * head
                out_ref[0, :, across[j, k]] = part_refs[r][:, at : at + head]

        for s in range(sections):

            @pl.when(mine == s)
            def _(s=s):
                for r in range(sections):
                    fill((s - r) % sections, r)

    vmem = pl.BlockSpec(memory_space=pltpu.VMEM)
    return pl.pallas_call(
        kernel,
        out_shape=jax.ShapeDtypeStruct((1, count, total), BF16),
        in_specs=[IN_SMEM] + [vmem] * sections + [ANYWHERE] * len(after),
        out_specs=vmem,
        compiler_params=params(SMALL),
        name="compact",
    )(section, *parts, *after)


def merge(first, second, after):
    count = first.shape[0]

    def kernel(first_ref, second_ref, *refs):
        refs[-1][:count] = first_ref[...]
        refs[-1][count:] = second_ref[...]

    return pl.pallas_call(
        kernel,
        out_shape=jax.ShapeDtypeStruct((2 * count,) + first.shape[1:], first.dtype),
        in_specs=[IN_VMEM] * 2 + [ANYWHERE] * len(after),
        out_specs=IN_VMEM,
        compiler_params=params(SMALL),
        name="merge",
    )(first, second, *after)


def serial(xz, pieces, places, norms, mask, section, gain, w_layer, out_layer, streams):
    sections = len(xz)
    tokens = norms.shape[0]
    head, width = out_layer.shape
    wide = 3 * head
    scale = 1.0 / math.sqrt(head)
    lead = slice(0, streams[-1].stop)
    through_at, across_at, _ = layout(sections, wide, head)
    count, packed = pieces[0].shape[-2:]
    plane = head // count
    n_in = sections + len(pieces)
    copies = sections + plane + 2

    def kernel(s_ref, p_ref, *refs):
        xz_refs, piece_refs = refs[:sections], refs[sections:n_in]
        n_ref, mask_ref, g_ref, w_ref, o_ref = refs[n_in : n_in + 5]
        n_out = n_in + 5
        v_ref, t_ref, a_ref = refs[n_out : n_out + 3]
        first_refs = refs[n_out + 3 : n_out + 3 + len(streams)]
        scratch = refs[n_out + 3 + len(streams) :]
        xz_all, table, mixes, weights, projs, dmix, w_in, o_in, sems = scratch
        mine = s_ref[0]
        started = []

        def start(source, target):
            copy = pltpu.make_async_copy(source, target, sems.at[len(started)])
            copy.start()
            started.append(copy)

        for r in range(sections):
            start(xz_refs[r], xz_all.at[mine ^ r])
        at = 0
        for ref in piece_refs:
            for i in range(ref.shape[0]):
                start(ref.at[i], table.at[p_ref[at]])
                at += 1
        small = list(started)
        start(w_ref.at[lead], w_in)
        start(o_ref.at[:, lead], o_in)
        for copy in small:
            copy.wait()

        def through(j, k):
            return table[:, :, through_at[j, k]].reshape(head, wide)

        def across(j, k):
            return table[:, :, across_at[j, k]].reshape(head, head)

        allowed = mask_ref[...] > 0.5
        norm = n_ref[...]
        rstds, tails, mixed = [], [], []
        for s in range(sections):
            proj = xz_all[s, :, :wide].astype(F32)
            for j in range(s):
                proj = proj + dot_nn(mixed[j], through(j, s))
            rstd = lax.rsqrt(norm * (1.0 / width) + EPS)
            proj = proj * rstd
            projs[s] = proj.astype(BF16)
            q, k, v = (projs[s, :, i * head : (i + 1) * head] for i in range(3))
            scores = jnp.where(allowed, dot_nt(q, k) * scale, -1e30)
            scores = jnp.exp(scores - jnp.max(scores, axis=1, keepdims=True))
            soft = scores / jnp.sum(scores, axis=1, keepdims=True)
            weights[s] = soft
            mix = dot_nn(soft.astype(BF16), v).astype(BF16)
            mixed.append(mix)
            mixes[:, s * head : (s + 1) * head] = mix
            rstds.append(rstd)
            dmix[:, s * head : (s + 1) * head] = xz_all[s, :, wide + head :].astype(F32)
            if s == sections - 1:
                break
            y = xz_all[s, :, wide : wide + head].astype(F32)
            for j in range(s):
                y = y + dot_nn(mixed[j], across(j, s))
            tail = y + dot_nn(mix, across(s, s))
            norm = norm + jnp.sum(mix.astype(F32) * (y + tail), axis=1, keepdims=True)
            norm = jnp.maximum(norm, 0.0)
            tails.append(tail)
        total = jnp.zeros((tokens, 1), F32)
        a_ref[...] = jnp.zeros_like(a_ref)
        for s in reversed(range(sections)):
            cols = slice(s * head, (s + 1) * head)
            da = dmix[:, cols]
            if s < sections - 1:
                da = da - total * tails[s]
            da = da.astype(BF16)
            q, k, v = (projs[s, :, i * head : (i + 1) * head] for i in range(3))
            soft = weights[s]
            dv = dot_tn(soft.astype(BF16), da)
            dsoft = dot_nt(da, v)
            dscore = soft * (dsoft - jnp.sum(dsoft * soft, axis=1, keepdims=True))
            dscore = (dscore * scale).astype(BF16)
            dproj = jnp.concatenate([dot_nn(dscore, k), dot_tn(dscore, q), dv], axis=1)
            along = jnp.sum(dproj * projs[s].astype(F32), axis=1, keepdims=True)
            first = (dproj * rstds[s]).astype(BF16)
            second = (-total * mixes[:, cols].astype(F32)).astype(BF16)
            total = total + rstds[s] * rstds[s] * along * (1.0 / width)
            for j in reversed(range(s)):
                term = dot_nt(first, through(j, s))
                if s < sections - 1:
                    term = term + dot_nt(second, across(j, s))
                dmix[:, j * head : (j + 1) * head] += term

            @pl.when(mine == s)
            def _(first=first, second=second, total=total):
                v_ref[:, :wide] = first
                v_ref[:, wide:] = second
                t_ref[...] = total

            for r in range(1, sections - s):

                @pl.when(mine == s + r)
                def _(r=r, cols=cols):
                    a_ref[:, (r - 1) * head : r * head] = mixes[:, cols]

        for copy in started[len(small) :]:
            copy.wait()
        own = dot_nt(v_ref[:, :wide], w_in[...]) * g_ref[:, lead]
        own = (own + dot_nn(v_ref[:, wide:], o_in[...])).astype(BF16)
        for ref, part in zip(first_refs, streams):
            ref[...] = own[:, part]

    vmem = pl.BlockSpec(memory_space=pltpu.VMEM)
    smem = pl.BlockSpec(memory_space=pltpu.SMEM)
    return pl.pallas_call(
        kernel,
        out_shape=[
            pltpu.VMEM((tokens, wide + head), BF16),
            pltpu.VMEM((tokens, 1), F32),
            pltpu.VMEM((tokens, (sections - 1) * head), BF16),
        ]
        + [pltpu.VMEM((tokens, part.stop - part.start), BF16) for part in streams],
        in_specs=[smem, smem] + [ANYWHERE] * n_in + [vmem, vmem, vmem, IN_HBM, IN_HBM],
        out_specs=[vmem] * (3 + len(streams)),
        scratch_shapes=[
            pltpu.VMEM((sections,) + xz[0].shape, BF16),
            pltpu.VMEM((plane, count, packed), BF16),
            pltpu.VMEM((tokens, sections * head), BF16),
            pltpu.VMEM((sections, tokens, tokens), F32),
            pltpu.VMEM((sections, tokens, wide), BF16),
            pltpu.VMEM((tokens, sections * head), F32),
            pltpu.VMEM((lead.stop, wide), BF16),
            pltpu.VMEM((head, lead.stop), BF16),
            pltpu.SemaphoreType.DMA((copies,)),
        ],
        compiler_params=params(),
        name="serial",
    )(
        section,
        places,
        *xz,
        *pieces,
        norms,
        mask,
        gain,
        in_hbm(w_layer),
        in_hbm(out_layer),
    )


def hold(array, after):
    def kernel(*refs):
        pass

    return pl.pallas_call(
        kernel,
        out_shape=jax.ShapeDtypeStruct(array.shape, array.dtype),
        in_specs=[ANYWHERE] * (1 + len(after)),
        out_specs=ANYWHERE,
        input_output_aliases={0: 0},
        compiler_params=params(SMALL),
        name="hold",
    )(array, *after)


def gather_two(first, second, after):
    count = first.shape[0]

    def kernel(first_ref, second_ref, *refs):
        out_ref, sems = refs[len(after) :]
        start = mover(sems)
        copies = [start(first_ref, out_ref.at[:count]), start(second_ref, out_ref.at[count:])]
        for copy in copies:
            copy.wait()

    return pl.pallas_call(
        kernel,
        out_shape=jax.ShapeDtypeStruct((2 * count,) + first.shape[1:], first.dtype),
        in_specs=[ANYWHERE] * (2 + len(after)),
        out_specs=IN_VMEM,
        scratch_shapes=[pltpu.SemaphoreType.DMA((2,))],
        compiler_params=params(SMALL),
        name="gather_two",
    )(first, second, *after)


def widen(sent, gain, w_layer, out_layer, chunk):
    tokens = sent.shape[0]
    head, width = out_layer.shape
    wide = w_layer.shape[1]
    cuts = [slice(at, at + chunk) for at in range(0, width, chunk)]

    def kernel(v_ref, g_ref, w_ref, o_ref, back_ref, pair_ref, back_in, w_in, o_in, sems):
        start = mover(sems)
        loads = [
            (start(w_ref.at[cut], w_in.at[cut]), start(o_ref.at[:, cut], o_in.at[:, cut]))
            for cut in cuts
        ]
        stores = []
        for i, (cut, mine) in enumerate(zip(cuts, loads)):
            for load in mine:
                load.wait()
            back = dot_nt(v_ref[:, :wide], w_in[cut, :])
            own = back * g_ref[:, cut] + dot_nn(v_ref[:, wide:], o_in[:, cut])
            back_in[:, cut] = back.astype(BF16)
            stores.append(start(back_in.at[:, cut], back_ref.at[:, cut]))
            pair_ref[0, i] = own.astype(BF16)
            pair_ref[1, i] = jnp.zeros_like(pair_ref[1, i])
        for store in stores:
            store.wait()

    return pl.pallas_call(
        kernel,
        out_shape=[
            pltpu.HBM((tokens, width), BF16),
            pltpu.VMEM((2, len(cuts), tokens, chunk), BF16),
        ],
        in_specs=[IN_VMEM, IN_VMEM, IN_HBM, IN_HBM],
        out_specs=[IN_HBM, IN_VMEM],
        scratch_shapes=[
            pltpu.VMEM((tokens, width), BF16),
            pltpu.VMEM((width, wide), BF16),
            pltpu.VMEM((head, width), BF16),
            pltpu.SemaphoreType.DMA((3 * len(cuts),)),
        ],
        compiler_params=params(),
        name="widen",
    )(in_vmem(sent), gain, in_hbm(w_layer), in_hbm(out_layer))


def settle(total, mixes, stacks, places, x, cotangent, back, chunk, part, parts):
    tokens, width = x.shape
    layers, rows = stacks[0].shape[1:3]
    entries = [(i, e) for i, stack in enumerate(stacks) for e in range(stack.shape[0])]
    plane = len(entries)
    head = plane * rows
    span = width // parts
    base = part * span
    cuts = [slice(at, at + chunk) for at in range(0, span, chunk)]
    copies = plane * layers + 3 * len(cuts)

    def kernel(p_ref, t_ref, a_ref, x_ref, c_ref, back_ref, *refs):
        stack_refs = refs[: len(stacks)]
        rest_ref, dg_ref = refs[len(stacks) : len(stacks) + 2]
        lower, x_in, c_in, back_in, sems = refs[len(stacks) + 2 :]
        start = mover(sems)
        first = []
        for at, (i, e) in enumerate(entries):
            for r in range(layers):
                here = pl.ds(base, span)
                first.append(start(stack_refs[i].at[e, r, :, here], lower.at[r, p_ref[at]]))
        loads = []
        for cut in cuts:
            there = pl.ds(base + cut.start, chunk)
            mine = [start(x_ref.at[:, there], x_in.at[:, cut])]
            mine.append(start(c_ref.at[:, there], c_in.at[:, cut]))
            mine.append(start(back_ref.at[:, there], back_in.at[:, cut]))
            loads.append(mine)
        for load in first:
            load.wait()
        for i, (cut, mine) in enumerate(zip(cuts, loads)):
            for load in mine:
                load.wait()
            below = lower[:, :, :, cut].reshape(layers * head, chunk)
            here = x_in[:, cut].astype(F32) + dot_nn(a_ref[...], below)
            rest_ref[i] = (c_in[:, cut].astype(F32) - t_ref[...] * here).astype(BF16)
            gain = jnp.sum(back_in[:, cut].astype(F32) * here, axis=0, keepdims=True)
            for at in range(0, chunk, head):
                row = (cut.start + at) // head
                dg_ref[row : row + 1, :] = gain[:, at : at + head]

    return pl.pallas_call(
        kernel,
        out_shape=[
            pltpu.VMEM((len(cuts), tokens, chunk), BF16),
            pltpu.VMEM((span // head, head), F32),
        ],
        in_specs=[IN_SMEM] + [IN_VMEM] * 2 + [IN_HBM] * (3 + len(stacks)),
        out_specs=[IN_VMEM] * 2,
        scratch_shapes=[
            pltpu.VMEM((layers, plane, rows, span), BF16),
            pltpu.VMEM((tokens, span), BF16),
            pltpu.VMEM((tokens, span), BF16),
            pltpu.VMEM((tokens, span), BF16),
            pltpu.SemaphoreType.DMA((copies,)),
        ],
        compiler_params=params(),
        name="settle",
    )(
        places,
        in_vmem(total),
        in_vmem(mixes),
        *[in_hbm(array) for array in (x, cotangent, back, *stacks)],
    )


def join(index, arrived, pair, cols, after):
    tokens, part = arrived.shape

    def kernel(i_ref, r_ref, _, *refs):
        send_ref, pair_ref = refs[len(after) :]
        at = i_ref[0]
        r = r_ref[...]
        send_ref[...] = (pair_ref[0, at, :, cols].astype(F32) + r.astype(F32)).astype(BF16)
        pair_ref[1, at, :, cols] = r

    return pl.pallas_call(
        kernel,
        out_shape=[pltpu.VMEM((tokens, part), BF16), pltpu.VMEM(pair.shape, BF16)],
        in_specs=[IN_SMEM] + [IN_VMEM] * 2 + [ANYWHERE] * len(after),
        out_specs=[IN_VMEM] * 2,
        input_output_aliases={2: 1},
        compiler_params=params(SMALL),
        name="join",
    )(index, in_vmem(arrived), in_vmem(pair), *after)


def finish(index, arrived, pair, rests, streams):
    _, count, tokens, chunk = pair.shape

    def kernel(i_ref, *refs):
        r_refs = refs[: len(streams)]
        pair_ref, rest_refs = refs[len(streams)], refs[len(streams) + 1 :][: len(rests)]
        whole_ref, whole, sems = refs[len(streams) + 1 + len(rests) :]
        each = count // len(rests)
        at = i_ref[0]
        copies = []
        for i in range(count):
            full = rest_refs[i // each][i % each].astype(F32) + pair_ref[0, i].astype(F32)
            whole[i] = (full + pair_ref[1, i].astype(F32)).astype(BF16)

            @pl.when(at == i)
            def _(i=i, full=full):
                for ref, cols in zip(r_refs, streams):
                    whole[i, :, cols] = (full[:, cols] + ref[...].astype(F32)).astype(BF16)

            there = whole_ref.at[:, pl.ds(i * chunk, chunk)]
            copies.append(pltpu.make_async_copy(whole.at[i], there, sems.at[i]))
            copies[-1].start()
        for copy in copies:
            copy.wait()

    return pl.pallas_call(
        kernel,
        out_shape=pltpu.HBM((tokens, count * chunk), BF16),
        in_specs=[IN_SMEM] + [IN_VMEM] * (len(streams) + 1 + len(rests)),
        out_specs=IN_HBM,
        scratch_shapes=[
            pltpu.VMEM((count, tokens, chunk), BF16),
            pltpu.SemaphoreType.DMA((count,)),
        ],
        compiler_params=params(SMALL),
        name="finish",
    )(index, *[in_vmem(array) for array in (*arrived, pair, *rests)])


def stacked(arrays):
    rows = arrays[0].shape[0]

    def kernel(*refs):
        for i, ref in enumerate(refs[:-1]):
            refs[-1][i * rows : (i + 1) * rows, :] = ref[...]

    return pl.pallas_call(
        kernel,
        out_shape=pltpu.VMEM((len(arrays) * rows, arrays[0].shape[1]), F32),
        in_specs=[IN_VMEM] * len(arrays),
        out_specs=IN_VMEM,
        compiler_params=params(SMALL),
        name="stacked",
    )(*[in_vmem(array) for array in arrays])


def added(arrays):
    def kernel(*refs):
        total = refs[0][...]
        for ref in refs[1:-1]:
            total = total + ref[...]
        refs[-1][...] = total

    return pl.pallas_call(
        kernel,
        out_shape=pltpu.VMEM(arrays[0].shape, F32),
        in_specs=[IN_VMEM] * len(arrays),
        out_specs=IN_VMEM,
        compiler_params=params(SMALL),
        name="added",
    )(*[in_vmem(array) for array in arrays])


STREAMS = 2
CHUNKS = 4
PARTS = 1


def stream_columns(chunk):
    lanes = 128
    tiles = chunk // lanes
    ends = [-(-tiles * (i + 1) // STREAMS) * lanes for i in range(STREAMS)]
    return [slice(start, end) for start, end in zip([0] + ends, ends)]


def shifted(array, by):
    sections = lax.axis_size("section")
    return lax.ppermute(array, "section", [(i, (i + by) % sections) for i in range(sections)])


def raised(array, by):
    sections = lax.axis_size("section")
    return lax.ppermute(array, "section", [(i, i + by) for i in range(sections - by)])


def swapped(array, step):
    groups = lax.axis_size("group")
    devices = lax.axis_size("dp")
    bits = devices.bit_length() - 1
    pairs = []
    for p in range(devices):
        for g in range(groups):
            pairs.append((p * groups + g, (p ^ (1 << ((step + g) % bits))) * groups + g))
    return lax.ppermute(array, ("dp", "group"), pairs)


def handed(array, by):
    groups = lax.axis_size("group")
    return lax.ppermute(array, "group", [(i, (i + by) % groups) for i in range(groups)])


def plane_places():
    groups = lax.axis_size("group")
    bits = lax.axis_size("dp").bit_length() - 1
    masks = []
    for g in range(groups):
        order = [0]
        for step in range(bits):
            order = order + [m ^ (1 << ((step + g) % bits)) for m in order]
        masks.append(order)
    masks = jnp.asarray(masks, jnp.int32)
    dp, member = lax.axis_index("dp"), lax.axis_index("group")
    places = []
    for r in range(groups):
        giver = (member + groups - r) % groups
        places.append((dp ^ masks[giver]) * groups + giver)
    return jnp.concatenate(places).astype(jnp.int32)


def local(tokens_in, cotangent, gains, w_qkv, w_out, segments, plan):
    sections = lax.axis_size("section")
    groups = lax.axis_size("group")
    devices = lax.axis_size("dp")
    plane = devices * groups
    section = lax.axis_index("section")
    member = lax.axis_index("group")
    rows_dev = plan.shape[1]
    length = segments.shape[1]
    tokens, width = tokens_in.shape
    head = w_out.shape[1]
    share = rows_dev // groups
    w_layer, out_layer = w_qkv[0], w_out[0]
    place = member.astype(jnp.int32)[None]
    layer = section.astype(jnp.int32)[None]

    slice_rows = head // plane
    mine = lax.axis_index("dp") * groups + member
    own_rows, *parts = pick(
        tokens_in.reshape(rows_dev, length, width),
        plan,
        place,
        groups,
        out_layer,
        mine.astype(jnp.int32)[None],
        slice_rows,
    )
    slices = [raised(own_rows, r) for r in range(sections - 1, 0, -1)]
    slices = [own_rows] + slices[::-1]
    chosen = jnp.take(segments, plan[0], axis=0, mode="clip").astype(BF16)
    chosen = chosen.reshape(groups, share, length)
    moved, moved_seg = [], []
    for r in range(groups):
        outgoing = lax.dynamic_index_in_dim(chosen, (member + r) % groups, 0, keepdims=False)
        moved.append(handed(parts[r], r) if r else parts[r])
        moved_seg.append(handed(outgoing, r) if r else outgoing)
    moved = [part.reshape(share * length, width) for part in moved]
    order = (member - jnp.arange(groups)) % groups
    seg = jnp.take(jnp.stack(moved_seg), order, axis=0, mode="clip").reshape(tokens)
    at = jnp.arange(tokens)
    mask = (
        (at[:, None] >= at[None, :])
        & (at[:, None] // length == at[None, :] // length)
        & (seg[:, None] == seg[None, :])
    ).astype(F32)

    last = (section == sections - 1).astype(jnp.int32)[None]
    bits = devices.bit_length() - 1
    places = plane_places()
    x, xz, norms = project(
        moved, cotangent, gains, w_layer, out_layer, place, []
    )
    coupling, stack = couple(slices, gains, w_layer, out_layer, last, [mask, places, xz])
    others = [shifted(coupling, r) for r in range(1, sections)]

    streams = stream_columns(width // CHUNKS)

    def facing(array, by):
        return lax.ppermute(array, "section", [(i, i ^ by) for i in range(sections)])

    arrays, masks, by = [hold(xz, others)], [0], sections // 2
    while by > 0:
        arrays = arrays + [facing(array, by) for array in arrays]
        masks = masks + [mask_of ^ by for mask_of in masks]
        by = by // 2
    xz_all = [arrays[masks.index(r)] for r in range(sections)]
    early = [xz_all[r] for r in range(1, sections) if r & (r - 1) == 0]
    late = [xz_all[r] for r in range(1, sections) if r & (r - 1) != 0]
    pieces = [compact([coupling] + others, layer, 3 * head, head, [xz])]

    rows = [stack[None]]
    for step in range(bits):
        if step > 0:
            pieces = [merge(*pieces, early)]
        pieces = pieces + [swapped(pieces[0], step)]
        if step == bits - 1:
            pieces[-1] = hold(pieces[-1], late)
        if step > 0:
            rows = [gather_two(*rows, pieces[-1:])]
        rows = rows + [swapped(rows[0], step)]
    pieces = pieces + [handed(array, r) for r in range(1, groups) for array in pieces]
    sent, total, mixes, *leaving = serial(
        xz_all, pieces, places, norms, mask, layer, gains, w_layer, out_layer, streams
    )
    back, pair = widen(sent, gains, w_layer, out_layer, width // CHUNKS)

    down = [(i, i - 1) for i in range(1, sections)]
    behind = sections - 1 - section

    def index(tick):
        return jnp.clip(tick - behind, 0, CHUNKS - 1).astype(jnp.int32)[None]

    def lowered(arrays):
        return [lax.ppermute(array, "section", down) for array in arrays]

    ticks = CHUNKS + sections - 1
    after = {}
    for tick in range(1, ticks):
        arrived = lowered(leaving)
        if tick < ticks - 1:
            for i, cols in enumerate(streams):
                leaving[i], pair = join(
                    index(tick), arrived[i], pair, cols, after.get(tick, [])
                )
        if tick == 1:
            rows = [hold(array, leaving) for array in rows]
            rows = rows + [handed(array, r) for r in range(1, groups) for array in rows]
            rests, halves = [], []
            for part in range(PARTS):
                rest, half = settle(
                    total, mixes, rows, places, x, cotangent, back, width // CHUNKS, part, PARTS
                )
                rests.append(rest)
                halves.append(half)
            sums = [stacked(halves)]
            for step in range(bits):
                sums.append(added([sums[-1], swapped(sums[-1], step)]))
            sums.append(added(sums[-1:] + [handed(sums[-1], r) for r in range(1, groups)]))
            gain_whole = sums[-1].reshape(1, width)
            after = {2 + i: [array] for i, array in enumerate(sums)}
    out = finish(index(ticks - 1), arrived, pair, rests, streams)
    return (out[None], gain_whole)


def attend(hidden, segment, gain_row, w_layer, out_layer):
    count, length, width = hidden.shape
    head = out_layer.shape[0]
    scaled = hidden * lax.rsqrt(jnp.mean(hidden * hidden, axis=-1, keepdims=True) + EPS) * gain_row
    normed = scaled.astype(BF16).reshape(count * length, width)
    projected = jnp.dot(normed, w_layer, preferred_element_type=F32).reshape(count, length, 3 * head)
    query = projected[:, :, :head]
    keyed = projected[:, :, head : 2 * head]
    valued = projected[:, :, 2 * head :]
    positions = jnp.arange(length)
    allowed = (positions[:, None] >= positions[None, :])[None] & (
        segment[:, :, None] == segment[:, None, :]
    )
    scores = jnp.einsum("rid,rjd->rij", query, keyed, precision=lax.Precision.HIGHEST)
    scores = jnp.where(allowed, scores / math.sqrt(head), -1e30)
    weights = jax.nn.softmax(scores, axis=-1)
    mixed = jnp.einsum("rij,rjd->rid", weights, valued, precision=lax.Precision.HIGHEST)
    mixed = mixed.astype(BF16).reshape(count * length, head)
    output = jnp.dot(mixed, out_layer, preferred_element_type=F32).reshape(count, length, width)
    return hidden + output


MB_ROWS = 2


def relay(tokens_in, cotangent, gains, w_qkv, w_out, segments, plan):
    sections = lax.axis_size("section")
    section = lax.axis_index("section")
    rows_dev = plan.shape[1]
    width = tokens_in.shape[1]
    length = segments.shape[1]
    micro = rows_dev // MB_ROWS
    blocks = tokens_in.reshape(rows_dev, length, width)
    chosen = jnp.take(blocks, plan[0], axis=0)
    chosen_seg = jnp.take(segments, plan[0], axis=0).astype(BF16)
    assigned = lax.all_to_all(chosen, "group", split_axis=0, concat_axis=0, tiled=True)
    moved_seg = lax.all_to_all(chosen_seg, "group", split_axis=0, concat_axis=0, tiled=True)
    assigned = assigned.reshape(micro, MB_ROWS, length, width)
    seg_groups = moved_seg.reshape(micro, MB_ROWS, length)
    gain_row, w_layer, out_layer = gains[0], w_qkv[0], w_out[0]
    grad_rows = cotangent.reshape(micro, MB_ROWS, length, width)
    ticks = micro + sections - 1

    def passed_along(array, by):
        pairs = [(i, i + by) for i in range(sections) if 0 <= i + by < sections]
        return lax.ppermute(array, "section", pairs)

    def at(array, i):
        return lax.dynamic_index_in_dim(array, i, 0, keepdims=False)

    def forward_tick(tick, carry):
        saved, arrived = carry
        index = tick - section
        valid = (index >= 0) & (index < micro)
        clipped = jnp.clip(index, 0, micro - 1)
        entering = jnp.where(section == 0, at(assigned, clipped), arrived)
        kept = jnp.where(valid, entering, at(saved, clipped))
        saved = lax.dynamic_update_index_in_dim(saved, kept, clipped, 0)
        segment = at(seg_groups, clipped)

        def run_layer(value):
            return attend(value.astype(F32), segment, gain_row, w_layer, out_layer).astype(BF16)

        leaving = lax.cond(valid, run_layer, jnp.zeros_like, entering)
        return (saved, passed_along(leaving, 1))

    saved_init = jnp.zeros((micro, MB_ROWS, length, width), BF16)
    arrive_init = jnp.zeros((MB_ROWS, length, width), BF16)
    saved, _ = lax.fori_loop(0, ticks, forward_tick, (saved_init, arrive_init))

    def backward_tick(tick, carry):
        grads_x, gain_total, arrived = carry
        index = tick - (sections - 1 - section)
        valid = (index >= 0) & (index < micro)
        clipped = jnp.clip(index, 0, micro - 1)
        entering = jnp.where(section == sections - 1, at(grad_rows, clipped), arrived)
        segment = at(seg_groups, clipped)
        stored = at(saved, clipped).astype(F32)

        def local_layer(hidden, gains_here):
            return attend(hidden, segment, gains_here, w_layer, out_layer)

        def run_back(value):
            _, pullback = jax.vjp(local_layer, stored, gain_row)
            grad_hidden, grad_gain = pullback(value.astype(F32))
            return (grad_hidden.astype(BF16), grad_gain)

        def skip_back(value):
            return (jnp.zeros_like(value), jnp.zeros(gain_row.shape, F32))

        sending, grad_gain = lax.cond(valid, run_back, skip_back, entering)
        kept = jnp.where(valid, sending, at(grads_x, clipped))
        grads_x = lax.dynamic_update_index_in_dim(grads_x, kept, clipped, 0)
        return (grads_x, gain_total + grad_gain, passed_along(sending, -1))

    gain_init = jnp.zeros(gain_row.shape, F32)
    grads_x, gain_total, _ = lax.fori_loop(
        0, ticks, backward_tick, (saved_init, gain_init, arrive_init)
    )
    gain_whole = lax.psum(gain_total, ("dp", "group"))
    return (grads_x.reshape(1, rows_dev * length, width), gain_whole[None])


def solution(mesh):
    placed = (
        P(("dp", "group"), None),
        P(("dp", "group"), None),
        P("section", None),
        P("section", None, None),
        P("section", None, None),
        P(("dp", "group"), None),
        P(("dp", "group"), None),
    )

    def chosen(tokens_in, cotangent, gains, w_qkv, w_out, segments, plan):
        sections, head, width = w_out.shape
        devices = mesh.shape["dp"]
        small = sections * 4 * head < width and sections > 1
        halves = devices & (devices - 1) == 0 and sections & (sections - 1) == 0
        body = local if small and halves else relay
        return jax.shard_map(
            body,
            mesh=mesh,
            in_specs=placed,
            out_specs=(P("section", ("dp", "group"), None), P("section", None)),
            check_vma=False,
        )(tokens_in, cotangent, gains, w_qkv, w_out, segments, plan)

    return chosen
```

profile of v0, /device:TPU:0, one launch (start us, length us, event | category | flops | bytes accessed | tf_op | source)
XLA Modules:
  0.0 121.4 jit_solution(15392359065009046733)
XLA Ops:
  1.4 2.7 %pick.1 = (bf16[16,4096]{1,0:T(8,128)(2,1)}, bf16[4,16,4096]{2,1,0:T(8,128)(2,1)}, bf16[4,16,4096]{2,1,0:T(8,128)(2,1)}) custom-call(s32[1,8]{1,0:T(1,128)S(1)} %copy-done.10, s32[1]{0:T(128)} %bitcast.9.place_ref, s32[1]{0:T(128)} %bitcast.10.mine_ref, bf16[8,16,4096]{2,1,0:T(8,128)(2,1)} %bitcast.45, bf16[128,4096]{1,0:T(8,128)(2,1)} %bitcast.39), custom_call_target="tpu_custom_call" | custom-call | tf_op jit(solution)/shard_map/pick/pallas_call | solution.py:87
  4.1 7.0 %collective-permute-start.1 = (bf16[16,4096]{1,0:T(8,128)(2,1)}, bf16[16,4096]{1,0:T(8,128)(2,1)S(1)}, u32[]{:S(2)}, u32[]{:S(2)}) collective-permute-start(bf16[16,4096]{1,0:T(8,128)(2,1)} %get-tuple-element.42.refs_3_), channel_id=1, source_target_pairs={{0,6},{1,7},{8,14},{9,15},{16,22},{17,23},{24,30},{25,31}} | collective-permute-start | bytes 393224 | tf_op jit(solution)/shard_map/ppermute | solution.py:737
  11.1 1.3 %collective-permute-start.2 = (bf16[16,4096]{1,0:T(8,128)(2,1)}, bf16[16,4096]{1,0:T(8,128)(2,1)S(1)}, u32[]{:S(2)}, u32[]{:S(2)}) collective-permute-start(bf16[16,4096]{1,0:T(8,128)(2,1)} %get-tuple-element.42.refs_3_), channel_id=1, source_target_pairs={{0,4},{2,6},{1,5},{3,7},{8,12},{10,14},{9,13},{11,15},{16,20},{18,... | collective-permute-start | bytes 393224 | tf_op jit(solution)/shard_map/ppermute | solution.py:737
  12.4 2.5 %collective-permute-start.3 = (bf16[16,4096]{1,0:T(8,128)(2,1)}, bf16[16,4096]{1,0:T(8,128)(2,1)S(1)}, u32[]{:S(2)}, u32[]{:S(2)}) collective-permute-start(bf16[16,4096]{1,0:T(8,128)(2,1)} %get-tuple-element.42.refs_3_), channel_id=1, source_target_pairs={{0,2},{2,4},{4,6},{1,3},{3,5},{5,7},{8,10},{10,12},{12,14},{9,11},... | collective-permute-start | bytes 393224 | tf_op jit(solution)/shard_map/ppermute | solution.py:737
  18.9 3.6 %project.1 = (bf16[128,4096]{1,0:T(8,128)(2,1)}, bf16[128,640]{1,0:T(8,128)(2,1)S(1)}, f32[128,1]{1,0:T(8,128)S(1)}) custom-call(s32[1]{0:T(128)} %bitcast.9.place_ref, bf16[64,4096]{1,0:T(8,128)(2,1)S(1)} %bitcast.30, bf16[64,4096]{1,0:T(8,128)(2,1)S(1)} %bitcast.31, bf16[128,4096]{1,0:T(8,128)(2,1)} %c_ref.1, f32[1,4096]{1,0:T(1,128)S(1)} %copy-done.6, ...), custom_call_target="tpu_custom_call" | custom-call | tf_op jit(solution)/shard_map/project/pallas_call | solution.py:150
  22.5 3.4 %couple.1 = (bf16[16,1152]{1,0:T(8,128)(2,1)S(1)}, bf16[3,16,4096]{2,1,0:T(8,128)(2,1)}) custom-call(s32[1]{0:T(128)} %bitcast.16.last_ref, bf16[16,4096]{1,0:T(8,128)(2,1)S(1)} %collective-permute-done.1.refs_0_, bf16[16,4096]{1,0:T(8,128)(2,1)S(1)} %collective-permute-done.2.refs_1_, bf16[16,4096]{1,0:T(8,128)(2,1)S(1)} %collective-permute-done.3.refs_2_, ...), custom_call_target="tpu_custom_call" | custom-call | tf_op jit(solution)/shard_map/couple/pallas_call | solution.py:232
  26.0 1.6 %collective-permute-start.5 = (bf16[16,1152]{1,0:T(8,128)(2,1)S(1)}, bf16[16,1152]{1,0:T(8,128)(2,1)S(1)}, u32[]{:S(2)}, u32[]{:S(2)}) collective-permute-start(bf16[16,1152]{1,0:T(8,128)(2,1)S(1)} %get-tuple-element.43.refs_0_), channel_id=1, source_target_pairs={{0,2},{2,4},{4,6},{6,0},{1,3},{3,5},{5,7},{7,1},{8,10},{10,12},{12... | collective-permute-start | bytes 110600 | tf_op jit(solution)/shard_map/ppermute | solution.py:732
  27.5 1.9 %collective-permute-start.6 = (bf16[16,1152]{1,0:T(8,128)(2,1)S(1)}, bf16[16,1152]{1,0:T(8,128)(2,1)S(1)}, u32[]{:S(2)}, u32[]{:S(2)}) collective-permute-start(bf16[16,1152]{1,0:T(8,128)(2,1)S(1)} %get-tuple-element.43.refs_0_), channel_id=1, source_target_pairs={{0,4},{2,6},{4,0},{6,2},{1,5},{3,7},{5,1},{7,3},{8,12},{10,14},{12... | collective-permute-start | bytes 110600 | tf_op jit(solution)/shard_map/ppermute | solution.py:732
  29.4 2.8 %collective-permute-start.7 = (bf16[16,1152]{1,0:T(8,128)(2,1)S(1)}, bf16[16,1152]{1,0:T(8,128)(2,1)S(1)}, u32[]{:S(2)}, u32[]{:S(2)}) collective-permute-start(bf16[16,1152]{1,0:T(8,128)(2,1)S(1)} %get-tuple-element.43.refs_0_), channel_id=1, source_target_pairs={{0,6},{2,0},{4,2},{6,4},{1,7},{3,1},{5,3},{7,5},{8,14},{10,8},{12,... | collective-permute-start | bytes 110600 | tf_op jit(solution)/shard_map/ppermute | solution.py:732
  32.3 1.5 %collective-permute-start.18 = (bf16[1,3,16,4096]{3,2,1,0:T(8,128)(2,1)}, bf16[1,3,16,4096]{3,2,1,0:T(8,128)(2,1)S(1)}, u32[]{:S(2)}, u32[]{:S(2)}) collective-permute-start(bf16[1,3,16,4096]{3,2,1,0:T(8,128)(2,1)} %bitcast.32), channel_id=1, source_target_pairs={{0,8},{1,17},{8,0},{9,25},{16,24},{17,1},{24,16},{25,9},{2,10},{3,... | collective-permute-start | bytes 1179656 | tf_op jit(solution)/shard_map/ppermute | solution.py:748
  34.9 3.8 %collective-permute-start.9 = (bf16[128,640]{1,0:T(8,128)(2,1)S(1)}, bf16[128,640]{1,0:T(8,128)(2,1)S(1)}, u32[]{:S(2)}, u32[]{:S(2)}) collective-permute-start(bf16[128,640]{1,0:T(8,128)(2,1)S(1)} %hold.4.refs_0_), channel_id=1, source_target_pairs={{0,4},{2,6},{4,0},{6,2},{1,5},{3,7},{5,1},{7,3},{8,12},{10,14},{12... | collective-permute-start | bytes 491528 | tf_op jit(solution)/shard_map/ppermute | solution.py:832
  38.7 1.5 %collective-permute-start.11 = (bf16[1,16,3072]{2,1,0:T(8,128)(2,1)S(1)}, bf16[1,16,3072]{2,1,0:T(8,128)(2,1)S(1)}, u32[]{:S(2)}, u32[]{:S(2)}) collective-permute-start(bf16[1,16,3072]{2,1,0:T(8,128)(2,1)S(1)} %compact.1.first_ref), channel_id=1, source_target_pairs={{0,8},{1,17},{8,0},{9,25},{16,24},{17,1},{24,16},{25,9},{2,10},{3,... | collective-permute-start | bytes 294920 | tf_op jit(solution)/shard_map/ppermute | solution.py:748
  40.2 3.6 %collective-permute-done.11.second_ref = bf16[1,16,3072]{2,1,0:T(8,128)(2,1)S(1)} collective-permute-done((bf16[1,16,3072]{2,1,0:T(8,128)(2,1)S(1)}, bf16[1,16,3072]{2,1,0:T(8,128)(2,1)S(1)}, u32[]{:S(2)}, u32[]{:S(2)}) %collective-permute-start.11) | collective-permute-done | bytes 98336 | tf_op jit(solution)/shard_map/ppermute | solution.py:748
  44.7 1.6 %collective-permute-start.12 = (bf16[2,16,3072]{2,1,0:T(8,128)(2,1)S(1)}, bf16[2,16,3072]{2,1,0:T(8,128)(2,1)S(1)}, u32[]{:S(2)}, u32[]{:S(2)}) collective-permute-start(bf16[2,16,3072]{2,1,0:T(8,128)(2,1)S(1)} %merge.1.refs_4_), channel_id=1, source_target_pairs={{0,16},{1,9},{8,24},{9,1},{16,0},{17,25},{24,8},{25,17},{2,18},{3,... | collective-permute-start | bytes 589832 | tf_op jit(solution)/shard_map/ppermute | solution.py:748
  46.6 5.0 %collective-permute-done.10.refs_1_.refs_3_ = bf16[128,640]{1,0:T(8,128)(2,1)S(1)} collective-permute-done((bf16[128,640]{1,0:T(8,128)(2,1)S(1)}, bf16[128,640]{1,0:T(8,128)(2,1)S(1)}, u32[]{:S(2)}, u32[]{:S(2)}) %collective-permute-start.10) | collective-permute-done | bytes 163872 | tf_op jit(solution)/shard_map/ppermute | solution.py:832
  54.3 8.9 %serial.1 = (bf16[128,512]{1,0:T(8,128)(2,1)S(1)}, f32[128,1]{1,0:T(8,128)S(1)}, bf16[128,384]{1,0:T(8,128)(2,1)S(1)}, bf16[128,512]{1,0:T(8,128)(2,1)}, bf16[128,512]{1,0:T(8,128)(2,1)}) custom-call(s32[1]{0:T(128)} %bitcast.6.s_ref, s32[8]{0:T(128)S(1)} %pad_add_fusion.refs_8_.p_ref, bf16[128,640]{1,0:T(8,128)(2,1)S(1)} %hold.4.refs_0_, ...), custom_call_target="tpu_custom_call" | custom-call | tf_op jit(solution)/shard_map/serial/pallas_call | solution.py:442
  65.1 1.3 %collective-permute-start.17 = (bf16[128,512]{1,0:T(8,128)(2,1)}, bf16[128,512]{1,0:T(8,128)(2,1)S(1)}, u32[]{:S(2)}, u32[]{:S(2)}) collective-permute-start(bf16[128,512]{1,0:T(8,128)(2,1)} %get-tuple-element.49), channel_id=1, source_target_pairs={{2,0},{4,2},{6,4},{3,1},{5,3},{7,5},{10,8},{12,10},{14,12},{11,9},... | collective-permute-start | bytes 393224 | tf_op jit(solution)/shard_map/ppermute | solution.py:867
  66.4 3.8 %widen.1 = (bf16[128,4096]{1,0:T(8,128)(2,1)}, bf16[2,4,128,1024]{3,2,1,0:T(8,128)(2,1)S(1)}) custom-call(bf16[128,512]{1,0:T(8,128)(2,1)S(1)} %get-tuple-element.46.v_ref, f32[1,4096]{1,0:T(1,128)S(1)} %copy-done.6, bf16[4096,384]{1,0:T(8,128)(2,1)} %bitcast.38, bf16[128,4096]{1,0:T(8,128)(2,1)} %bitcast.43), custom_call_target="tpu_custom_call" | custom-call | tf_op jit(solution)/shard_map/widen/pallas_call | solution.py:539
  70.3 2.0 %collective-permute-done.15.r_ref = bf16[128,512]{1,0:T(8,128)(2,1)S(1)} collective-permute-done((bf16[128,512]{1,0:T(8,128)(2,1)}, bf16[128,512]{1,0:T(8,128)(2,1)S(1)}, u32[]{:S(2)}, u32[]{:S(2)}) %collective-permute-start.15) | collective-permute-done | bytes 131104 | tf_op jit(solution)/shard_map/ppermute | solution.py:867
  72.3 2.1 %collective-permute-done.17.r_ref = bf16[128,512]{1,0:T(8,128)(2,1)S(1)} collective-permute-done((bf16[128,512]{1,0:T(8,128)(2,1)}, bf16[128,512]{1,0:T(8,128)(2,1)S(1)}, u32[]{:S(2)}, u32[]{:S(2)}) %collective-permute-start.17) | collective-permute-done | bytes 131104 | tf_op jit(solution)/shard_map/ppermute | solution.py:867
  78.9 4.5 %settle.1 = (bf16[4,128,1024]{2,1,0:T(8,128)(2,1)S(1)}, f32[32,128]{1,0:T(8,128)S(1)}) custom-call(s32[8]{0:T(128)S(1)} %pad_add_fusion.refs_8_.p_ref, f32[128,1]{1,0:T(8,128)S(1)} %copy-done.9, bf16[128,384]{1,0:T(8,128)(2,1)S(1)} %get-tuple-element.53.a_ref, bf16[128,4096]{1,0:T(8,128)(2,1)} %get-tuple-element.54.x_ref, bf16[128,4096]{1,0:T(8,128)(2,1)} %c_ref.1, ...), custom_call_target="tpu_custom_call" | custom-call | tf_op jit(solution)/shard_map/settle/pallas_call | solution.py:599
  83.5 1.3 %collective-permute-start.22 = (bf16[128,512]{1,0:T(8,128)(2,1)S(1)}, bf16[128,512]{1,0:T(8,128)(2,1)S(1)}, u32[]{:S(2)}, u32[]{:S(2)}) collective-permute-start(bf16[128,512]{1,0:T(8,128)(2,1)S(1)} %get-tuple-element.59), channel_id=1, source_target_pairs={{2,0},{4,2},{6,4},{3,1},{5,3},{7,5},{10,8},{12,10},{14,12},{11,9},... | collective-permute-start | bytes 393224 | tf_op jit(solution)/shard_map/ppermute | solution.py:867
  86.6 1.6 %collective-permute-start.24 = (f32[32,128]{1,0:T(8,128)S(1)}, f32[32,128]{1,0:T(8,128)S(1)}, u32[]{:S(2)}, u32[]{:S(2)}) collective-permute-start(f32[32,128]{1,0:T(8,128)S(1)} %stacked.1.refs_0_), channel_id=1, source_target_pairs={{0,8},{1,17},{8,0},{9,25},{16,24},{17,1},{24,16},{25,9},{2,10},{3,... | collective-permute-start | bytes 49160 | tf_op jit(solution)/shard_map/ppermute | solution.py:748
  88.1 2.3 %collective-permute-done.24.refs_1_ = f32[32,128]{1,0:T(8,128)S(1)} collective-permute-done((f32[32,128]{1,0:T(8,128)S(1)}, f32[32,128]{1,0:T(8,128)S(1)}, u32[]{:S(2)}, u32[]{:S(2)}) %collective-permute-start.24) | collective-permute-done | bytes 16416 | tf_op jit(solution)/shard_map/ppermute | solution.py:748
  90.4 2.1 %collective-permute-done.22.r_ref = bf16[128,512]{1,0:T(8,128)(2,1)S(1)} collective-permute-done((bf16[128,512]{1,0:T(8,128)(2,1)S(1)}, bf16[128,512]{1,0:T(8,128)(2,1)S(1)}, u32[]{:S(2)}, u32[]{:S(2)}) %collective-permute-start.22) | collective-permute-done | bytes 131104 | tf_op jit(solution)/shard_map/ppermute | solution.py:867
  94.6 1.3 %collective-permute-start.29 = (bf16[128,512]{1,0:T(8,128)(2,1)S(1)}, bf16[128,512]{1,0:T(8,128)(2,1)S(1)}, u32[]{:S(2)}, u32[]{:S(2)}) collective-permute-start(bf16[128,512]{1,0:T(8,128)(2,1)S(1)} %get-tuple-element.67), channel_id=1, source_target_pairs={{2,0},{4,2},{6,4},{3,1},{5,3},{7,5},{10,8},{12,10},{14,12},{11,9},... | collective-permute-start | bytes 393224 | tf_op jit(solution)/shard_map/ppermute | solution.py:867
  95.9 1.6 %collective-permute-start.27 = (f32[32,128]{1,0:T(8,128)S(1)}, f32[32,128]{1,0:T(8,128)S(1)}, u32[]{:S(2)}, u32[]{:S(2)}) collective-permute-start(f32[32,128]{1,0:T(8,128)S(1)} %added.3.refs_0_), channel_id=1, source_target_pairs={{0,16},{1,9},{8,24},{9,1},{16,0},{17,25},{24,8},{25,17},{2,18},{3,... | collective-permute-start | bytes 49160 | tf_op jit(solution)/shard_map/ppermute | solution.py:748
  97.4 2.2 %collective-permute-done.27.refs_1_ = f32[32,128]{1,0:T(8,128)S(1)} collective-permute-done((f32[32,128]{1,0:T(8,128)S(1)}, f32[32,128]{1,0:T(8,128)S(1)}, u32[]{:S(2)}, u32[]{:S(2)}) %collective-permute-start.27) | collective-permute-done | bytes 16416 | tf_op jit(solution)/shard_map/ppermute | solution.py:748
  105.5 2.9 %collective-permute-done.28.r_ref = bf16[128,512]{1,0:T(8,128)(2,1)S(1)} collective-permute-done((bf16[128,512]{1,0:T(8,128)(2,1)S(1)}, bf16[128,512]{1,0:T(8,128)(2,1)S(1)}, u32[]{:S(2)}, u32[]{:S(2)}) %collective-permute-start.28) | collective-permute-done | bytes 131104 | tf_op jit(solution)/shard_map/ppermute | solution.py:867
  112.3 1.3 %collective-permute-start.31 = (bf16[128,512]{1,0:T(8,128)(2,1)}, bf16[128,512]{1,0:T(8,128)(2,1)S(1)}, u32[]{:S(2)}, u32[]{:S(2)}) collective-permute-start(bf16[128,512]{1,0:T(8,128)(2,1)} %get-tuple-element.70), channel_id=1, source_target_pairs={{2,0},{4,2},{6,4},{3,1},{5,3},{7,5},{10,8},{12,10},{14,12},{11,9},... | collective-permute-start | bytes 393224 | tf_op jit(solution)/shard_map/ppermute | solution.py:867
  114.2 4.7 %collective-permute-done.33.refs_1_ = bf16[128,512]{1,0:T(8,128)(2,1)S(1)} collective-permute-done((bf16[128,512]{1,0:T(8,128)(2,1)}, bf16[128,512]{1,0:T(8,128)(2,1)S(1)}, u32[]{:S(2)}, u32[]{:S(2)}) %collective-permute-start.33) | collective-permute-done | bytes 131104 | tf_op jit(solution)/shard_map/ppermute | solution.py:867
  118.8 1.4 %collective-permute-done.31.refs_0_ = bf16[128,512]{1,0:T(8,128)(2,1)S(1)} collective-permute-done((bf16[128,512]{1,0:T(8,128)(2,1)}, bf16[128,512]{1,0:T(8,128)(2,1)S(1)}, u32[]{:S(2)}, u32[]{:S(2)}) %collective-permute-start.31) | collective-permute-done | bytes 131104 | tf_op jit(solution)/shard_map/ppermute | solution.py:867
  (104 shorter events, 31.3 us)
Async XLA Ops:
  4.1 18.4 %collective-permute-start.1 = (bf16[16,4096]{1,0:T(8,128)(2,1)}, bf16[16,4096]{1,0:T(8,128)(2,1)S(1)}, u32[]{:S(2)}, u32[]{:S(2)}) collective-permute-start(bf16[16,4096]{1,0:T(8,128)(2,1)} %get-tuple-element.42.refs_3_), channel_id=1, source_target_pairs={{0,6},{1,7},{8,14},{9,15},{16,22},{17,23},{24,30},{25,31}} | collective-permute-start | bytes 393224 | tf_op jit(solution)/shard_map/ppermute | solution.py:737
  11.1 11.4 %collective-permute-start.2 = (bf16[16,4096]{1,0:T(8,128)(2,1)}, bf16[16,4096]{1,0:T(8,128)(2,1)S(1)}, u32[]{:S(2)}, u32[]{:S(2)}) collective-permute-start(bf16[16,4096]{1,0:T(8,128)(2,1)} %get-tuple-element.42.refs_3_), channel_id=1, source_target_pairs={{0,4},{2,6},{1,5},{3,7},{8,12},{10,14},{9,13},{11,15},{16,20},{18,... | collective-permute-start | bytes 393224 | tf_op jit(solution)/shard_map/ppermute | solution.py:737
  12.4 10.1 %collective-permute-start.3 = (bf16[16,4096]{1,0:T(8,128)(2,1)}, bf16[16,4096]{1,0:T(8,128)(2,1)S(1)}, u32[]{:S(2)}, u32[]{:S(2)}) collective-permute-start(bf16[16,4096]{1,0:T(8,128)(2,1)} %get-tuple-element.42.refs_3_), channel_id=1, source_target_pairs={{0,2},{2,4},{4,6},{1,3},{3,5},{5,7},{8,10},{10,12},{12,14},{9,11},... | collective-permute-start | bytes 393224 | tf_op jit(solution)/shard_map/ppermute | solution.py:737
  15.6 2.2 %collective-permute-start = (bf16[4,16,4096]{2,1,0:T(8,128)(2,1)}, bf16[4,16,4096]{2,1,0:T(8,128)(2,1)S(1)}, u32[]{:S(2)}, u32[]{:S(2)}) collective-permute-start(bf16[4,16,4096]{2,1,0:T(8,128)(2,1)} %get-tuple-element.40), channel_id=1, source_target_pairs={{0,1},{1,0},{2,3},{3,2},{4,5},{5,4},{6,7},{7,6},{8,9},{9,8},{10,11... | collective-permute-start | bytes 1572872 | tf_op jit(solution)/shard_map/ppermute | solution.py:753
  26.0 7.8 %collective-permute-start.5 = (bf16[16,1152]{1,0:T(8,128)(2,1)S(1)}, bf16[16,1152]{1,0:T(8,128)(2,1)S(1)}, u32[]{:S(2)}, u32[]{:S(2)}) collective-permute-start(bf16[16,1152]{1,0:T(8,128)(2,1)S(1)} %get-tuple-element.43.refs_0_), channel_id=1, source_target_pairs={{0,2},{2,4},{4,6},{6,0},{1,3},{3,5},{5,7},{7,1},{8,10},{10,12},{12... | collective-permute-start | bytes 110600 | tf_op jit(solution)/shard_map/ppermute | solution.py:732
  27.5 6.2 %collective-permute-start.6 = (bf16[16,1152]{1,0:T(8,128)(2,1)S(1)}, bf16[16,1152]{1,0:T(8,128)(2,1)S(1)}, u32[]{:S(2)}, u32[]{:S(2)}) collective-permute-start(bf16[16,1152]{1,0:T(8,128)(2,1)S(1)} %get-tuple-element.43.refs_0_), channel_id=1, source_target_pairs={{0,4},{2,6},{4,0},{6,2},{1,5},{3,7},{5,1},{7,3},{8,12},{10,14},{12... | collective-permute-start | bytes 110600 | tf_op jit(solution)/shard_map/ppermute | solution.py:732
  29.4 4.5 %collective-permute-start.7 = (bf16[16,1152]{1,0:T(8,128)(2,1)S(1)}, bf16[16,1152]{1,0:T(8,128)(2,1)S(1)}, u32[]{:S(2)}, u32[]{:S(2)}) collective-permute-start(bf16[16,1152]{1,0:T(8,128)(2,1)S(1)} %get-tuple-element.43.refs_0_), channel_id=1, source_target_pairs={{0,6},{2,0},{4,2},{6,4},{1,7},{3,1},{5,3},{7,5},{8,14},{10,8},{12,... | collective-permute-start | bytes 110600 | tf_op jit(solution)/shard_map/ppermute | solution.py:732
  32.3 19.4 %collective-permute-start.18 = (bf16[1,3,16,4096]{3,2,1,0:T(8,128)(2,1)}, bf16[1,3,16,4096]{3,2,1,0:T(8,128)(2,1)S(1)}, u32[]{:S(2)}, u32[]{:S(2)}) collective-permute-start(bf16[1,3,16,4096]{3,2,1,0:T(8,128)(2,1)} %bitcast.32), channel_id=1, source_target_pairs={{0,8},{1,17},{8,0},{9,25},{16,24},{17,1},{24,16},{25,9},{2,10},{3,... | collective-permute-start | bytes 1179656 | tf_op jit(solution)/shard_map/ppermute | solution.py:748
  33.9 9.8 %collective-permute-start.8 = (bf16[128,640]{1,0:T(8,128)(2,1)S(1)}, bf16[128,640]{1,0:T(8,128)(2,1)S(1)}, u32[]{:S(2)}, u32[]{:S(2)}) collective-permute-start(bf16[128,640]{1,0:T(8,128)(2,1)S(1)} %hold.4.refs_0_), channel_id=1, source_target_pairs={{0,2},{2,0},{4,6},{6,4},{1,3},{3,1},{5,7},{7,5},{8,10},{10,8},{12,... | collective-permute-start | bytes 491528 | tf_op jit(solution)/shard_map/ppermute | solution.py:832
  34.9 9.8 %collective-permute-start.9 = (bf16[128,640]{1,0:T(8,128)(2,1)S(1)}, bf16[128,640]{1,0:T(8,128)(2,1)S(1)}, u32[]{:S(2)}, u32[]{:S(2)}) collective-permute-start(bf16[128,640]{1,0:T(8,128)(2,1)S(1)} %hold.4.refs_0_), channel_id=1, source_target_pairs={{0,4},{2,6},{4,0},{6,2},{1,5},{3,7},{5,1},{7,3},{8,12},{10,14},{12... | collective-permute-start | bytes 491528 | tf_op jit(solution)/shard_map/ppermute | solution.py:832
  38.7 5.1 %collective-permute-start.11 = (bf16[1,16,3072]{2,1,0:T(8,128)(2,1)S(1)}, bf16[1,16,3072]{2,1,0:T(8,128)(2,1)S(1)}, u32[]{:S(2)}, u32[]{:S(2)}) collective-permute-start(bf16[1,16,3072]{2,1,0:T(8,128)(2,1)S(1)} %compact.1.first_ref), channel_id=1, source_target_pairs={{0,8},{1,17},{8,0},{9,25},{16,24},{17,1},{24,16},{25,9},{2,10},{3,... | collective-permute-start | bytes 294920 | tf_op jit(solution)/shard_map/ppermute | solution.py:748
  44.7 6.9 %collective-permute-start.12 = (bf16[2,16,3072]{2,1,0:T(8,128)(2,1)S(1)}, bf16[2,16,3072]{2,1,0:T(8,128)(2,1)S(1)}, u32[]{:S(2)}, u32[]{:S(2)}) collective-permute-start(bf16[2,16,3072]{2,1,0:T(8,128)(2,1)S(1)} %merge.1.refs_4_), channel_id=1, source_target_pairs={{0,16},{1,9},{8,24},{9,1},{16,0},{17,25},{24,8},{25,17},{2,18},{3,... | collective-permute-start | bytes 589832 | tf_op jit(solution)/shard_map/ppermute | solution.py:748
  46.3 5.3 %collective-permute-start.10 = (bf16[128,640]{1,0:T(8,128)(2,1)S(1)}, bf16[128,640]{1,0:T(8,128)(2,1)S(1)}, u32[]{:S(2)}, u32[]{:S(2)}) collective-permute-start(bf16[128,640]{1,0:T(8,128)(2,1)S(1)} %collective-permute-done.9.refs_1_.refs_2_), channel_id=1, source_target_pairs={{0,2},{2,0},{4,6},{6,4},{1,3},{3,1},{5,7},{7,5},{8,10},{10,8},{12,... | collective-permute-start | bytes 491528 | tf_op jit(solution)/shard_map/ppermute | solution.py:832
  52.0 22.4 %collective-permute-start.19 = (bf16[2,3,16,4096]{3,2,1,0:T(8,128)(2,1)S(1)}, bf16[2,3,16,4096]{3,2,1,0:T(8,128)(2,1)}, u32[]{:S(2)}, u32[]{:S(2)}) collective-permute-start(bf16[2,3,16,4096]{3,2,1,0:T(8,128)(2,1)S(1)} %gather_two.1.refs_0_), channel_id=1, source_target_pairs={{0,16},{1,9},{8,24},{9,1},{16,0},{17,25},{24,8},{25,17},{2,18},{3,... | collective-permute-start | bytes 2359304 | tf_op jit(solution)/shard_map/ppermute | solution.py:748
  52.6 1.4 %collective-permute-start.13 = (bf16[2,16,3072]{2,1,0:T(8,128)(2,1)S(1)}, bf16[2,16,3072]{2,1,0:T(8,128)(2,1)S(1)}, u32[]{:S(2)}, u32[]{:S(2)}) collective-permute-start(bf16[2,16,3072]{2,1,0:T(8,128)(2,1)S(1)} %merge.1.refs_4_), channel_id=1, source_target_pairs={{0,1},{1,0},{2,3},{3,2},{4,5},{5,4},{6,7},{7,6},{8,9},{9,8},{10,11... | collective-permute-start | bytes 589832 | tf_op jit(solution)/shard_map/ppermute | solution.py:753
  52.6 1.7 %collective-permute-start.14 = (bf16[2,16,3072]{2,1,0:T(8,128)(2,1)S(1)}, bf16[2,16,3072]{2,1,0:T(8,128)(2,1)S(1)}, u32[]{:S(2)}, u32[]{:S(2)}) collective-permute-start(bf16[2,16,3072]{2,1,0:T(8,128)(2,1)S(1)} %hold.5.refs_5_.refs_0_), channel_id=1, source_target_pairs={{0,1},{1,0},{2,3},{3,2},{4,5},{5,4},{6,7},{7,6},{8,9},{9,8},{10,11... | collective-permute-start | bytes 589832 | tf_op jit(solution)/shard_map/ppermute | solution.py:753
  63.9 8.4 %collective-permute-start.15 = (bf16[128,512]{1,0:T(8,128)(2,1)}, bf16[128,512]{1,0:T(8,128)(2,1)S(1)}, u32[]{:S(2)}, u32[]{:S(2)}) collective-permute-start(bf16[128,512]{1,0:T(8,128)(2,1)} %get-tuple-element.45), channel_id=1, source_target_pairs={{2,0},{4,2},{6,4},{3,1},{5,3},{7,5},{10,8},{12,10},{14,12},{11,9},... | collective-permute-start | bytes 393224 | tf_op jit(solution)/shard_map/ppermute | solution.py:867
  65.1 9.2 %collective-permute-start.17 = (bf16[128,512]{1,0:T(8,128)(2,1)}, bf16[128,512]{1,0:T(8,128)(2,1)S(1)}, u32[]{:S(2)}, u32[]{:S(2)}) collective-permute-start(bf16[128,512]{1,0:T(8,128)(2,1)} %get-tuple-element.49), channel_id=1, source_target_pairs={{2,0},{4,2},{6,4},{3,1},{5,3},{7,5},{10,8},{12,10},{14,12},{11,9},... | collective-permute-start | bytes 393224 | tf_op jit(solution)/shard_map/ppermute | solution.py:867
  74.5 3.2 %collective-permute-start.21 = (bf16[2,3,16,4096]{3,2,1,0:T(8,128)(2,1)}, bf16[2,3,16,4096]{3,2,1,0:T(8,128)(2,1)}, u32[]{:S(2)}, u32[]{:S(2)}) collective-permute-start(bf16[2,3,16,4096]{3,2,1,0:T(8,128)(2,1)} %hold.7.refs_1_), channel_id=1, source_target_pairs={{0,1},{1,0},{2,3},{3,2},{4,5},{5,4},{6,7},{7,6},{8,9},{9,8},{10,11... | collective-permute-start | bytes 2359304 | tf_op jit(solution)/shard_map/ppermute | solution.py:753
  74.5 3.5 %collective-permute-start.20 = (bf16[2,3,16,4096]{3,2,1,0:T(8,128)(2,1)S(1)}, bf16[2,3,16,4096]{3,2,1,0:T(8,128)(2,1)}, u32[]{:S(2)}, u32[]{:S(2)}) collective-permute-start(bf16[2,3,16,4096]{3,2,1,0:T(8,128)(2,1)S(1)} %hold.6.refs_0_), channel_id=1, source_target_pairs={{0,1},{1,0},{2,3},{3,2},{4,5},{5,4},{6,7},{7,6},{8,9},{9,8},{10,11... | collective-permute-start | bytes 2359304 | tf_op jit(solution)/shard_map/ppermute | solution.py:753
  75.0 8.4 %collective-permute-start.16 = (bf16[128,512]{1,0:T(8,128)(2,1)S(1)}, bf16[128,512]{1,0:T(8,128)(2,1)S(1)}, u32[]{:S(2)}, u32[]{:S(2)}) collective-permute-start(bf16[128,512]{1,0:T(8,128)(2,1)S(1)} %get-tuple-element.48.refs_1_), channel_id=1, source_target_pairs={{2,0},{4,2},{6,4},{3,1},{5,3},{7,5},{10,8},{12,10},{14,12},{11,9},... | collective-permute-start | bytes 393224 | tf_op jit(solution)/shard_map/ppermute | solution.py:867
  76.3 8.9 %collective-permute-start.23 = (bf16[128,512]{1,0:T(8,128)(2,1)S(1)}, bf16[128,512]{1,0:T(8,128)(2,1)S(1)}, u32[]{:S(2)}, u32[]{:S(2)}) collective-permute-start(bf16[128,512]{1,0:T(8,128)(2,1)S(1)} %get-tuple-element.57.refs_2_), channel_id=1, source_target_pairs={{2,0},{4,2},{6,4},{3,1},{5,3},{7,5},{10,8},{12,10},{14,12},{11,9},... | collective-permute-start | bytes 393224 | tf_op jit(solution)/shard_map/ppermute | solution.py:867
  83.5 9.0 %collective-permute-start.22 = (bf16[128,512]{1,0:T(8,128)(2,1)S(1)}, bf16[128,512]{1,0:T(8,128)(2,1)S(1)}, u32[]{:S(2)}, u32[]{:S(2)}) collective-permute-start(bf16[128,512]{1,0:T(8,128)(2,1)S(1)} %get-tuple-element.59), channel_id=1, source_target_pairs={{2,0},{4,2},{6,4},{3,1},{5,3},{7,5},{10,8},{12,10},{14,12},{11,9},... | collective-permute-start | bytes 393224 | tf_op jit(solution)/shard_map/ppermute | solution.py:867
  85.3 9.3 %collective-permute-start.26 = (bf16[128,512]{1,0:T(8,128)(2,1)S(1)}, bf16[128,512]{1,0:T(8,128)(2,1)S(1)}, u32[]{:S(2)}, u32[]{:S(2)}) collective-permute-start(bf16[128,512]{1,0:T(8,128)(2,1)S(1)} %get-tuple-element.63), channel_id=1, source_target_pairs={{2,0},{4,2},{6,4},{3,1},{5,3},{7,5},{10,8},{12,10},{14,12},{11,9},... | collective-permute-start | bytes 393224 | tf_op jit(solution)/shard_map/ppermute | solution.py:867
  86.6 3.8 %collective-permute-start.24 = (f32[32,128]{1,0:T(8,128)S(1)}, f32[32,128]{1,0:T(8,128)S(1)}, u32[]{:S(2)}, u32[]{:S(2)}) collective-permute-start(f32[32,128]{1,0:T(8,128)S(1)} %stacked.1.refs_0_), channel_id=1, source_target_pairs={{0,8},{1,17},{8,0},{9,25},{16,24},{17,1},{24,16},{25,9},{2,10},{3,... | collective-permute-start | bytes 49160 | tf_op jit(solution)/shard_map/ppermute | solution.py:748
  92.5 8.0 %collective-permute-start.25 = (bf16[128,512]{1,0:T(8,128)(2,1)S(1)}, bf16[128,512]{1,0:T(8,128)(2,1)S(1)}, u32[]{:S(2)}, u32[]{:S(2)}) collective-permute-start(bf16[128,512]{1,0:T(8,128)(2,1)S(1)} %get-tuple-element.62), channel_id=1, source_target_pairs={{2,0},{4,2},{6,4},{3,1},{5,3},{7,5},{10,8},{12,10},{14,12},{11,9},... | collective-permute-start | bytes 393224 | tf_op jit(solution)/shard_map/ppermute | solution.py:867
  94.6 7.7 %collective-permute-start.29 = (bf16[128,512]{1,0:T(8,128)(2,1)S(1)}, bf16[128,512]{1,0:T(8,128)(2,1)S(1)}, u32[]{:S(2)}, u32[]{:S(2)}) collective-permute-start(bf16[128,512]{1,0:T(8,128)(2,1)S(1)} %get-tuple-element.67), channel_id=1, source_target_pairs={{2,0},{4,2},{6,4},{3,1},{5,3},{7,5},{10,8},{12,10},{14,12},{11,9},... | collective-permute-start | bytes 393224 | tf_op jit(solution)/shard_map/ppermute | solution.py:867
  95.9 3.8 %collective-permute-start.27 = (f32[32,128]{1,0:T(8,128)S(1)}, f32[32,128]{1,0:T(8,128)S(1)}, u32[]{:S(2)}, u32[]{:S(2)}) collective-permute-start(f32[32,128]{1,0:T(8,128)S(1)} %added.3.refs_0_), channel_id=1, source_target_pairs={{0,16},{1,9},{8,24},{9,1},{16,0},{17,25},{24,8},{25,17},{2,18},{3,... | collective-permute-start | bytes 49160 | tf_op jit(solution)/shard_map/ppermute | solution.py:748
  100.6 7.8 %collective-permute-start.28 = (bf16[128,512]{1,0:T(8,128)(2,1)S(1)}, bf16[128,512]{1,0:T(8,128)(2,1)S(1)}, u32[]{:S(2)}, u32[]{:S(2)}) collective-permute-start(bf16[128,512]{1,0:T(8,128)(2,1)S(1)} %get-tuple-element.66), channel_id=1, source_target_pairs={{2,0},{4,2},{6,4},{3,1},{5,3},{7,5},{10,8},{12,10},{14,12},{11,9},... | collective-permute-start | bytes 393224 | tf_op jit(solution)/shard_map/ppermute | solution.py:867
  102.9 7.4 %collective-permute-start.32 = (bf16[128,512]{1,0:T(8,128)(2,1)}, bf16[128,512]{1,0:T(8,128)(2,1)S(1)}, u32[]{:S(2)}, u32[]{:S(2)}) collective-permute-start(bf16[128,512]{1,0:T(8,128)(2,1)} %get-tuple-element.71), channel_id=1, source_target_pairs={{2,0},{4,2},{6,4},{3,1},{5,3},{7,5},{10,8},{12,10},{14,12},{11,9},... | collective-permute-start | bytes 393224 | tf_op jit(solution)/shard_map/ppermute | solution.py:867
  111.0 7.9 %collective-permute-start.33 = (bf16[128,512]{1,0:T(8,128)(2,1)}, bf16[128,512]{1,0:T(8,128)(2,1)S(1)}, u32[]{:S(2)}, u32[]{:S(2)}) collective-permute-start(bf16[128,512]{1,0:T(8,128)(2,1)} %get-tuple-element.73), channel_id=1, source_target_pairs={{2,0},{4,2},{6,4},{3,1},{5,3},{7,5},{10,8},{12,10},{14,12},{11,9},... | collective-permute-start | bytes 393224 | tf_op jit(solution)/shard_map/ppermute | solution.py:867
  112.3 8.0 %collective-permute-start.31 = (bf16[128,512]{1,0:T(8,128)(2,1)}, bf16[128,512]{1,0:T(8,128)(2,1)S(1)}, u32[]{:S(2)}, u32[]{:S(2)}) collective-permute-start(bf16[128,512]{1,0:T(8,128)(2,1)} %get-tuple-element.70), channel_id=1, source_target_pairs={{2,0},{4,2},{6,4},{3,1},{5,3},{7,5},{10,8},{12,10},{14,12},{11,9},... | collective-permute-start | bytes 393224 | tf_op jit(solution)/shard_map/ppermute | solution.py:867
  (15 other events, 113.4 us)
where the time goes:
time: 122 us; the launch traced here: 121 us
  starting transfers between devices  47.5 us (39%)
  waiting for transfers between devices  36.6 us (30%)
  Pallas kernels  30.8 us (25%)
  local copies, waits for them, and re-layouts  5.08 us (4%)
  between operations  1.22 us (1%)
    ppermute x12, waiting for transfers between devices, lowered(): return [lax.ppermute(array, 'section', down) for array in arrays]  18.8 us
    ppermute x12, starting transfers between devices, lowered(): return [lax.ppermute(array, 'section', down) for array in arrays]  15.5 us
    ppermute x3, starting transfers between devices, raised(): lax.ppermute(array, 'section', [(i, i + by) for i in range(sections - by)])  10.7 us
    pallas_call x1, Pallas kernels, serial(): pl.pallas_call(kernel, out_shape=[pltpu.VMEM((tokens, wide + head), BF16)...  8.9 us
    ppermute x6, starting transfers between devices, swapped(): return lax.ppermute(array, ('dp', 'group'), pairs)  8.29 us
    ppermute x6, waiting for transfers between devices, swapped(): return lax.ppermute(array, ('dp', 'group'), pairs)  8.06 us
    ppermute x3, starting transfers between devices, shifted(): lax.ppermute(array, 'section', [(i, (i + by) % sections) for i in range(s...  6.29 us
    ppermute x3, waiting for transfers between devices, facing(): lax.ppermute(array, 'section', [(i, i ^ by) for i in range(sections)])  5.96 us
  transfers between devices with their start and end apart: 34, of which 23 were waited for; matrix products, arithmetic and copies ran while one was open for 2% of the time, Pallas kernels for 18%

commit v1 on v0

--- a/solution.py
+++ b/solution.py
@@ -61,16 +61,35 @@
     return pltpu.CompilerParams(vmem_limit_bytes=limit)
 
 
-def pick(tokens, plan, place, groups, out_layer, mine, slice_rows):
+def cut(out_layer, mine, rows):
+    width = out_layer.shape[1]
+
+    def kernel(mine_ref, o_ref, slice_ref, sem):
+        at = pl.ds(pl.multiple_of(mine_ref[0] * rows, rows), rows)
+        copy = pltpu.make_async_copy(o_ref.at[at], slice_ref, sem)
+        copy.start()
+        copy.wait()
+
+    return pl.pallas_call(
+        kernel,
+        out_shape=jax.ShapeDtypeStruct((rows, width), BF16),
+        in_specs=[IN_SMEM, IN_HBM],
+        out_specs=IN_VMEM,
+        scratch_shapes=[pltpu.SemaphoreType.DMA(())],
+        compiler_params=params(SMALL),
+        name="cut",
+    )(mine, in_hbm(out_layer))
+
+
+def pick(tokens, plan, place, groups, after):
     rows, length, width = tokens.shape
     share = rows // groups
 
-    def kernel(plan_ref, place_ref, mine_ref, tokens_ref, o_ref, *rest):
-        slice_ref, parts = rest[0], rest[1 : 1 + groups]
-        slice_in, rows_in, sems = rest[1 + groups :]
+    def kernel(plan_ref, place_ref, tokens_ref, *rest):
+        parts = rest[len(after) : len(after) + groups]
+        rows_in, sems = rest[len(after) + groups :]
         start = mover(sems)
-        at = pl.ds(pl.multiple_of(mine_ref[0] * slice_rows, slice_rows), slice_rows)
-        loads = [(start(o_ref.at[at], slice_in), slice_in, slice_ref)]
+        loads = []
         for r in range(groups):
             target = lax.rem(place_ref[0] + r, groups)
             for c in range(share):
@@ -86,18 +105,16 @@
 
     return pl.pallas_call(
         kernel,
-        out_shape=[pltpu.HBM((slice_rows, width), BF16)]
-        + [pltpu.HBM((share, length, width), BF16)] * groups,
-        in_specs=[IN_SMEM, IN_SMEM, IN_SMEM, IN_HBM, IN_HBM],
-        out_specs=[IN_HBM] * (1 + groups),
+        out_shape=[pltpu.HBM((share, length, width), BF16)] * groups,
+        in_specs=[IN_SMEM, IN_SMEM, IN_HBM] + [ANYWHERE] * len(after),
+        out_specs=[IN_HBM] * groups,
         scratch_shapes=[
-            pltpu.VMEM((slice_rows, width), BF16),
             pltpu.VMEM((rows, length, width), BF16),
-            pltpu.SemaphoreType.DMA((2 * rows + 2,)),
+            pltpu.SemaphoreType.DMA((2 * rows,)),
         ],
         compiler_params=params(),
         name="pick",
-    )(plan, place, mine, in_hbm(tokens), in_hbm(out_layer))
+    )(plan, place, in_hbm(tokens), *after)
 
 
 def project(parts, cotangent, gain, w_layer, out_layer, place, after):
@@ -789,15 +806,8 @@
 
     slice_rows = head // plane
     mine = lax.axis_index("dp") * groups + member
-    own_rows, *parts = pick(
-        tokens_in.reshape(rows_dev, length, width),
-        plan,
-        place,
-        groups,
-        out_layer,
-        mine.astype(jnp.int32)[None],
-        slice_rows,
-    )
+    own_rows = cut(out_layer, mine.astype(jnp.int32)[None], slice_rows)
+    parts = pick(tokens_in.reshape(rows_dev, length, width), plan, place, groups, [own_rows])
     slices = [raised(own_rows, r) for r in range(sections - 1, 0, -1)]
     slices = [own_rows] + slices[::-1]
     chosen = jnp.take(segments, plan[0], axis=0, mode="clip").astype(BF16)
@@ -831,7 +841,7 @@
     def facing(array, by):
         return lax.ppermute(array, "section", [(i, i ^ by) for i in range(sections)])
 
-    arrays, masks, by = [hold(xz, others)], [0], sections // 2
+    arrays, masks, by = [hold(xz, others[:1])], [0], sections // 2
     while by > 0:
         arrays = arrays + [facing(array, by) for array in arrays]
         masks = masks + [mask_of ^ by for mask_of in masks]

time: 122 us -> 123 us (level)
  starting transfers between devices: 47.5 us -> 39.8 us
  waiting for transfers between devices: 36.6 us -> 44.3 us
    ppermute x3, starting transfers between devices: 6.29 us -> 2.1 us  [shifted(): lax.ppermute(array, 'section', [(i, (i + by) % sections) for i in range(s...]
    ppermute x3, waiting for transfers between devices: 0.14 us -> 3.67 us  [shifted(): lax.ppermute(array, 'section', [(i, (i + by) % sections) for i in range(s...]
    ppermute x3, waiting for transfers between devices: 5.96 us -> 9.25 us  [facing(): lax.ppermute(array, 'section', [(i, i ^ by) for i in range(sections)])]
    ppermute x3, starting transfers between devices: 5.01 us -> 2.17 us  [facing(): lax.ppermute(array, 'section', [(i, i ^ by) for i in range(sections)])]
    pallas_call x1 -> x2, Pallas kernels: 2.7 us -> 3.56 us  [the longest x1 2.64 us: pick(): pl.pallas_call(kernel, out_shape=[pltpu.HBM((share, length, width), BF16)...]
    unnamed x27 -> x23, local copies, waits for them, and re-layouts: 3.85 us -> 3.79 us
  transfers between devices with their start and end apart: 34 -> 34, of which waited for: 23 -> 25; matrix products, arithmetic and copies ran while one was open for 2% -> 2% of each run, Pallas kernels for 18% -> 20%
where the time goes in v1:
time: 123 us
  waiting for transfers between devices  44.3 us (36%)
  starting transfers between devices  39.8 us (32%)
  Pallas kernels  31.6 us (26%)
  local copies, waits for them, and re-layouts  5.02 us (4%)
    ppermute x12, waiting for transfers between devices, lowered(): return [lax.ppermute(array, 'section', down) for array in arrays]  18.8 us
    ppermute x12, starting transfers between devices, lowered(): return [lax.ppermute(array, 'section', down) for array in arrays]  15.5 us
    ppermute x3, starting transfers between devices, raised(): lax.ppermute(array, 'section', [(i, i + by) for i in range(sections - by)])  10.7 us
    ppermute x3, waiting for transfers between devices, facing(): lax.ppermute(array, 'section', [(i, i ^ by) for i in range(sections)])  9.25 us
    ppermute x6, waiting for transfers between devices, swapped(): return lax.ppermute(array, ('dp', 'group'), pairs)  8.97 us
    pallas_call x1, Pallas kernels, serial(): pl.pallas_call(kernel, out_shape=[pltpu.VMEM((tokens, wide + head), BF16)...  8.88 us
    ppermute x6, starting transfers between devices, swapped(): return lax.ppermute(array, ('dp', 'group'), pairs)  7.56 us
    pallas_call x1, Pallas kernels, settle(): pl.pallas_call(kernel, out_shape=[pltpu.VMEM((len(cuts), tokens, chunk),...  4.49 us
  transfers between devices with their start and end apart: 34, of which 25 were waited for; matrix products, arithmetic and copies ran while one was open for 2% of the time, Pallas kernels for 20%

profile of v1, /device:TPU:0, one launch (start us, length us, event | category | flops | bytes accessed | tf_op | source)
XLA Modules:
  0.0 122.8 jit_solution(11275041158924550822)
XLA Ops:
  1.6 7.0 %collective-permute-start.1 = (bf16[16,4096]{1,0:T(8,128)(2,1)S(1)}, bf16[16,4096]{1,0:T(8,128)(2,1)S(1)}, u32[]{:S(2)}, u32[]{:S(2)}) collective-permute-start(bf16[16,4096]{1,0:T(8,128)(2,1)S(1)} %cut.1.rest_0_.refs_3_), channel_id=1, source_target_pairs={{0,6},{1,7},{8,14},{9,15},{16,22},{17,23},{24,30},{25,31}} | collective-permute-start | bytes 393224 | tf_op jit(solution)/shard_map/ppermute | solution.py:754
  8.6 1.3 %collective-permute-start.2 = (bf16[16,4096]{1,0:T(8,128)(2,1)S(1)}, bf16[16,4096]{1,0:T(8,128)(2,1)S(1)}, u32[]{:S(2)}, u32[]{:S(2)}) collective-permute-start(bf16[16,4096]{1,0:T(8,128)(2,1)S(1)} %cut.1.rest_0_.refs_3_), channel_id=1, source_target_pairs={{0,4},{2,6},{1,5},{3,7},{8,12},{10,14},{9,13},{11,15},{16,20},{18,... | collective-permute-start | bytes 393224 | tf_op jit(solution)/shard_map/ppermute | solution.py:754
  9.9 2.5 %collective-permute-start.3 = (bf16[16,4096]{1,0:T(8,128)(2,1)S(1)}, bf16[16,4096]{1,0:T(8,128)(2,1)S(1)}, u32[]{:S(2)}, u32[]{:S(2)}) collective-permute-start(bf16[16,4096]{1,0:T(8,128)(2,1)S(1)} %cut.1.rest_0_.refs_3_), channel_id=1, source_target_pairs={{0,2},{2,4},{4,6},{1,3},{3,5},{5,7},{8,10},{10,12},{12,14},{9,11},... | collective-permute-start | bytes 393224 | tf_op jit(solution)/shard_map/ppermute | solution.py:754
  14.4 2.6 %pick.1 = (bf16[4,16,4096]{2,1,0:T(8,128)(2,1)}, bf16[4,16,4096]{2,1,0:T(8,128)(2,1)}) custom-call(s32[1,8]{1,0:T(1,128)S(1)} %copy-done.9, s32[1]{0:T(128)} %bitcast.9.place_ref, bf16[8,16,4096]{2,1,0:T(8,128)(2,1)} %bitcast.45, bf16[16,4096]{1,0:T(8,128)(2,1)S(1)} %cut.1.rest_0_.refs_3_), custom_call_target="tpu_custom_call" | custom-call | tf_op jit(solution)/shard_map/pick/pallas_call | solution.py:106
  20.4 3.5 %project.1 = (bf16[128,4096]{1,0:T(8,128)(2,1)}, bf16[128,640]{1,0:T(8,128)(2,1)S(1)}, f32[128,1]{1,0:T(8,128)S(1)}) custom-call(s32[1]{0:T(128)} %bitcast.9.place_ref, bf16[64,4096]{1,0:T(8,128)(2,1)S(1)} %bitcast.30, bf16[64,4096]{1,0:T(8,128)(2,1)S(1)} %bitcast.31, bf16[128,4096]{1,0:T(8,128)(2,1)} %c_ref.1, f32[1,4096]{1,0:T(1,128)S(1)} %copy-done.6, ...), custom_call_target="tpu_custom_call" | custom-call | tf_op jit(solution)/shard_map/project/pallas_call | solution.py:167
  24.0 3.4 %couple.1 = (bf16[16,1152]{1,0:T(8,128)(2,1)S(1)}, bf16[3,16,4096]{2,1,0:T(8,128)(2,1)}) custom-call(s32[1]{0:T(128)} %bitcast.16.last_ref, bf16[16,4096]{1,0:T(8,128)(2,1)S(1)} %collective-permute-done.1.refs_0_, bf16[16,4096]{1,0:T(8,128)(2,1)S(1)} %collective-permute-done.2.refs_1_, bf16[16,4096]{1,0:T(8,128)(2,1)S(1)} %collective-permute-done.3.refs_2_, ...), custom_call_target="tpu_custom_call" | custom-call | tf_op jit(solution)/shard_map/couple/pallas_call | solution.py:249
  27.5 2.0 %collective-permute-start.5 = (bf16[16,1152]{1,0:T(8,128)(2,1)S(1)}, bf16[16,1152]{1,0:T(8,128)(2,1)S(1)}, u32[]{:S(2)}, u32[]{:S(2)}) collective-permute-start(bf16[16,1152]{1,0:T(8,128)(2,1)S(1)} %get-tuple-element.41.refs_0_), channel_id=1, source_target_pairs={{0,2},{2,4},{4,6},{6,0},{1,3},{3,5},{5,7},{7,1},{8,10},{10,12},{12... | collective-permute-start | bytes 110600 | tf_op jit(solution)/shard_map/ppermute | solution.py:749
  29.5 1.5 %collective-permute-start.18 = (bf16[1,3,16,4096]{3,2,1,0:T(8,128)(2,1)}, bf16[1,3,16,4096]{3,2,1,0:T(8,128)(2,1)S(1)}, u32[]{:S(2)}, u32[]{:S(2)}) collective-permute-start(bf16[1,3,16,4096]{3,2,1,0:T(8,128)(2,1)} %bitcast.32), channel_id=1, source_target_pairs={{0,8},{1,17},{8,0},{9,25},{16,24},{17,1},{24,16},{25,9},{2,10},{3,... | collective-permute-start | bytes 1179656 | tf_op jit(solution)/shard_map/ppermute | solution.py:765
  31.5 2.1 %collective-permute-done.5.refs_1_ = bf16[16,1152]{1,0:T(8,128)(2,1)S(1)} collective-permute-done((bf16[16,1152]{1,0:T(8,128)(2,1)S(1)}, bf16[16,1152]{1,0:T(8,128)(2,1)S(1)}, u32[]{:S(2)}, u32[]{:S(2)}) %collective-permute-start.5) | collective-permute-done | bytes 36896 | tf_op jit(solution)/shard_map/ppermute | solution.py:749
  34.8 2.1 %collective-permute-start.7 = (bf16[128,640]{1,0:T(8,128)(2,1)S(1)}, bf16[128,640]{1,0:T(8,128)(2,1)S(1)}, u32[]{:S(2)}, u32[]{:S(2)}) collective-permute-start(bf16[128,640]{1,0:T(8,128)(2,1)S(1)} %hold.4.refs_0_), channel_id=1, source_target_pairs={{0,4},{2,6},{4,0},{6,2},{1,5},{3,7},{5,1},{7,3},{8,12},{10,14},{12... | collective-permute-start | bytes 491528 | tf_op jit(solution)/shard_map/ppermute | solution.py:842
  36.9 1.5 %collective-permute-start.11 = (bf16[1,16,3072]{2,1,0:T(8,128)(2,1)S(1)}, bf16[1,16,3072]{2,1,0:T(8,128)(2,1)S(1)}, u32[]{:S(2)}, u32[]{:S(2)}) collective-permute-start(bf16[1,16,3072]{2,1,0:T(8,128)(2,1)S(1)} %compact.1.first_ref), channel_id=1, source_target_pairs={{0,8},{1,17},{8,0},{9,25},{16,24},{17,1},{24,16},{25,9},{2,10},{3,... | collective-permute-start | bytes 294920 | tf_op jit(solution)/shard_map/ppermute | solution.py:765
  38.4 3.1 %collective-permute-done.11.second_ref = bf16[1,16,3072]{2,1,0:T(8,128)(2,1)S(1)} collective-permute-done((bf16[1,16,3072]{2,1,0:T(8,128)(2,1)S(1)}, bf16[1,16,3072]{2,1,0:T(8,128)(2,1)S(1)}, u32[]{:S(2)}, u32[]{:S(2)}) %collective-permute-start.11) | collective-permute-done | bytes 98336 | tf_op jit(solution)/shard_map/ppermute | solution.py:765
  42.3 3.1 %collective-permute-done.7.refs_1_.refs_2_ = bf16[128,640]{1,0:T(8,128)(2,1)S(1)} collective-permute-done((bf16[128,640]{1,0:T(8,128)(2,1)S(1)}, bf16[128,640]{1,0:T(8,128)(2,1)S(1)}, u32[]{:S(2)}, u32[]{:S(2)}) %collective-permute-start.7) | collective-permute-done | bytes 163872 | tf_op jit(solution)/shard_map/ppermute | solution.py:842
  45.5 1.6 %collective-permute-start.12 = (bf16[2,16,3072]{2,1,0:T(8,128)(2,1)S(1)}, bf16[2,16,3072]{2,1,0:T(8,128)(2,1)S(1)}, u32[]{:S(2)}, u32[]{:S(2)}) collective-permute-start(bf16[2,16,3072]{2,1,0:T(8,128)(2,1)S(1)} %merge.1.refs_4_), channel_id=1, source_target_pairs={{0,16},{1,9},{8,24},{9,1},{16,0},{17,25},{24,8},{25,17},{2,18},{3,... | collective-permute-start | bytes 589832 | tf_op jit(solution)/shard_map/ppermute | solution.py:765
  47.0 5.3 %collective-permute-done.8.refs_1_.refs_3_ = bf16[128,640]{1,0:T(8,128)(2,1)S(1)} collective-permute-done((bf16[128,640]{1,0:T(8,128)(2,1)S(1)}, bf16[128,640]{1,0:T(8,128)(2,1)S(1)}, u32[]{:S(2)}, u32[]{:S(2)}) %collective-permute-start.8) | collective-permute-done | bytes 163872 | tf_op jit(solution)/shard_map/ppermute | solution.py:842
  55.7 8.9 %serial.1 = (bf16[128,512]{1,0:T(8,128)(2,1)S(1)}, f32[128,1]{1,0:T(8,128)S(1)}, bf16[128,384]{1,0:T(8,128)(2,1)S(1)}, bf16[128,512]{1,0:T(8,128)(2,1)}, bf16[128,512]{1,0:T(8,128)(2,1)}) custom-call(s32[1]{0:T(128)} %bitcast.6.s_ref, s32[8]{0:T(128)S(1)} %pad_add_fusion.refs_8_.p_ref, bf16[128,640]{1,0:T(8,128)(2,1)S(1)} %hold.4.refs_0_, ...), custom_call_target="tpu_custom_call" | custom-call | tf_op jit(solution)/shard_map/serial/pallas_call | solution.py:459
  66.5 1.3 %collective-permute-start.17 = (bf16[128,512]{1,0:T(8,128)(2,1)}, bf16[128,512]{1,0:T(8,128)(2,1)S(1)}, u32[]{:S(2)}, u32[]{:S(2)}) collective-permute-start(bf16[128,512]{1,0:T(8,128)(2,1)} %get-tuple-element.47), channel_id=1, source_target_pairs={{2,0},{4,2},{6,4},{3,1},{5,3},{7,5},{10,8},{12,10},{14,12},{11,9},... | collective-permute-start | bytes 393224 | tf_op jit(solution)/shard_map/ppermute | solution.py:877
  67.8 3.8 %widen.1 = (bf16[128,4096]{1,0:T(8,128)(2,1)}, bf16[2,4,128,1024]{3,2,1,0:T(8,128)(2,1)S(1)}) custom-call(bf16[128,512]{1,0:T(8,128)(2,1)S(1)} %get-tuple-element.44.v_ref, f32[1,4096]{1,0:T(1,128)S(1)} %copy-done.6, bf16[4096,384]{1,0:T(8,128)(2,1)} %bitcast.38, bf16[128,4096]{1,0:T(8,128)(2,1)} %bitcast.43), custom_call_target="tpu_custom_call" | custom-call | tf_op jit(solution)/shard_map/widen/pallas_call | solution.py:556
  71.7 2.0 %collective-permute-done.15.r_ref = bf16[128,512]{1,0:T(8,128)(2,1)S(1)} collective-permute-done((bf16[128,512]{1,0:T(8,128)(2,1)}, bf16[128,512]{1,0:T(8,128)(2,1)S(1)}, u32[]{:S(2)}, u32[]{:S(2)}) %collective-permute-start.15) | collective-permute-done | bytes 131104 | tf_op jit(solution)/shard_map/ppermute | solution.py:877
  73.7 2.1 %collective-permute-done.17.r_ref = bf16[128,512]{1,0:T(8,128)(2,1)S(1)} collective-permute-done((bf16[128,512]{1,0:T(8,128)(2,1)}, bf16[128,512]{1,0:T(8,128)(2,1)S(1)}, u32[]{:S(2)}, u32[]{:S(2)}) %collective-permute-start.17) | collective-permute-done | bytes 131104 | tf_op jit(solution)/shard_map/ppermute | solution.py:877
  77.7 1.3 %collective-permute-start.23 = (bf16[128,512]{1,0:T(8,128)(2,1)S(1)}, bf16[128,512]{1,0:T(8,128)(2,1)S(1)}, u32[]{:S(2)}, u32[]{:S(2)}) collective-permute-start(bf16[128,512]{1,0:T(8,128)(2,1)S(1)} %get-tuple-element.55.refs_2_), channel_id=1, source_target_pairs={{2,0},{4,2},{6,4},{3,1},{5,3},{7,5},{10,8},{12,10},{14,12},{11,9},... | collective-permute-start | bytes 393224 | tf_op jit(solution)/shard_map/ppermute | solution.py:877
  80.3 4.5 %settle.1 = (bf16[4,128,1024]{2,1,0:T(8,128)(2,1)S(1)}, f32[32,128]{1,0:T(8,128)S(1)}) custom-call(s32[8]{0:T(128)S(1)} %pad_add_fusion.refs_8_.p_ref, f32[128,1]{1,0:T(8,128)S(1)} %copy-done.8, bf16[128,384]{1,0:T(8,128)(2,1)S(1)} %get-tuple-element.51.a_ref, bf16[128,4096]{1,0:T(8,128)(2,1)} %get-tuple-element.52.x_ref, bf16[128,4096]{1,0:T(8,128)(2,1)} %c_ref.1, ...), custom_call_target="tpu_custom_call" | custom-call | tf_op jit(solution)/shard_map/settle/pallas_call | solution.py:616
  84.9 1.3 %collective-permute-start.22 = (bf16[128,512]{1,0:T(8,128)(2,1)S(1)}, bf16[128,512]{1,0:T(8,128)(2,1)S(1)}, u32[]{:S(2)}, u32[]{:S(2)}) collective-permute-start(bf16[128,512]{1,0:T(8,128)(2,1)S(1)} %get-tuple-element.57), channel_id=1, source_target_pairs={{2,0},{4,2},{6,4},{3,1},{5,3},{7,5},{10,8},{12,10},{14,12},{11,9},... | collective-permute-start | bytes 393224 | tf_op jit(solution)/shard_map/ppermute | solution.py:877
  88.8 2.9 %collective-permute-done.24.refs_1_ = f32[32,128]{1,0:T(8,128)S(1)} collective-permute-done((f32[32,128]{1,0:T(8,128)S(1)}, f32[32,128]{1,0:T(8,128)S(1)}, u32[]{:S(2)}, u32[]{:S(2)}) %collective-permute-start.24) | collective-permute-done | bytes 16416 | tf_op jit(solution)/shard_map/ppermute | solution.py:765
  91.8 2.2 %collective-permute-done.22.r_ref = bf16[128,512]{1,0:T(8,128)(2,1)S(1)} collective-permute-done((bf16[128,512]{1,0:T(8,128)(2,1)S(1)}, bf16[128,512]{1,0:T(8,128)(2,1)S(1)}, u32[]{:S(2)}, u32[]{:S(2)}) %collective-permute-start.22) | collective-permute-done | bytes 131104 | tf_op jit(solution)/shard_map/ppermute | solution.py:877
  94.0 1.3 %collective-permute-start.25 = (bf16[128,512]{1,0:T(8,128)(2,1)S(1)}, bf16[128,512]{1,0:T(8,128)(2,1)S(1)}, u32[]{:S(2)}, u32[]{:S(2)}) collective-permute-start(bf16[128,512]{1,0:T(8,128)(2,1)S(1)} %get-tuple-element.60), channel_id=1, source_target_pairs={{2,0},{4,2},{6,4},{3,1},{5,3},{7,5},{10,8},{12,10},{14,12},{11,9},... | collective-permute-start | bytes 393224 | tf_op jit(solution)/shard_map/ppermute | solution.py:877
  98.2 2.9 %collective-permute-done.27.refs_1_ = f32[32,128]{1,0:T(8,128)S(1)} collective-permute-done((f32[32,128]{1,0:T(8,128)S(1)}, f32[32,128]{1,0:T(8,128)S(1)}, u32[]{:S(2)}, u32[]{:S(2)}) %collective-permute-start.27) | collective-permute-done | bytes 16416 | tf_op jit(solution)/shard_map/ppermute | solution.py:765
  102.0 1.3 %collective-permute-start.28 = (bf16[128,512]{1,0:T(8,128)(2,1)S(1)}, bf16[128,512]{1,0:T(8,128)(2,1)S(1)}, u32[]{:S(2)}, u32[]{:S(2)}) collective-permute-start(bf16[128,512]{1,0:T(8,128)(2,1)S(1)} %get-tuple-element.64), channel_id=1, source_target_pairs={{2,0},{4,2},{6,4},{3,1},{5,3},{7,5},{10,8},{12,10},{14,12},{11,9},... | collective-permute-start | bytes 393224 | tf_op jit(solution)/shard_map/ppermute | solution.py:877
  106.9 2.9 %collective-permute-done.28.r_ref = bf16[128,512]{1,0:T(8,128)(2,1)S(1)} collective-permute-done((bf16[128,512]{1,0:T(8,128)(2,1)S(1)}, bf16[128,512]{1,0:T(8,128)(2,1)S(1)}, u32[]{:S(2)}, u32[]{:S(2)}) %collective-permute-start.28) | collective-permute-done | bytes 131104 | tf_op jit(solution)/shard_map/ppermute | solution.py:877
  113.7 1.3 %collective-permute-start.31 = (bf16[128,512]{1,0:T(8,128)(2,1)}, bf16[128,512]{1,0:T(8,128)(2,1)S(1)}, u32[]{:S(2)}, u32[]{:S(2)}) collective-permute-start(bf16[128,512]{1,0:T(8,128)(2,1)} %get-tuple-element.68), channel_id=1, source_target_pairs={{2,0},{4,2},{6,4},{3,1},{5,3},{7,5},{10,8},{12,10},{14,12},{11,9},... | collective-permute-start | bytes 393224 | tf_op jit(solution)/shard_map/ppermute | solution.py:877
  115.6 4.6 %collective-permute-done.33.refs_1_ = bf16[128,512]{1,0:T(8,128)(2,1)S(1)} collective-permute-done((bf16[128,512]{1,0:T(8,128)(2,1)}, bf16[128,512]{1,0:T(8,128)(2,1)S(1)}, u32[]{:S(2)}, u32[]{:S(2)}) %collective-permute-start.33) | collective-permute-done | bytes 131104 | tf_op jit(solution)/shard_map/ppermute | solution.py:877
  120.2 1.4 %collective-permute-done.31.refs_0_ = bf16[128,512]{1,0:T(8,128)(2,1)S(1)} collective-permute-done((bf16[128,512]{1,0:T(8,128)(2,1)}, bf16[128,512]{1,0:T(8,128)(2,1)S(1)}, u32[]{:S(2)}, u32[]{:S(2)}) %collective-permute-start.31) | collective-permute-done | bytes 131104 | tf_op jit(solution)/shard_map/ppermute | solution.py:877
  (101 shorter events, 32.9 us)
Async XLA Ops:
  1.6 22.3 %collective-permute-start.1 = (bf16[16,4096]{1,0:T(8,128)(2,1)S(1)}, bf16[16,4096]{1,0:T(8,128)(2,1)S(1)}, u32[]{:S(2)}, u32[]{:S(2)}) collective-permute-start(bf16[16,4096]{1,0:T(8,128)(2,1)S(1)} %cut.1.rest_0_.refs_3_), channel_id=1, source_target_pairs={{0,6},{1,7},{8,14},{9,15},{16,22},{17,23},{24,30},{25,31}} | collective-permute-start | bytes 393224 | tf_op jit(solution)/shard_map/ppermute | solution.py:754
  8.6 15.4 %collective-permute-start.2 = (bf16[16,4096]{1,0:T(8,128)(2,1)S(1)}, bf16[16,4096]{1,0:T(8,128)(2,1)S(1)}, u32[]{:S(2)}, u32[]{:S(2)}) collective-permute-start(bf16[16,4096]{1,0:T(8,128)(2,1)S(1)} %cut.1.rest_0_.refs_3_), channel_id=1, source_target_pairs={{0,4},{2,6},{1,5},{3,7},{8,12},{10,14},{9,13},{11,15},{16,20},{18,... | collective-permute-start | bytes 393224 | tf_op jit(solution)/shard_map/ppermute | solution.py:754
  9.9 14.1 %collective-permute-start.3 = (bf16[16,4096]{1,0:T(8,128)(2,1)S(1)}, bf16[16,4096]{1,0:T(8,128)(2,1)S(1)}, u32[]{:S(2)}, u32[]{:S(2)}) collective-permute-start(bf16[16,4096]{1,0:T(8,128)(2,1)S(1)} %cut.1.rest_0_.refs_3_), channel_id=1, source_target_pairs={{0,2},{2,4},{4,6},{1,3},{3,5},{5,7},{8,10},{10,12},{12,14},{9,11},... | collective-permute-start | bytes 393224 | tf_op jit(solution)/shard_map/ppermute | solution.py:754
  13.6 4.1 %collective-permute-start.4 = (bf16[4,16]{1,0:T(4,128)(2,1)S(1)}, bf16[4,16]{1,0:T(4,128)(2,1)S(1)}, u32[]{:S(2)}, u32[]{:S(2)}) collective-permute-start(bf16[4,16]{1,0:T(4,128)(2,1)S(1)} %get-tuple-element.75), channel_id=1, source_target_pairs={{0,1},{1,0},{2,3},{3,2},{4,5},{5,4},{6,7},{7,6},{8,9},{9,8},{10,11... | collective-permute-start | bytes 392 | tf_op jit(solution)/shard_map/ppermute | solution.py:770
  17.0 2.3 %collective-permute-start = (bf16[4,16,4096]{2,1,0:T(8,128)(2,1)}, bf16[4,16,4096]{2,1,0:T(8,128)(2,1)S(1)}, u32[]{:S(2)}, u32[]{:S(2)}) collective-permute-start(bf16[4,16,4096]{2,1,0:T(8,128)(2,1)} %get-tuple-element.39), channel_id=1, source_target_pairs={{0,1},{1,0},{2,3},{3,2},{4,5},{5,4},{6,7},{7,6},{8,9},{9,8},{10,11... | collective-permute-start | bytes 1572872 | tf_op jit(solution)/shard_map/ppermute | solution.py:770
  27.4 4.0 %collective-permute-start.10 = (bf16[16,1152]{1,0:T(8,128)(2,1)S(1)}, bf16[16,1152]{1,0:T(8,128)(2,1)S(1)}, u32[]{:S(2)}, u32[]{:S(2)}) collective-permute-start(bf16[16,1152]{1,0:T(8,128)(2,1)S(1)} %get-tuple-element.41.refs_0_), channel_id=1, source_target_pairs={{0,6},{2,0},{4,2},{6,4},{1,7},{3,1},{5,3},{7,5},{8,14},{10,8},{12,... | collective-permute-start | bytes 110600 | tf_op jit(solution)/shard_map/ppermute | solution.py:749
  27.5 6.1 %collective-permute-start.5 = (bf16[16,1152]{1,0:T(8,128)(2,1)S(1)}, bf16[16,1152]{1,0:T(8,128)(2,1)S(1)}, u32[]{:S(2)}, u32[]{:S(2)}) collective-permute-start(bf16[16,1152]{1,0:T(8,128)(2,1)S(1)} %get-tuple-element.41.refs_0_), channel_id=1, source_target_pairs={{0,2},{2,4},{4,6},{6,0},{1,3},{3,5},{5,7},{7,1},{8,10},{10,12},{12... | collective-permute-start | bytes 110600 | tf_op jit(solution)/shard_map/ppermute | solution.py:749
  29.5 5.2 %collective-permute-start.9 = (bf16[16,1152]{1,0:T(8,128)(2,1)S(1)}, bf16[16,1152]{1,0:T(8,128)(2,1)S(1)}, u32[]{:S(2)}, u32[]{:S(2)}) collective-permute-start(bf16[16,1152]{1,0:T(8,128)(2,1)S(1)} %get-tuple-element.41.refs_0_), channel_id=1, source_target_pairs={{0,4},{2,6},{4,0},{6,2},{1,5},{3,7},{5,1},{7,3},{8,12},{10,14},{12... | collective-permute-start | bytes 110600 | tf_op jit(solution)/shard_map/ppermute | solution.py:749
  29.5 22.8 %collective-permute-start.18 = (bf16[1,3,16,4096]{3,2,1,0:T(8,128)(2,1)}, bf16[1,3,16,4096]{3,2,1,0:T(8,128)(2,1)S(1)}, u32[]{:S(2)}, u32[]{:S(2)}) collective-permute-start(bf16[1,3,16,4096]{3,2,1,0:T(8,128)(2,1)} %bitcast.32), channel_id=1, source_target_pairs={{0,8},{1,17},{8,0},{9,25},{16,24},{17,1},{24,16},{25,9},{2,10},{3,... | collective-permute-start | bytes 1179656 | tf_op jit(solution)/shard_map/ppermute | solution.py:765
  34.7 7.6 %collective-permute-start.6 = (bf16[128,640]{1,0:T(8,128)(2,1)S(1)}, bf16[128,640]{1,0:T(8,128)(2,1)S(1)}, u32[]{:S(2)}, u32[]{:S(2)}) collective-permute-start(bf16[128,640]{1,0:T(8,128)(2,1)S(1)} %hold.4.refs_0_), channel_id=1, source_target_pairs={{0,2},{2,0},{4,6},{6,4},{1,3},{3,1},{5,7},{7,5},{8,10},{10,8},{12,... | collective-permute-start | bytes 491528 | tf_op jit(solution)/shard_map/ppermute | solution.py:842
  34.8 10.6 %collective-permute-start.7 = (bf16[128,640]{1,0:T(8,128)(2,1)S(1)}, bf16[128,640]{1,0:T(8,128)(2,1)S(1)}, u32[]{:S(2)}, u32[]{:S(2)}) collective-permute-start(bf16[128,640]{1,0:T(8,128)(2,1)S(1)} %hold.4.refs_0_), channel_id=1, source_target_pairs={{0,4},{2,6},{4,0},{6,2},{1,5},{3,7},{5,1},{7,3},{8,12},{10,14},{12... | collective-permute-start | bytes 491528 | tf_op jit(solution)/shard_map/ppermute | solution.py:842
  36.9 4.6 %collective-permute-start.11 = (bf16[1,16,3072]{2,1,0:T(8,128)(2,1)S(1)}, bf16[1,16,3072]{2,1,0:T(8,128)(2,1)S(1)}, u32[]{:S(2)}, u32[]{:S(2)}) collective-permute-start(bf16[1,16,3072]{2,1,0:T(8,128)(2,1)S(1)} %compact.1.first_ref), channel_id=1, source_target_pairs={{0,8},{1,17},{8,0},{9,25},{16,24},{17,1},{24,16},{25,9},{2,10},{3,... | collective-permute-start | bytes 294920 | tf_op jit(solution)/shard_map/ppermute | solution.py:765
  45.5 6.9 %collective-permute-start.12 = (bf16[2,16,3072]{2,1,0:T(8,128)(2,1)S(1)}, bf16[2,16,3072]{2,1,0:T(8,128)(2,1)S(1)}, u32[]{:S(2)}, u32[]{:S(2)}) collective-permute-start(bf16[2,16,3072]{2,1,0:T(8,128)(2,1)S(1)} %merge.1.refs_4_), channel_id=1, source_target_pairs={{0,16},{1,9},{8,24},{9,1},{16,0},{17,25},{24,8},{25,17},{2,18},{3,... | collective-permute-start | bytes 589832 | tf_op jit(solution)/shard_map/ppermute | solution.py:765
  47.0 5.3 %collective-permute-start.8 = (bf16[128,640]{1,0:T(8,128)(2,1)S(1)}, bf16[128,640]{1,0:T(8,128)(2,1)S(1)}, u32[]{:S(2)}, u32[]{:S(2)}) collective-permute-start(bf16[128,640]{1,0:T(8,128)(2,1)S(1)} %collective-permute-done.7.refs_1_.refs_2_), channel_id=1, source_target_pairs={{0,2},{2,0},{4,6},{6,4},{1,3},{3,1},{5,7},{7,5},{8,10},{10,8},{12,... | collective-permute-start | bytes 491528 | tf_op jit(solution)/shard_map/ppermute | solution.py:842
  52.8 23.1 %collective-permute-start.19 = (bf16[2,3,16,4096]{3,2,1,0:T(8,128)(2,1)S(1)}, bf16[2,3,16,4096]{3,2,1,0:T(8,128)(2,1)}, u32[]{:S(2)}, u32[]{:S(2)}) collective-permute-start(bf16[2,3,16,4096]{3,2,1,0:T(8,128)(2,1)S(1)} %gather_two.1.refs_0_), channel_id=1, source_target_pairs={{0,16},{1,9},{8,24},{9,1},{16,0},{17,25},{24,8},{25,17},{2,18},{3,... | collective-permute-start | bytes 2359304 | tf_op jit(solution)/shard_map/ppermute | solution.py:765
  54.0 1.7 %collective-permute-start.14 = (bf16[2,16,3072]{2,1,0:T(8,128)(2,1)S(1)}, bf16[2,16,3072]{2,1,0:T(8,128)(2,1)S(1)}, u32[]{:S(2)}, u32[]{:S(2)}) collective-permute-start(bf16[2,16,3072]{2,1,0:T(8,128)(2,1)S(1)} %hold.5.refs_5_.refs_0_), channel_id=1, source_target_pairs={{0,1},{1,0},{2,3},{3,2},{4,5},{5,4},{6,7},{7,6},{8,9},{9,8},{10,11... | collective-permute-start | bytes 589832 | tf_op jit(solution)/shard_map/ppermute | solution.py:770
  65.3 8.4 %collective-permute-start.15 = (bf16[128,512]{1,0:T(8,128)(2,1)}, bf16[128,512]{1,0:T(8,128)(2,1)S(1)}, u32[]{:S(2)}, u32[]{:S(2)}) collective-permute-start(bf16[128,512]{1,0:T(8,128)(2,1)} %get-tuple-element.43), channel_id=1, source_target_pairs={{2,0},{4,2},{6,4},{3,1},{5,3},{7,5},{10,8},{12,10},{14,12},{11,9},... | collective-permute-start | bytes 393224 | tf_op jit(solution)/shard_map/ppermute | solution.py:877
  66.5 9.2 %collective-permute-start.17 = (bf16[128,512]{1,0:T(8,128)(2,1)}, bf16[128,512]{1,0:T(8,128)(2,1)S(1)}, u32[]{:S(2)}, u32[]{:S(2)}) collective-permute-start(bf16[128,512]{1,0:T(8,128)(2,1)} %get-tuple-element.47), channel_id=1, source_target_pairs={{2,0},{4,2},{6,4},{3,1},{5,3},{7,5},{10,8},{12,10},{14,12},{11,9},... | collective-permute-start | bytes 393224 | tf_op jit(solution)/shard_map/ppermute | solution.py:877
  75.9 3.2 %collective-permute-start.21 = (bf16[2,3,16,4096]{3,2,1,0:T(8,128)(2,1)}, bf16[2,3,16,4096]{3,2,1,0:T(8,128)(2,1)}, u32[]{:S(2)}, u32[]{:S(2)}) collective-permute-start(bf16[2,3,16,4096]{3,2,1,0:T(8,128)(2,1)} %hold.7.refs_1_), channel_id=1, source_target_pairs={{0,1},{1,0},{2,3},{3,2},{4,5},{5,4},{6,7},{7,6},{8,9},{9,8},{10,11... | collective-permute-start | bytes 2359304 | tf_op jit(solution)/shard_map/ppermute | solution.py:770
  75.9 3.5 %collective-permute-start.20 = (bf16[2,3,16,4096]{3,2,1,0:T(8,128)(2,1)S(1)}, bf16[2,3,16,4096]{3,2,1,0:T(8,128)(2,1)}, u32[]{:S(2)}, u32[]{:S(2)}) collective-permute-start(bf16[2,3,16,4096]{3,2,1,0:T(8,128)(2,1)S(1)} %hold.6.refs_0_), channel_id=1, source_target_pairs={{0,1},{1,0},{2,3},{3,2},{4,5},{5,4},{6,7},{7,6},{8,9},{9,8},{10,11... | collective-permute-start | bytes 2359304 | tf_op jit(solution)/shard_map/ppermute | solution.py:770
  76.4 8.4 %collective-permute-start.16 = (bf16[128,512]{1,0:T(8,128)(2,1)S(1)}, bf16[128,512]{1,0:T(8,128)(2,1)S(1)}, u32[]{:S(2)}, u32[]{:S(2)}) collective-permute-start(bf16[128,512]{1,0:T(8,128)(2,1)S(1)} %get-tuple-element.46.refs_1_), channel_id=1, source_target_pairs={{2,0},{4,2},{6,4},{3,1},{5,3},{7,5},{10,8},{12,10},{14,12},{11,9},... | collective-permute-start | bytes 393224 | tf_op jit(solution)/shard_map/ppermute | solution.py:877
  77.7 8.9 %collective-permute-start.23 = (bf16[128,512]{1,0:T(8,128)(2,1)S(1)}, bf16[128,512]{1,0:T(8,128)(2,1)S(1)}, u32[]{:S(2)}, u32[]{:S(2)}) collective-permute-start(bf16[128,512]{1,0:T(8,128)(2,1)S(1)} %get-tuple-element.55.refs_2_), channel_id=1, source_target_pairs={{2,0},{4,2},{6,4},{3,1},{5,3},{7,5},{10,8},{12,10},{14,12},{11,9},... | collective-permute-start | bytes 393224 | tf_op jit(solution)/shard_map/ppermute | solution.py:877
  84.9 9.0 %collective-permute-start.22 = (bf16[128,512]{1,0:T(8,128)(2,1)S(1)}, bf16[128,512]{1,0:T(8,128)(2,1)S(1)}, u32[]{:S(2)}, u32[]{:S(2)}) collective-permute-start(bf16[128,512]{1,0:T(8,128)(2,1)S(1)} %get-tuple-element.57), channel_id=1, source_target_pairs={{2,0},{4,2},{6,4},{3,1},{5,3},{7,5},{10,8},{12,10},{14,12},{11,9},... | collective-permute-start | bytes 393224 | tf_op jit(solution)/shard_map/ppermute | solution.py:877
  86.7 9.3 %collective-permute-start.26 = (bf16[128,512]{1,0:T(8,128)(2,1)S(1)}, bf16[128,512]{1,0:T(8,128)(2,1)S(1)}, u32[]{:S(2)}, u32[]{:S(2)}) collective-permute-start(bf16[128,512]{1,0:T(8,128)(2,1)S(1)} %get-tuple-element.61), channel_id=1, source_target_pairs={{2,0},{4,2},{6,4},{3,1},{5,3},{7,5},{10,8},{12,10},{14,12},{11,9},... | collective-permute-start | bytes 393224 | tf_op jit(solution)/shard_map/ppermute | solution.py:877
  88.0 3.8 %collective-permute-start.24 = (f32[32,128]{1,0:T(8,128)S(1)}, f32[32,128]{1,0:T(8,128)S(1)}, u32[]{:S(2)}, u32[]{:S(2)}) collective-permute-start(f32[32,128]{1,0:T(8,128)S(1)} %stacked.1.refs_0_), channel_id=1, source_target_pairs={{0,8},{1,17},{8,0},{9,25},{16,24},{17,1},{24,16},{25,9},{2,10},{3,... | collective-permute-start | bytes 49160 | tf_op jit(solution)/shard_map/ppermute | solution.py:765
  94.0 8.0 %collective-permute-start.25 = (bf16[128,512]{1,0:T(8,128)(2,1)S(1)}, bf16[128,512]{1,0:T(8,128)(2,1)S(1)}, u32[]{:S(2)}, u32[]{:S(2)}) collective-permute-start(bf16[128,512]{1,0:T(8,128)(2,1)S(1)} %get-tuple-element.60), channel_id=1, source_target_pairs={{2,0},{4,2},{6,4},{3,1},{5,3},{7,5},{10,8},{12,10},{14,12},{11,9},... | collective-permute-start | bytes 393224 | tf_op jit(solution)/shard_map/ppermute | solution.py:877
  96.0 7.7 %collective-permute-start.29 = (bf16[128,512]{1,0:T(8,128)(2,1)S(1)}, bf16[128,512]{1,0:T(8,128)(2,1)S(1)}, u32[]{:S(2)}, u32[]{:S(2)}) collective-permute-start(bf16[128,512]{1,0:T(8,128)(2,1)S(1)} %get-tuple-element.65), channel_id=1, source_target_pairs={{2,0},{4,2},{6,4},{3,1},{5,3},{7,5},{10,8},{12,10},{14,12},{11,9},... | collective-permute-start | bytes 393224 | tf_op jit(solution)/shard_map/ppermute | solution.py:877
  97.3 3.8 %collective-permute-start.27 = (f32[32,128]{1,0:T(8,128)S(1)}, f32[32,128]{1,0:T(8,128)S(1)}, u32[]{:S(2)}, u32[]{:S(2)}) collective-permute-start(f32[32,128]{1,0:T(8,128)S(1)} %added.3.refs_0_), channel_id=1, source_target_pairs={{0,16},{1,9},{8,24},{9,1},{16,0},{17,25},{24,8},{25,17},{2,18},{3,... | collective-permute-start | bytes 49160 | tf_op jit(solution)/shard_map/ppermute | solution.py:765
  102.0 7.8 %collective-permute-start.28 = (bf16[128,512]{1,0:T(8,128)(2,1)S(1)}, bf16[128,512]{1,0:T(8,128)(2,1)S(1)}, u32[]{:S(2)}, u32[]{:S(2)}) collective-permute-start(bf16[128,512]{1,0:T(8,128)(2,1)S(1)} %get-tuple-element.64), channel_id=1, source_target_pairs={{2,0},{4,2},{6,4},{3,1},{5,3},{7,5},{10,8},{12,10},{14,12},{11,9},... | collective-permute-start | bytes 393224 | tf_op jit(solution)/shard_map/ppermute | solution.py:877
  104.3 7.4 %collective-permute-start.32 = (bf16[128,512]{1,0:T(8,128)(2,1)}, bf16[128,512]{1,0:T(8,128)(2,1)S(1)}, u32[]{:S(2)}, u32[]{:S(2)}) collective-permute-start(bf16[128,512]{1,0:T(8,128)(2,1)} %get-tuple-element.69), channel_id=1, source_target_pairs={{2,0},{4,2},{6,4},{3,1},{5,3},{7,5},{10,8},{12,10},{14,12},{11,9},... | collective-permute-start | bytes 393224 | tf_op jit(solution)/shard_map/ppermute | solution.py:877
  112.4 7.8 %collective-permute-start.33 = (bf16[128,512]{1,0:T(8,128)(2,1)}, bf16[128,512]{1,0:T(8,128)(2,1)S(1)}, u32[]{:S(2)}, u32[]{:S(2)}) collective-permute-start(bf16[128,512]{1,0:T(8,128)(2,1)} %get-tuple-element.71), channel_id=1, source_target_pairs={{2,0},{4,2},{6,4},{3,1},{5,3},{7,5},{10,8},{12,10},{14,12},{11,9},... | collective-permute-start | bytes 393224 | tf_op jit(solution)/shard_map/ppermute | solution.py:877
  113.7 8.0 %collective-permute-start.31 = (bf16[128,512]{1,0:T(8,128)(2,1)}, bf16[128,512]{1,0:T(8,128)(2,1)S(1)}, u32[]{:S(2)}, u32[]{:S(2)}) collective-permute-start(bf16[128,512]{1,0:T(8,128)(2,1)} %get-tuple-element.68), channel_id=1, source_target_pairs={{2,0},{4,2},{6,4},{3,1},{5,3},{7,5},{10,8},{12,10},{14,12},{11,9},... | collective-permute-start | bytes 393224 | tf_op jit(solution)/shard_map/ppermute | solution.py:877
  (13 other events, 96.2 us)

commit v2 on v0

--- a/solution.py
+++ b/solution.py
@@ -170,7 +170,8 @@
         name="project",
     )(
         place,
-        *parts,
+        in_hbm(parts[0]),
+        *[in_vmem(part) for part in parts[1:]],
         in_hbm(cotangent),
         gain,
         in_hbm(w_layer),
@@ -872,9 +873,8 @@
         arrived = lowered(leaving)
         if tick < ticks - 1:
             for i, cols in enumerate(streams):
-                leaving[i], pair = join(
-                    index(tick), arrived[i], pair, cols, after.get(tick, [])
-                )
+                waits = after.get(tick, []) if tick < ticks - 2 or i == STREAMS - 1 else []
+                leaving[i], pair = join(index(tick), arrived[i], pair, cols, waits)
         if tick == 1:
             rows = [hold(array, leaving) for array in rows]
             rows = rows + [handed(array, r) for r in range(1, groups) for array in rows]

time: 122 us -> 122 us (level)
    unnamed x27 -> x25, local copies, waits for them, and re-layouts: 3.85 us -> 2.8 us
  transfers between devices with their start and end apart: 34 -> 34, of which waited for: 23 -> 23; matrix products, arithmetic and copies ran while one was open for 2% -> 2% of each run, Pallas kernels for 18% -> 19%
where the time goes in v2:
time: 122 us; the launch traced here: 121 us
  starting transfers between devices  48.4 us (40%)
  waiting for transfers between devices  36.4 us (30%)
  Pallas kernels  31 us (25%)
  local copies, waits for them, and re-layouts  4.03 us (3%)
  between operations  1.22 us (1%)
    ppermute x12, waiting for transfers between devices, lowered(): return [lax.ppermute(array, 'section', down) for array in arrays]  18.8 us
    ppermute x12, starting transfers between devices, lowered(): return [lax.ppermute(array, 'section', down) for array in arrays]  15.5 us
    ppermute x3, starting transfers between devices, raised(): lax.ppermute(array, 'section', [(i, i + by) for i in range(sections - by)])  10.7 us
    pallas_call x1, Pallas kernels, serial(): pl.pallas_call(kernel, out_shape=[pltpu.VMEM((tokens, wide + head), BF16)...  8.89 us
    ppermute x6, starting transfers between devices, swapped(): return lax.ppermute(array, ('dp', 'group'), pairs)  8.27 us
    ppermute x6, waiting for transfers between devices, swapped(): return lax.ppermute(array, ('dp', 'group'), pairs)  8.19 us
    ppermute x3, starting transfers between devices, shifted(): lax.ppermute(array, 'section', [(i, (i + by) % sections) for i in range(s...  7.12 us
    ppermute x3, waiting for transfers between devices, facing(): lax.ppermute(array, 'section', [(i, i ^ by) for i in range(sections)])  5.71 us
  transfers between devices with their start and end apart: 34, of which 23 were waited for; matrix products, arithmetic and copies ran while one was open for 2% of the time, Pallas kernels for 19%

profile of v2, /device:TPU:0, one launch (start us, length us, event | category | flops | bytes accessed | tf_op | source)
XLA Modules:
  0.0 121.4 jit_solution(911374280191077817)
XLA Ops:
  1.4 2.7 %pick.1 = (bf16[16,4096]{1,0:T(8,128)(2,1)}, bf16[4,16,4096]{2,1,0:T(8,128)(2,1)}, bf16[4,16,4096]{2,1,0:T(8,128)(2,1)}) custom-call(s32[1,8]{1,0:T(1,128)S(1)} %copy-done.9, s32[1]{0:T(128)} %bitcast.9.place_ref, s32[1]{0:T(128)} %bitcast.10.mine_ref, bf16[8,16,4096]{2,1,0:T(8,128)(2,1)} %bitcast.44, bf16[128,4096]{1,0:T(8,128)(2,1)} %bitcast.38), custom_call_target="tpu_custom_call" | custom-call | tf_op jit(solution)/shard_map/pick/pallas_call | solution.py:87
  4.1 7.0 %collective-permute-start.1 = (bf16[16,4096]{1,0:T(8,128)(2,1)}, bf16[16,4096]{1,0:T(8,128)(2,1)S(1)}, u32[]{:S(2)}, u32[]{:S(2)}) collective-permute-start(bf16[16,4096]{1,0:T(8,128)(2,1)} %get-tuple-element.42.refs_3_), channel_id=1, source_target_pairs={{0,6},{1,7},{8,14},{9,15},{16,22},{17,23},{24,30},{25,31}} | collective-permute-start | bytes 393224 | tf_op jit(solution)/shard_map/ppermute | solution.py:738
  11.1 1.3 %collective-permute-start.2 = (bf16[16,4096]{1,0:T(8,128)(2,1)}, bf16[16,4096]{1,0:T(8,128)(2,1)S(1)}, u32[]{:S(2)}, u32[]{:S(2)}) collective-permute-start(bf16[16,4096]{1,0:T(8,128)(2,1)} %get-tuple-element.42.refs_3_), channel_id=1, source_target_pairs={{0,4},{2,6},{1,5},{3,7},{8,12},{10,14},{9,13},{11,15},{16,20},{18,... | collective-permute-start | bytes 393224 | tf_op jit(solution)/shard_map/ppermute | solution.py:738
  12.4 2.5 %collective-permute-start.3 = (bf16[16,4096]{1,0:T(8,128)(2,1)}, bf16[16,4096]{1,0:T(8,128)(2,1)S(1)}, u32[]{:S(2)}, u32[]{:S(2)}) collective-permute-start(bf16[16,4096]{1,0:T(8,128)(2,1)} %get-tuple-element.42.refs_3_), channel_id=1, source_target_pairs={{0,2},{2,4},{4,6},{1,3},{3,5},{5,7},{8,10},{10,12},{12,14},{9,11},... | collective-permute-start | bytes 393224 | tf_op jit(solution)/shard_map/ppermute | solution.py:738
  17.8 3.8 %project.1 = (bf16[128,4096]{1,0:T(8,128)(2,1)}, bf16[128,640]{1,0:T(8,128)(2,1)S(1)}, f32[128,1]{1,0:T(8,128)S(1)}) custom-call(s32[1]{0:T(128)} %bitcast.9.place_ref, bf16[64,4096]{1,0:T(8,128)(2,1)} %bitcast.45, bf16[64,4096]{1,0:T(8,128)(2,1)S(1)} %bitcast.30, bf16[128,4096]{1,0:T(8,128)(2,1)} %c_ref.1, f32[1,4096]{1,0:T(1,128)S(1)} %copy-done.5, ...), custom_call_target="tpu_custom_call" | custom-call | tf_op jit(solution)/shard_map/project/pallas_call | solution.py:150
  21.6 3.4 %couple.1 = (bf16[16,1152]{1,0:T(8,128)(2,1)S(1)}, bf16[3,16,4096]{2,1,0:T(8,128)(2,1)}) custom-call(s32[1]{0:T(128)} %bitcast.16.last_ref, bf16[16,4096]{1,0:T(8,128)(2,1)S(1)} %collective-permute-done.1.refs_0_, bf16[16,4096]{1,0:T(8,128)(2,1)S(1)} %collective-permute-done.2.refs_1_, bf16[16,4096]{1,0:T(8,128)(2,1)S(1)} %collective-permute-done.3.refs_2_, ...), custom_call_target="tpu_custom_call" | custom-call | tf_op jit(solution)/shard_map/couple/pallas_call | solution.py:233
  25.1 2.4 %collective-permute-start.5 = (bf16[16,1152]{1,0:T(8,128)(2,1)S(1)}, bf16[16,1152]{1,0:T(8,128)(2,1)S(1)}, u32[]{:S(2)}, u32[]{:S(2)}) collective-permute-start(bf16[16,1152]{1,0:T(8,128)(2,1)S(1)} %get-tuple-element.43.refs_0_), channel_id=1, source_target_pairs={{0,2},{2,4},{4,6},{6,0},{1,3},{3,5},{5,7},{7,1},{8,10},{10,12},{12... | collective-permute-start | bytes 110600 | tf_op jit(solution)/shard_map/ppermute | solution.py:733
  27.5 1.9 %collective-permute-start.6 = (bf16[16,1152]{1,0:T(8,128)(2,1)S(1)}, bf16[16,1152]{1,0:T(8,128)(2,1)S(1)}, u32[]{:S(2)}, u32[]{:S(2)}) collective-permute-start(bf16[16,1152]{1,0:T(8,128)(2,1)S(1)} %get-tuple-element.43.refs_0_), channel_id=1, source_target_pairs={{0,4},{2,6},{4,0},{6,2},{1,5},{3,7},{5,1},{7,3},{8,12},{10,14},{12... | collective-permute-start | bytes 110600 | tf_op jit(solution)/shard_map/ppermute | solution.py:733
  29.4 2.8 %collective-permute-start.7 = (bf16[16,1152]{1,0:T(8,128)(2,1)S(1)}, bf16[16,1152]{1,0:T(8,128)(2,1)S(1)}, u32[]{:S(2)}, u32[]{:S(2)}) collective-permute-start(bf16[16,1152]{1,0:T(8,128)(2,1)S(1)} %get-tuple-element.43.refs_0_), channel_id=1, source_target_pairs={{0,6},{2,0},{4,2},{6,4},{1,7},{3,1},{5,3},{7,5},{8,14},{10,8},{12,... | collective-permute-start | bytes 110600 | tf_op jit(solution)/shard_map/ppermute | solution.py:733
  32.2 1.5 %collective-permute-start.18 = (bf16[1,3,16,4096]{3,2,1,0:T(8,128)(2,1)}, bf16[1,3,16,4096]{3,2,1,0:T(8,128)(2,1)S(1)}, u32[]{:S(2)}, u32[]{:S(2)}) collective-permute-start(bf16[1,3,16,4096]{3,2,1,0:T(8,128)(2,1)} %bitcast.31), channel_id=1, source_target_pairs={{0,8},{1,17},{8,0},{9,25},{16,24},{17,1},{24,16},{25,9},{2,10},{3,... | collective-permute-start | bytes 1179656 | tf_op jit(solution)/shard_map/ppermute | solution.py:749
  34.8 4.0 %collective-permute-start.9 = (bf16[128,640]{1,0:T(8,128)(2,1)S(1)}, bf16[128,640]{1,0:T(8,128)(2,1)S(1)}, u32[]{:S(2)}, u32[]{:S(2)}) collective-permute-start(bf16[128,640]{1,0:T(8,128)(2,1)S(1)} %hold.4.refs_0_), channel_id=1, source_target_pairs={{0,4},{2,6},{4,0},{6,2},{1,5},{3,7},{5,1},{7,3},{8,12},{10,14},{12... | collective-permute-start | bytes 491528 | tf_op jit(solution)/shard_map/ppermute | solution.py:833
  38.8 1.5 %collective-permute-start.11 = (bf16[1,16,3072]{2,1,0:T(8,128)(2,1)S(1)}, bf16[1,16,3072]{2,1,0:T(8,128)(2,1)S(1)}, u32[]{:S(2)}, u32[]{:S(2)}) collective-permute-start(bf16[1,16,3072]{2,1,0:T(8,128)(2,1)S(1)} %compact.1.first_ref), channel_id=1, source_target_pairs={{0,8},{1,17},{8,0},{9,25},{16,24},{17,1},{24,16},{25,9},{2,10},{3,... | collective-permute-start | bytes 294920 | tf_op jit(solution)/shard_map/ppermute | solution.py:749
  40.3 3.7 %collective-permute-done.11.second_ref = bf16[1,16,3072]{2,1,0:T(8,128)(2,1)S(1)} collective-permute-done((bf16[1,16,3072]{2,1,0:T(8,128)(2,1)S(1)}, bf16[1,16,3072]{2,1,0:T(8,128)(2,1)S(1)}, u32[]{:S(2)}, u32[]{:S(2)}) %collective-permute-start.11) | collective-permute-done | bytes 98336 | tf_op jit(solution)/shard_map/ppermute | solution.py:749
  44.7 1.6 %collective-permute-start.12 = (bf16[2,16,3072]{2,1,0:T(8,128)(2,1)S(1)}, bf16[2,16,3072]{2,1,0:T(8,128)(2,1)S(1)}, u32[]{:S(2)}, u32[]{:S(2)}) collective-permute-start(bf16[2,16,3072]{2,1,0:T(8,128)(2,1)S(1)} %merge.1.refs_4_), channel_id=1, source_target_pairs={{0,16},{1,9},{8,24},{9,1},{16,0},{17,25},{24,8},{25,17},{2,18},{3,... | collective-permute-start | bytes 589832 | tf_op jit(solution)/shard_map/ppermute | solution.py:749
  46.5 5.0 %collective-permute-done.10.refs_1_.refs_3_ = bf16[128,640]{1,0:T(8,128)(2,1)S(1)} collective-permute-done((bf16[128,640]{1,0:T(8,128)(2,1)S(1)}, bf16[128,640]{1,0:T(8,128)(2,1)S(1)}, u32[]{:S(2)}, u32[]{:S(2)}) %collective-permute-start.10) | collective-permute-done | bytes 163872 | tf_op jit(solution)/shard_map/ppermute | solution.py:833
  54.3 8.9 %serial.1 = (bf16[128,512]{1,0:T(8,128)(2,1)S(1)}, f32[128,1]{1,0:T(8,128)S(1)}, bf16[128,384]{1,0:T(8,128)(2,1)S(1)}, bf16[128,512]{1,0:T(8,128)(2,1)}, bf16[128,512]{1,0:T(8,128)(2,1)}) custom-call(s32[1]{0:T(128)} %bitcast.6.s_ref, s32[8]{0:T(128)S(1)} %pad_add_fusion.refs_8_.p_ref, bf16[128,640]{1,0:T(8,128)(2,1)S(1)} %hold.4.refs_0_, ...), custom_call_target="tpu_custom_call" | custom-call | tf_op jit(solution)/shard_map/serial/pallas_call | solution.py:443
  65.1 1.3 %collective-permute-start.17 = (bf16[128,512]{1,0:T(8,128)(2,1)}, bf16[128,512]{1,0:T(8,128)(2,1)S(1)}, u32[]{:S(2)}, u32[]{:S(2)}) collective-permute-start(bf16[128,512]{1,0:T(8,128)(2,1)} %get-tuple-element.49), channel_id=1, source_target_pairs={{2,0},{4,2},{6,4},{3,1},{5,3},{7,5},{10,8},{12,10},{14,12},{11,9},... | collective-permute-start | bytes 393224 | tf_op jit(solution)/shard_map/ppermute | solution.py:868
  66.4 3.8 %widen.1 = (bf16[128,4096]{1,0:T(8,128)(2,1)}, bf16[2,4,128,1024]{3,2,1,0:T(8,128)(2,1)S(1)}) custom-call(bf16[128,512]{1,0:T(8,128)(2,1)S(1)} %get-tuple-element.46.v_ref, f32[1,4096]{1,0:T(1,128)S(1)} %copy-done.5, bf16[4096,384]{1,0:T(8,128)(2,1)} %bitcast.37, bf16[128,4096]{1,0:T(8,128)(2,1)} %bitcast.42), custom_call_target="tpu_custom_call" | custom-call | tf_op jit(solution)/shard_map/widen/pallas_call | solution.py:540
  70.2 2.0 %collective-permute-done.15.r_ref = bf16[128,512]{1,0:T(8,128)(2,1)S(1)} collective-permute-done((bf16[128,512]{1,0:T(8,128)(2,1)}, bf16[128,512]{1,0:T(8,128)(2,1)S(1)}, u32[]{:S(2)}, u32[]{:S(2)}) %collective-permute-start.15) | collective-permute-done | bytes 131104 | tf_op jit(solution)/shard_map/ppermute | solution.py:868
  72.3 2.1 %collective-permute-done.17.r_ref = bf16[128,512]{1,0:T(8,128)(2,1)S(1)} collective-permute-done((bf16[128,512]{1,0:T(8,128)(2,1)}, bf16[128,512]{1,0:T(8,128)(2,1)S(1)}, u32[]{:S(2)}, u32[]{:S(2)}) %collective-permute-start.17) | collective-permute-done | bytes 131104 | tf_op jit(solution)/shard_map/ppermute | solution.py:868
  76.3 1.3 %collective-permute-start.23 = (bf16[128,512]{1,0:T(8,128)(2,1)S(1)}, bf16[128,512]{1,0:T(8,128)(2,1)S(1)}, u32[]{:S(2)}, u32[]{:S(2)}) collective-permute-start(bf16[128,512]{1,0:T(8,128)(2,1)S(1)} %get-tuple-element.57.refs_2_), channel_id=1, source_target_pairs={{2,0},{4,2},{6,4},{3,1},{5,3},{7,5},{10,8},{12,10},{14,12},{11,9},... | collective-permute-start | bytes 393224 | tf_op jit(solution)/shard_map/ppermute | solution.py:868
  78.9 4.5 %settle.1 = (bf16[4,128,1024]{2,1,0:T(8,128)(2,1)S(1)}, f32[32,128]{1,0:T(8,128)S(1)}) custom-call(s32[8]{0:T(128)S(1)} %pad_add_fusion.refs_8_.p_ref, f32[128,1]{1,0:T(8,128)S(1)} %copy-done.8, bf16[128,384]{1,0:T(8,128)(2,1)S(1)} %get-tuple-element.53.a_ref, bf16[128,4096]{1,0:T(8,128)(2,1)} %get-tuple-element.54.x_ref, bf16[128,4096]{1,0:T(8,128)(2,1)} %c_ref.1, ...), custom_call_target="tpu_custom_call" | custom-call | tf_op jit(solution)/shard_map/settle/pallas_call | solution.py:600
  83.4 1.3 %collective-permute-start.22 = (bf16[128,512]{1,0:T(8,128)(2,1)S(1)}, bf16[128,512]{1,0:T(8,128)(2,1)S(1)}, u32[]{:S(2)}, u32[]{:S(2)}) collective-permute-start(bf16[128,512]{1,0:T(8,128)(2,1)S(1)} %get-tuple-element.59), channel_id=1, source_target_pairs={{2,0},{4,2},{6,4},{3,1},{5,3},{7,5},{10,8},{12,10},{14,12},{11,9},... | collective-permute-start | bytes 393224 | tf_op jit(solution)/shard_map/ppermute | solution.py:868
  86.5 1.5 %collective-permute-start.24 = (f32[32,128]{1,0:T(8,128)S(1)}, f32[32,128]{1,0:T(8,128)S(1)}, u32[]{:S(2)}, u32[]{:S(2)}) collective-permute-start(f32[32,128]{1,0:T(8,128)S(1)} %stacked.1.refs_0_), channel_id=1, source_target_pairs={{0,8},{1,17},{8,0},{9,25},{16,24},{17,1},{24,16},{25,9},{2,10},{3,... | collective-permute-start | bytes 49160 | tf_op jit(solution)/shard_map/ppermute | solution.py:749
  88.1 2.3 %collective-permute-done.24.refs_1_ = f32[32,128]{1,0:T(8,128)S(1)} collective-permute-done((f32[32,128]{1,0:T(8,128)S(1)}, f32[32,128]{1,0:T(8,128)S(1)}, u32[]{:S(2)}, u32[]{:S(2)}) %collective-permute-start.24) | collective-permute-done | bytes 16416 | tf_op jit(solution)/shard_map/ppermute | solution.py:749
  90.3 2.1 %collective-permute-done.22.r_ref = bf16[128,512]{1,0:T(8,128)(2,1)S(1)} collective-permute-done((bf16[128,512]{1,0:T(8,128)(2,1)S(1)}, bf16[128,512]{1,0:T(8,128)(2,1)S(1)}, u32[]{:S(2)}, u32[]{:S(2)}) %collective-permute-start.22) | collective-permute-done | bytes 131104 | tf_op jit(solution)/shard_map/ppermute | solution.py:868
  94.5 1.3 %collective-permute-start.29 = (bf16[128,512]{1,0:T(8,128)(2,1)S(1)}, bf16[128,512]{1,0:T(8,128)(2,1)S(1)}, u32[]{:S(2)}, u32[]{:S(2)}) collective-permute-start(bf16[128,512]{1,0:T(8,128)(2,1)S(1)} %get-tuple-element.67), channel_id=1, source_target_pairs={{2,0},{4,2},{6,4},{3,1},{5,3},{7,5},{10,8},{12,10},{14,12},{11,9},... | collective-permute-start | bytes 393224 | tf_op jit(solution)/shard_map/ppermute | solution.py:868
  95.8 1.6 %collective-permute-start.27 = (f32[32,128]{1,0:T(8,128)S(1)}, f32[32,128]{1,0:T(8,128)S(1)}, u32[]{:S(2)}, u32[]{:S(2)}) collective-permute-start(f32[32,128]{1,0:T(8,128)S(1)} %added.3.refs_0_), channel_id=1, source_target_pairs={{0,16},{1,9},{8,24},{9,1},{16,0},{17,25},{24,8},{25,17},{2,18},{3,... | collective-permute-start | bytes 49160 | tf_op jit(solution)/shard_map/ppermute | solution.py:749
  97.4 2.2 %collective-permute-done.27.refs_1_ = f32[32,128]{1,0:T(8,128)S(1)} collective-permute-done((f32[32,128]{1,0:T(8,128)S(1)}, f32[32,128]{1,0:T(8,128)S(1)}, u32[]{:S(2)}, u32[]{:S(2)}) %collective-permute-start.27) | collective-permute-done | bytes 16416 | tf_op jit(solution)/shard_map/ppermute | solution.py:749
  105.4 2.9 %collective-permute-done.28.r_ref = bf16[128,512]{1,0:T(8,128)(2,1)S(1)} collective-permute-done((bf16[128,512]{1,0:T(8,128)(2,1)S(1)}, bf16[128,512]{1,0:T(8,128)(2,1)S(1)}, u32[]{:S(2)}, u32[]{:S(2)}) %collective-permute-start.28) | collective-permute-done | bytes 131104 | tf_op jit(solution)/shard_map/ppermute | solution.py:868
  114.1 4.7 %collective-permute-done.33.refs_1_ = bf16[128,512]{1,0:T(8,128)(2,1)S(1)} collective-permute-done((bf16[128,512]{1,0:T(8,128)(2,1)}, bf16[128,512]{1,0:T(8,128)(2,1)S(1)}, u32[]{:S(2)}, u32[]{:S(2)}) %collective-permute-start.33) | collective-permute-done | bytes 131104 | tf_op jit(solution)/shard_map/ppermute | solution.py:868
  118.8 1.4 %collective-permute-done.30.refs_0_ = bf16[128,512]{1,0:T(8,128)(2,1)S(1)} collective-permute-done((bf16[128,512]{1,0:T(8,128)(2,1)}, bf16[128,512]{1,0:T(8,128)(2,1)S(1)}, u32[]{:S(2)}, u32[]{:S(2)}) %collective-permute-start.30) | collective-permute-done | bytes 131104 | tf_op jit(solution)/shard_map/ppermute | solution.py:868
  (102 shorter events, 30.0 us)
Async XLA Ops:
  4.1 17.5 %collective-permute-start.1 = (bf16[16,4096]{1,0:T(8,128)(2,1)}, bf16[16,4096]{1,0:T(8,128)(2,1)S(1)}, u32[]{:S(2)}, u32[]{:S(2)}) collective-permute-start(bf16[16,4096]{1,0:T(8,128)(2,1)} %get-tuple-element.42.refs_3_), channel_id=1, source_target_pairs={{0,6},{1,7},{8,14},{9,15},{16,22},{17,23},{24,30},{25,31}} | collective-permute-start | bytes 393224 | tf_op jit(solution)/shard_map/ppermute | solution.py:738
  11.1 10.6 %collective-permute-start.2 = (bf16[16,4096]{1,0:T(8,128)(2,1)}, bf16[16,4096]{1,0:T(8,128)(2,1)S(1)}, u32[]{:S(2)}, u32[]{:S(2)}) collective-permute-start(bf16[16,4096]{1,0:T(8,128)(2,1)} %get-tuple-element.42.refs_3_), channel_id=1, source_target_pairs={{0,4},{2,6},{1,5},{3,7},{8,12},{10,14},{9,13},{11,15},{16,20},{18,... | collective-permute-start | bytes 393224 | tf_op jit(solution)/shard_map/ppermute | solution.py:738
  12.4 9.3 %collective-permute-start.3 = (bf16[16,4096]{1,0:T(8,128)(2,1)}, bf16[16,4096]{1,0:T(8,128)(2,1)S(1)}, u32[]{:S(2)}, u32[]{:S(2)}) collective-permute-start(bf16[16,4096]{1,0:T(8,128)(2,1)} %get-tuple-element.42.refs_3_), channel_id=1, source_target_pairs={{0,2},{2,4},{4,6},{1,3},{3,5},{5,7},{8,10},{10,12},{12,14},{9,11},... | collective-permute-start | bytes 393224 | tf_op jit(solution)/shard_map/ppermute | solution.py:738
  15.6 2.2 %collective-permute-start = (bf16[4,16,4096]{2,1,0:T(8,128)(2,1)}, bf16[4,16,4096]{2,1,0:T(8,128)(2,1)S(1)}, u32[]{:S(2)}, u32[]{:S(2)}) collective-permute-start(bf16[4,16,4096]{2,1,0:T(8,128)(2,1)} %get-tuple-element.40), channel_id=1, source_target_pairs={{0,1},{1,0},{2,3},{3,2},{4,5},{5,4},{6,7},{7,6},{8,9},{9,8},{10,11... | collective-permute-start | bytes 1572872 | tf_op jit(solution)/shard_map/ppermute | solution.py:754
  25.1 8.6 %collective-permute-start.5 = (bf16[16,1152]{1,0:T(8,128)(2,1)S(1)}, bf16[16,1152]{1,0:T(8,128)(2,1)S(1)}, u32[]{:S(2)}, u32[]{:S(2)}) collective-permute-start(bf16[16,1152]{1,0:T(8,128)(2,1)S(1)} %get-tuple-element.43.refs_0_), channel_id=1, source_target_pairs={{0,2},{2,4},{4,6},{6,0},{1,3},{3,5},{5,7},{7,1},{8,10},{10,12},{12... | collective-permute-start | bytes 110600 | tf_op jit(solution)/shard_map/ppermute | solution.py:733
  27.5 6.2 %collective-permute-start.6 = (bf16[16,1152]{1,0:T(8,128)(2,1)S(1)}, bf16[16,1152]{1,0:T(8,128)(2,1)S(1)}, u32[]{:S(2)}, u32[]{:S(2)}) collective-permute-start(bf16[16,1152]{1,0:T(8,128)(2,1)S(1)} %get-tuple-element.43.refs_0_), channel_id=1, source_target_pairs={{0,4},{2,6},{4,0},{6,2},{1,5},{3,7},{5,1},{7,3},{8,12},{10,14},{12... | collective-permute-start | bytes 110600 | tf_op jit(solution)/shard_map/ppermute | solution.py:733
  29.4 4.5 %collective-permute-start.7 = (bf16[16,1152]{1,0:T(8,128)(2,1)S(1)}, bf16[16,1152]{1,0:T(8,128)(2,1)S(1)}, u32[]{:S(2)}, u32[]{:S(2)}) collective-permute-start(bf16[16,1152]{1,0:T(8,128)(2,1)S(1)} %get-tuple-element.43.refs_0_), channel_id=1, source_target_pairs={{0,6},{2,0},{4,2},{6,4},{1,7},{3,1},{5,3},{7,5},{8,14},{10,8},{12,... | collective-permute-start | bytes 110600 | tf_op jit(solution)/shard_map/ppermute | solution.py:733
  32.2 19.4 %collective-permute-start.18 = (bf16[1,3,16,4096]{3,2,1,0:T(8,128)(2,1)}, bf16[1,3,16,4096]{3,2,1,0:T(8,128)(2,1)S(1)}, u32[]{:S(2)}, u32[]{:S(2)}) collective-permute-start(bf16[1,3,16,4096]{3,2,1,0:T(8,128)(2,1)} %bitcast.31), channel_id=1, source_target_pairs={{0,8},{1,17},{8,0},{9,25},{16,24},{17,1},{24,16},{25,9},{2,10},{3,... | collective-permute-start | bytes 1179656 | tf_op jit(solution)/shard_map/ppermute | solution.py:749
  33.9 10.1 %collective-permute-start.8 = (bf16[128,640]{1,0:T(8,128)(2,1)S(1)}, bf16[128,640]{1,0:T(8,128)(2,1)S(1)}, u32[]{:S(2)}, u32[]{:S(2)}) collective-permute-start(bf16[128,640]{1,0:T(8,128)(2,1)S(1)} %hold.4.refs_0_), channel_id=1, source_target_pairs={{0,2},{2,0},{4,6},{6,4},{1,3},{3,1},{5,7},{7,5},{8,10},{10,8},{12,... | collective-permute-start | bytes 491528 | tf_op jit(solution)/shard_map/ppermute | solution.py:833
  34.8 9.8 %collective-permute-start.9 = (bf16[128,640]{1,0:T(8,128)(2,1)S(1)}, bf16[128,640]{1,0:T(8,128)(2,1)S(1)}, u32[]{:S(2)}, u32[]{:S(2)}) collective-permute-start(bf16[128,640]{1,0:T(8,128)(2,1)S(1)} %hold.4.refs_0_), channel_id=1, source_target_pairs={{0,4},{2,6},{4,0},{6,2},{1,5},{3,7},{5,1},{7,3},{8,12},{10,14},{12... | collective-permute-start | bytes 491528 | tf_op jit(solution)/shard_map/ppermute | solution.py:833
  38.8 5.2 %collective-permute-start.11 = (bf16[1,16,3072]{2,1,0:T(8,128)(2,1)S(1)}, bf16[1,16,3072]{2,1,0:T(8,128)(2,1)S(1)}, u32[]{:S(2)}, u32[]{:S(2)}) collective-permute-start(bf16[1,16,3072]{2,1,0:T(8,128)(2,1)S(1)} %compact.1.first_ref), channel_id=1, source_target_pairs={{0,8},{1,17},{8,0},{9,25},{16,24},{17,1},{24,16},{25,9},{2,10},{3,... | collective-permute-start | bytes 294920 | tf_op jit(solution)/shard_map/ppermute | solution.py:749
  44.7 6.9 %collective-permute-start.12 = (bf16[2,16,3072]{2,1,0:T(8,128)(2,1)S(1)}, bf16[2,16,3072]{2,1,0:T(8,128)(2,1)S(1)}, u32[]{:S(2)}, u32[]{:S(2)}) collective-permute-start(bf16[2,16,3072]{2,1,0:T(8,128)(2,1)S(1)} %merge.1.refs_4_), channel_id=1, source_target_pairs={{0,16},{1,9},{8,24},{9,1},{16,0},{17,25},{24,8},{25,17},{2,18},{3,... | collective-permute-start | bytes 589832 | tf_op jit(solution)/shard_map/ppermute | solution.py:749
  46.3 5.3 %collective-permute-start.10 = (bf16[128,640]{1,0:T(8,128)(2,1)S(1)}, bf16[128,640]{1,0:T(8,128)(2,1)S(1)}, u32[]{:S(2)}, u32[]{:S(2)}) collective-permute-start(bf16[128,640]{1,0:T(8,128)(2,1)S(1)} %collective-permute-done.9.refs_1_.refs_2_), channel_id=1, source_target_pairs={{0,2},{2,0},{4,6},{6,4},{1,3},{3,1},{5,7},{7,5},{8,10},{10,8},{12,... | collective-permute-start | bytes 491528 | tf_op jit(solution)/shard_map/ppermute | solution.py:833
  52.0 22.4 %collective-permute-start.19 = (bf16[2,3,16,4096]{3,2,1,0:T(8,128)(2,1)S(1)}, bf16[2,3,16,4096]{3,2,1,0:T(8,128)(2,1)}, u32[]{:S(2)}, u32[]{:S(2)}) collective-permute-start(bf16[2,3,16,4096]{3,2,1,0:T(8,128)(2,1)S(1)} %gather_two.1.refs_0_), channel_id=1, source_target_pairs={{0,16},{1,9},{8,24},{9,1},{16,0},{17,25},{24,8},{25,17},{2,18},{3,... | collective-permute-start | bytes 2359304 | tf_op jit(solution)/shard_map/ppermute | solution.py:749
  52.6 1.4 %collective-permute-start.13 = (bf16[2,16,3072]{2,1,0:T(8,128)(2,1)S(1)}, bf16[2,16,3072]{2,1,0:T(8,128)(2,1)S(1)}, u32[]{:S(2)}, u32[]{:S(2)}) collective-permute-start(bf16[2,16,3072]{2,1,0:T(8,128)(2,1)S(1)} %merge.1.refs_4_), channel_id=1, source_target_pairs={{0,1},{1,0},{2,3},{3,2},{4,5},{5,4},{6,7},{7,6},{8,9},{9,8},{10,11... | collective-permute-start | bytes 589832 | tf_op jit(solution)/shard_map/ppermute | solution.py:754
  52.6 1.7 %collective-permute-start.14 = (bf16[2,16,3072]{2,1,0:T(8,128)(2,1)S(1)}, bf16[2,16,3072]{2,1,0:T(8,128)(2,1)S(1)}, u32[]{:S(2)}, u32[]{:S(2)}) collective-permute-start(bf16[2,16,3072]{2,1,0:T(8,128)(2,1)S(1)} %hold.5.refs_5_.refs_0_), channel_id=1, source_target_pairs={{0,1},{1,0},{2,3},{3,2},{4,5},{5,4},{6,7},{7,6},{8,9},{9,8},{10,11... | collective-permute-start | bytes 589832 | tf_op jit(solution)/shard_map/ppermute | solution.py:754
  63.8 8.4 %collective-permute-start.15 = (bf16[128,512]{1,0:T(8,128)(2,1)}, bf16[128,512]{1,0:T(8,128)(2,1)S(1)}, u32[]{:S(2)}, u32[]{:S(2)}) collective-permute-start(bf16[128,512]{1,0:T(8,128)(2,1)} %get-tuple-element.45), channel_id=1, source_target_pairs={{2,0},{4,2},{6,4},{3,1},{5,3},{7,5},{10,8},{12,10},{14,12},{11,9},... | collective-permute-start | bytes 393224 | tf_op jit(solution)/shard_map/ppermute | solution.py:868
  65.1 9.2 %collective-permute-start.17 = (bf16[128,512]{1,0:T(8,128)(2,1)}, bf16[128,512]{1,0:T(8,128)(2,1)S(1)}, u32[]{:S(2)}, u32[]{:S(2)}) collective-permute-start(bf16[128,512]{1,0:T(8,128)(2,1)} %get-tuple-element.49), channel_id=1, source_target_pairs={{2,0},{4,2},{6,4},{3,1},{5,3},{7,5},{10,8},{12,10},{14,12},{11,9},... | collective-permute-start | bytes 393224 | tf_op jit(solution)/shard_map/ppermute | solution.py:868
  74.4 3.2 %collective-permute-start.21 = (bf16[2,3,16,4096]{3,2,1,0:T(8,128)(2,1)}, bf16[2,3,16,4096]{3,2,1,0:T(8,128)(2,1)}, u32[]{:S(2)}, u32[]{:S(2)}) collective-permute-start(bf16[2,3,16,4096]{3,2,1,0:T(8,128)(2,1)} %hold.7.refs_1_), channel_id=1, source_target_pairs={{0,1},{1,0},{2,3},{3,2},{4,5},{5,4},{6,7},{7,6},{8,9},{9,8},{10,11... | collective-permute-start | bytes 2359304 | tf_op jit(solution)/shard_map/ppermute | solution.py:754
  74.5 3.5 %collective-permute-start.20 = (bf16[2,3,16,4096]{3,2,1,0:T(8,128)(2,1)S(1)}, bf16[2,3,16,4096]{3,2,1,0:T(8,128)(2,1)}, u32[]{:S(2)}, u32[]{:S(2)}) collective-permute-start(bf16[2,3,16,4096]{3,2,1,0:T(8,128)(2,1)S(1)} %hold.6.refs_0_), channel_id=1, source_target_pairs={{0,1},{1,0},{2,3},{3,2},{4,5},{5,4},{6,7},{7,6},{8,9},{9,8},{10,11... | collective-permute-start | bytes 2359304 | tf_op jit(solution)/shard_map/ppermute | solution.py:754
  75.0 8.4 %collective-permute-start.16 = (bf16[128,512]{1,0:T(8,128)(2,1)S(1)}, bf16[128,512]{1,0:T(8,128)(2,1)S(1)}, u32[]{:S(2)}, u32[]{:S(2)}) collective-permute-start(bf16[128,512]{1,0:T(8,128)(2,1)S(1)} %get-tuple-element.48.refs_1_), channel_id=1, source_target_pairs={{2,0},{4,2},{6,4},{3,1},{5,3},{7,5},{10,8},{12,10},{14,12},{11,9},... | collective-permute-start | bytes 393224 | tf_op jit(solution)/shard_map/ppermute | solution.py:868
  76.3 8.9 %collective-permute-start.23 = (bf16[128,512]{1,0:T(8,128)(2,1)S(1)}, bf16[128,512]{1,0:T(8,128)(2,1)S(1)}, u32[]{:S(2)}, u32[]{:S(2)}) collective-permute-start(bf16[128,512]{1,0:T(8,128)(2,1)S(1)} %get-tuple-element.57.refs_2_), channel_id=1, source_target_pairs={{2,0},{4,2},{6,4},{3,1},{5,3},{7,5},{10,8},{12,10},{14,12},{11,9},... | collective-permute-start | bytes 393224 | tf_op jit(solution)/shard_map/ppermute | solution.py:868
  83.4 9.0 %collective-permute-start.22 = (bf16[128,512]{1,0:T(8,128)(2,1)S(1)}, bf16[128,512]{1,0:T(8,128)(2,1)S(1)}, u32[]{:S(2)}, u32[]{:S(2)}) collective-permute-start(bf16[128,512]{1,0:T(8,128)(2,1)S(1)} %get-tuple-element.59), channel_id=1, source_target_pairs={{2,0},{4,2},{6,4},{3,1},{5,3},{7,5},{10,8},{12,10},{14,12},{11,9},... | collective-permute-start | bytes 393224 | tf_op jit(solution)/shard_map/ppermute | solution.py:868
  85.2 9.3 %collective-permute-start.26 = (bf16[128,512]{1,0:T(8,128)(2,1)S(1)}, bf16[128,512]{1,0:T(8,128)(2,1)S(1)}, u32[]{:S(2)}, u32[]{:S(2)}) collective-permute-start(bf16[128,512]{1,0:T(8,128)(2,1)S(1)} %get-tuple-element.63), channel_id=1, source_target_pairs={{2,0},{4,2},{6,4},{3,1},{5,3},{7,5},{10,8},{12,10},{14,12},{11,9},... | collective-permute-start | bytes 393224 | tf_op jit(solution)/shard_map/ppermute | solution.py:868
  86.5 3.8 %collective-permute-start.24 = (f32[32,128]{1,0:T(8,128)S(1)}, f32[32,128]{1,0:T(8,128)S(1)}, u32[]{:S(2)}, u32[]{:S(2)}) collective-permute-start(f32[32,128]{1,0:T(8,128)S(1)} %stacked.1.refs_0_), channel_id=1, source_target_pairs={{0,8},{1,17},{8,0},{9,25},{16,24},{17,1},{24,16},{25,9},{2,10},{3,... | collective-permute-start | bytes 49160 | tf_op jit(solution)/shard_map/ppermute | solution.py:749
  92.5 8.0 %collective-permute-start.25 = (bf16[128,512]{1,0:T(8,128)(2,1)S(1)}, bf16[128,512]{1,0:T(8,128)(2,1)S(1)}, u32[]{:S(2)}, u32[]{:S(2)}) collective-permute-start(bf16[128,512]{1,0:T(8,128)(2,1)S(1)} %get-tuple-element.62), channel_id=1, source_target_pairs={{2,0},{4,2},{6,4},{3,1},{5,3},{7,5},{10,8},{12,10},{14,12},{11,9},... | collective-permute-start | bytes 393224 | tf_op jit(solution)/shard_map/ppermute | solution.py:868
  94.5 7.7 %collective-permute-start.29 = (bf16[128,512]{1,0:T(8,128)(2,1)S(1)}, bf16[128,512]{1,0:T(8,128)(2,1)S(1)}, u32[]{:S(2)}, u32[]{:S(2)}) collective-permute-start(bf16[128,512]{1,0:T(8,128)(2,1)S(1)} %get-tuple-element.67), channel_id=1, source_target_pairs={{2,0},{4,2},{6,4},{3,1},{5,3},{7,5},{10,8},{12,10},{14,12},{11,9},... | collective-permute-start | bytes 393224 | tf_op jit(solution)/shard_map/ppermute | solution.py:868
  95.8 3.8 %collective-permute-start.27 = (f32[32,128]{1,0:T(8,128)S(1)}, f32[32,128]{1,0:T(8,128)S(1)}, u32[]{:S(2)}, u32[]{:S(2)}) collective-permute-start(f32[32,128]{1,0:T(8,128)S(1)} %added.3.refs_0_), channel_id=1, source_target_pairs={{0,16},{1,9},{8,24},{9,1},{16,0},{17,25},{24,8},{25,17},{2,18},{3,... | collective-permute-start | bytes 49160 | tf_op jit(solution)/shard_map/ppermute | solution.py:749
  100.5 7.7 %collective-permute-start.28 = (bf16[128,512]{1,0:T(8,128)(2,1)S(1)}, bf16[128,512]{1,0:T(8,128)(2,1)S(1)}, u32[]{:S(2)}, u32[]{:S(2)}) collective-permute-start(bf16[128,512]{1,0:T(8,128)(2,1)S(1)} %get-tuple-element.66), channel_id=1, source_target_pairs={{2,0},{4,2},{6,4},{3,1},{5,3},{7,5},{10,8},{12,10},{14,12},{11,9},... | collective-permute-start | bytes 393224 | tf_op jit(solution)/shard_map/ppermute | solution.py:868
  102.9 7.4 %collective-permute-start.31 = (bf16[128,512]{1,0:T(8,128)(2,1)}, bf16[128,512]{1,0:T(8,128)(2,1)S(1)}, u32[]{:S(2)}, u32[]{:S(2)}) collective-permute-start(bf16[128,512]{1,0:T(8,128)(2,1)} %get-tuple-element.71), channel_id=1, source_target_pairs={{2,0},{4,2},{6,4},{3,1},{5,3},{7,5},{10,8},{12,10},{14,12},{11,9},... | collective-permute-start | bytes 393224 | tf_op jit(solution)/shard_map/ppermute | solution.py:868
  110.9 7.9 %collective-permute-start.33 = (bf16[128,512]{1,0:T(8,128)(2,1)}, bf16[128,512]{1,0:T(8,128)(2,1)S(1)}, u32[]{:S(2)}, u32[]{:S(2)}) collective-permute-start(bf16[128,512]{1,0:T(8,128)(2,1)} %get-tuple-element.73), channel_id=1, source_target_pairs={{2,0},{4,2},{6,4},{3,1},{5,3},{7,5},{10,8},{12,10},{14,12},{11,9},... | collective-permute-start | bytes 393224 | tf_op jit(solution)/shard_map/ppermute | solution.py:868
  112.2 8.0 %collective-permute-start.30 = (bf16[128,512]{1,0:T(8,128)(2,1)}, bf16[128,512]{1,0:T(8,128)(2,1)S(1)}, u32[]{:S(2)}, u32[]{:S(2)}) collective-permute-start(bf16[128,512]{1,0:T(8,128)(2,1)} %get-tuple-element.70), channel_id=1, source_target_pairs={{2,0},{4,2},{6,4},{3,1},{5,3},{7,5},{10,8},{12,10},{14,12},{11,9},... | collective-permute-start | bytes 393224 | tf_op jit(solution)/shard_map/ppermute | solution.py:868
  (14 other events, 113.4 us)

commit v3 on v2

--- a/solution.py
+++ b/solution.py
@@ -253,22 +253,26 @@
 
 
 def layout(sections, wide, head):
-    through, across, at = {}, {}, 0
-    for k in range(sections):
-        for j in range(k):
+    through, across, spans, at = {}, {}, {}, 0
+    for j in range(sections - 1):
+        begin = at
+        across[j, j] = slice(at, at + head)
+        at += head
+        for k in range(j + 1, sections):
             through[j, k] = slice(at, at + wide)
             at += wide
-        for j in range(k + 1 if k < sections - 1 else 0):
-            across[j, k] = slice(at, at + head)
-            at += head
-    return through, across, at
+            if k < sections - 1:
+                across[j, k] = slice(at, at + head)
+                at += head
+        spans[j] = slice(begin, at)
+    return through, across, spans, at
 
 
 def compact(parts, section, wide, head, after):
     sections = len(parts)
     count = parts[0].shape[0]
     below = (sections - 2) * wide
-    through, across, total = layout(sections, wide, head)
+    through, across, _, total = layout(sections, wide, head)
 
     def kernel(s_ref, *refs):
         part_refs, out_ref = refs[:sections], refs[-1]
@@ -324,7 +328,7 @@
     wide = 3 * head
     scale = 1.0 / math.sqrt(head)
     lead = slice(0, streams[-1].stop)
-    through_at, across_at, _ = layout(sections, wide, head)
+    through_at, across_at, spans, _ = layout(sections, wide, head)
     count, packed = pieces[0].shape[-2:]
     plane = head // count
     n_in = sections + len(pieces)
@@ -359,19 +363,16 @@
         for copy in small:
             copy.wait()
 
-        def through(j, k):
-            return table[:, :, through_at[j, k]].reshape(head, wide)
-
-        def across(j, k):
-            return table[:, :, across_at[j, k]].reshape(head, head)
+        def couplings(cols):
+            return table[:, :, cols].reshape(head, cols.stop - cols.start)
 
         allowed = mask_ref[...] > 0.5
         norm = n_ref[...]
-        rstds, tails, mixed = [], [], []
+        rstds, tails = [], []
+        projected = [xz_all[s, :, :wide].astype(F32) for s in range(sections)]
+        crossed = [xz_all[s, :, wide : wide + head].astype(F32) for s in range(sections - 1)]
         for s in range(sections):
-            proj = xz_all[s, :, :wide].astype(F32)
-            for j in range(s):
-                proj = proj + dot_nn(mixed[j], through(j, s))
+            proj = projected[s]
             rstd = lax.rsqrt(norm * (1.0 / width) + EPS)
             proj = proj * rstd
             projs[s] = proj.astype(BF16)
@@ -381,16 +382,22 @@
             soft = scores / jnp.sum(scores, axis=1, keepdims=True)
             weights[s] = soft
             mix = dot_nn(soft.astype(BF16), v).astype(BF16)
-            mixed.append(mix)
             mixes[:, s * head : (s + 1) * head] = mix
             rstds.append(rstd)
             dmix[:, s * head : (s + 1) * head] = xz_all[s, :, wide + head :].astype(F32)
             if s == sections - 1:
                 break
-            y = xz_all[s, :, wide : wide + head].astype(F32)
-            for j in range(s):
-                y = y + dot_nn(mixed[j], across(j, s))
-            tail = y + dot_nn(mix, across(s, s))
+            added_on = dot_nn(mix, couplings(spans[s]))
+
+            def part(cols, added_on=added_on, begin=spans[s].start):
+                return added_on[:, cols.start - begin : cols.stop - begin]
+
+            for k in range(s + 1, sections):
+                projected[k] = projected[k] + part(through_at[s, k])
+                if k < sections - 1:
+                    crossed[k] = crossed[k] + part(across_at[s, k])
+            y = crossed[s]
+            tail = y + part(across_at[s, s])
             norm = norm + jnp.sum(mix.astype(F32) * (y + tail), axis=1, keepdims=True)
             norm = jnp.maximum(norm, 0.0)
             tails.append(tail)
@@ -414,9 +421,12 @@
             second = (-total * mixes[:, cols].astype(F32)).astype(BF16)
             total = total + rstds[s] * rstds[s] * along * (1.0 / width)
             for j in reversed(range(s)):
-                term = dot_nt(first, through(j, s))
+                cols = through_at[j, s]
                 if s < sections - 1:
-                    term = term + dot_nt(second, across(j, s))
+                    both = jnp.concatenate([first, second], axis=1)
+                    term = dot_nt(both, couplings(slice(cols.start, across_at[j, s].stop)))
+                else:
+                    term = dot_nt(first, couplings(cols))
                 dmix[:, j * head : (j + 1) * head] += term
 
             @pl.when(mine == s)
@@ -428,8 +438,8 @@
             for r in range(1, sections - s):
 
                 @pl.when(mine == s + r)
-                def _(r=r, cols=cols):
-                    a_ref[:, (r - 1) * head : r * head] = mixes[:, cols]
+                def _(r=r, s=s):
+                    a_ref[:, (r - 1) * head : r * head] = mixes[:, s * head : (s + 1) * head]
 
         for copy in started[len(small) :]:
             copy.wait()

time: 122 us -> 122 us (level)
  no operation moved by 1% of the time
where the time goes in v3:
time: 122 us; the launch traced here: 121 us
  starting transfers between devices  48.4 us (40%)
  waiting for transfers between devices  36.5 us (30%)
  Pallas kernels  31.1 us (25%)
  local copies, waits for them, and re-layouts  4.03 us (3%)
  between operations  1.22 us (1%)
    ppermute x12, waiting for transfers between devices, lowered(): return [lax.ppermute(array, 'section', down) for array in arrays]  18.8 us
    ppermute x12, starting transfers between devices, lowered(): return [lax.ppermute(array, 'section', down) for array in arrays]  15.5 us
    ppermute x3, starting transfers between devices, raised(): lax.ppermute(array, 'section', [(i, i + by) for i in range(sections - by)])  10.7 us
    pallas_call x1, Pallas kernels, serial(): pl.pallas_call(kernel, out_shape=[pltpu.VMEM((tokens, wide + head), BF16)...  8.98 us
    ppermute x6, starting transfers between devices, swapped(): return lax.ppermute(array, ('dp', 'group'), pairs)  8.26 us
    ppermute x6, waiting for transfers between devices, swapped(): return lax.ppermute(array, ('dp', 'group'), pairs)  8.2 us
    ppermute x3, starting transfers between devices, shifted(): lax.ppermute(array, 'section', [(i, (i + by) % sections) for i in range(s...  7.12 us
    ppermute x3, waiting for transfers between devices, facing(): lax.ppermute(array, 'section', [(i, i ^ by) for i in range(sections)])  5.71 us
  transfers between devices with their start and end apart: 34, of which 23 were waited for; matrix products, arithmetic and copies ran while one was open for 2% of the time, Pallas kernels for 19%

profile of v3, /device:TPU:0, one launch (start us, length us, event | category | flops | bytes accessed | tf_op | source)
XLA Modules:
  0.0 121.5 jit_solution(4297587447495698235)
XLA Ops:
  1.4 2.7 %pick.1 = (bf16[16,4096]{1,0:T(8,128)(2,1)}, bf16[4,16,4096]{2,1,0:T(8,128)(2,1)}, bf16[4,16,4096]{2,1,0:T(8,128)(2,1)}) custom-call(s32[1,8]{1,0:T(1,128)S(1)} %copy-done.9, s32[1]{0:T(128)} %bitcast.9.place_ref, s32[1]{0:T(128)} %bitcast.10.mine_ref, bf16[8,16,4096]{2,1,0:T(8,128)(2,1)} %bitcast.44, bf16[128,4096]{1,0:T(8,128)(2,1)} %bitcast.38), custom_call_target="tpu_custom_call" | custom-call | tf_op jit(solution)/shard_map/pick/pallas_call | solution.py:87
  4.1 7.0 %collective-permute-start.1 = (bf16[16,4096]{1,0:T(8,128)(2,1)}, bf16[16,4096]{1,0:T(8,128)(2,1)S(1)}, u32[]{:S(2)}, u32[]{:S(2)}) collective-permute-start(bf16[16,4096]{1,0:T(8,128)(2,1)} %get-tuple-element.42.refs_3_), channel_id=1, source_target_pairs={{0,6},{1,7},{8,14},{9,15},{16,22},{17,23},{24,30},{25,31}} | collective-permute-start | bytes 393224 | tf_op jit(solution)/shard_map/ppermute | solution.py:748
  11.1 1.3 %collective-permute-start.2 = (bf16[16,4096]{1,0:T(8,128)(2,1)}, bf16[16,4096]{1,0:T(8,128)(2,1)S(1)}, u32[]{:S(2)}, u32[]{:S(2)}) collective-permute-start(bf16[16,4096]{1,0:T(8,128)(2,1)} %get-tuple-element.42.refs_3_), channel_id=1, source_target_pairs={{0,4},{2,6},{1,5},{3,7},{8,12},{10,14},{9,13},{11,15},{16,20},{18,... | collective-permute-start | bytes 393224 | tf_op jit(solution)/shard_map/ppermute | solution.py:748
  12.4 2.5 %collective-permute-start.3 = (bf16[16,4096]{1,0:T(8,128)(2,1)}, bf16[16,4096]{1,0:T(8,128)(2,1)S(1)}, u32[]{:S(2)}, u32[]{:S(2)}) collective-permute-start(bf16[16,4096]{1,0:T(8,128)(2,1)} %get-tuple-element.42.refs_3_), channel_id=1, source_target_pairs={{0,2},{2,4},{4,6},{1,3},{3,5},{5,7},{8,10},{10,12},{12,14},{9,11},... | collective-permute-start | bytes 393224 | tf_op jit(solution)/shard_map/ppermute | solution.py:748
  17.8 3.8 %project.1 = (bf16[128,4096]{1,0:T(8,128)(2,1)}, bf16[128,640]{1,0:T(8,128)(2,1)S(1)}, f32[128,1]{1,0:T(8,128)S(1)}) custom-call(s32[1]{0:T(128)} %bitcast.9.place_ref, bf16[64,4096]{1,0:T(8,128)(2,1)} %bitcast.45, bf16[64,4096]{1,0:T(8,128)(2,1)S(1)} %bitcast.30, bf16[128,4096]{1,0:T(8,128)(2,1)} %c_ref.1, f32[1,4096]{1,0:T(1,128)S(1)} %copy-done.5, ...), custom_call_target="tpu_custom_call" | custom-call | tf_op jit(solution)/shard_map/project/pallas_call | solution.py:150
  21.6 3.4 %couple.1 = (bf16[16,1152]{1,0:T(8,128)(2,1)S(1)}, bf16[3,16,4096]{2,1,0:T(8,128)(2,1)}) custom-call(s32[1]{0:T(128)} %bitcast.16.last_ref, bf16[16,4096]{1,0:T(8,128)(2,1)S(1)} %collective-permute-done.1.refs_0_, bf16[16,4096]{1,0:T(8,128)(2,1)S(1)} %collective-permute-done.2.refs_1_, bf16[16,4096]{1,0:T(8,128)(2,1)S(1)} %collective-permute-done.3.refs_2_, ...), custom_call_target="tpu_custom_call" | custom-call | tf_op jit(solution)/shard_map/couple/pallas_call | solution.py:233
  25.1 2.4 %collective-permute-start.5 = (bf16[16,1152]{1,0:T(8,128)(2,1)S(1)}, bf16[16,1152]{1,0:T(8,128)(2,1)S(1)}, u32[]{:S(2)}, u32[]{:S(2)}) collective-permute-start(bf16[16,1152]{1,0:T(8,128)(2,1)S(1)} %get-tuple-element.43.refs_0_), channel_id=1, source_target_pairs={{0,2},{2,4},{4,6},{6,0},{1,3},{3,5},{5,7},{7,1},{8,10},{10,12},{12... | collective-permute-start | bytes 110600 | tf_op jit(solution)/shard_map/ppermute | solution.py:743
  27.5 1.9 %collective-permute-start.6 = (bf16[16,1152]{1,0:T(8,128)(2,1)S(1)}, bf16[16,1152]{1,0:T(8,128)(2,1)S(1)}, u32[]{:S(2)}, u32[]{:S(2)}) collective-permute-start(bf16[16,1152]{1,0:T(8,128)(2,1)S(1)} %get-tuple-element.43.refs_0_), channel_id=1, source_target_pairs={{0,4},{2,6},{4,0},{6,2},{1,5},{3,7},{5,1},{7,3},{8,12},{10,14},{12... | collective-permute-start | bytes 110600 | tf_op jit(solution)/shard_map/ppermute | solution.py:743
  29.4 2.8 %collective-permute-start.7 = (bf16[16,1152]{1,0:T(8,128)(2,1)S(1)}, bf16[16,1152]{1,0:T(8,128)(2,1)S(1)}, u32[]{:S(2)}, u32[]{:S(2)}) collective-permute-start(bf16[16,1152]{1,0:T(8,128)(2,1)S(1)} %get-tuple-element.43.refs_0_), channel_id=1, source_target_pairs={{0,6},{2,0},{4,2},{6,4},{1,7},{3,1},{5,3},{7,5},{8,14},{10,8},{12,... | collective-permute-start | bytes 110600 | tf_op jit(solution)/shard_map/ppermute | solution.py:743
  32.2 1.5 %collective-permute-start.18 = (bf16[1,3,16,4096]{3,2,1,0:T(8,128)(2,1)}, bf16[1,3,16,4096]{3,2,1,0:T(8,128)(2,1)S(1)}, u32[]{:S(2)}, u32[]{:S(2)}) collective-permute-start(bf16[1,3,16,4096]{3,2,1,0:T(8,128)(2,1)} %bitcast.31), channel_id=1, source_target_pairs={{0,8},{1,17},{8,0},{9,25},{16,24},{17,1},{24,16},{25,9},{2,10},{3,... | collective-permute-start | bytes 1179656 | tf_op jit(solution)/shard_map/ppermute | solution.py:759
  34.8 4.0 %collective-permute-start.9 = (bf16[128,640]{1,0:T(8,128)(2,1)S(1)}, bf16[128,640]{1,0:T(8,128)(2,1)S(1)}, u32[]{:S(2)}, u32[]{:S(2)}) collective-permute-start(bf16[128,640]{1,0:T(8,128)(2,1)S(1)} %hold.4.refs_0_), channel_id=1, source_target_pairs={{0,4},{2,6},{4,0},{6,2},{1,5},{3,7},{5,1},{7,3},{8,12},{10,14},{12... | collective-permute-start | bytes 491528 | tf_op jit(solution)/shard_map/ppermute | solution.py:843
  38.8 1.5 %collective-permute-start.11 = (bf16[1,16,3072]{2,1,0:T(8,128)(2,1)S(1)}, bf16[1,16,3072]{2,1,0:T(8,128)(2,1)S(1)}, u32[]{:S(2)}, u32[]{:S(2)}) collective-permute-start(bf16[1,16,3072]{2,1,0:T(8,128)(2,1)S(1)} %compact.1.first_ref), channel_id=1, source_target_pairs={{0,8},{1,17},{8,0},{9,25},{16,24},{17,1},{24,16},{25,9},{2,10},{3,... | collective-permute-start | bytes 294920 | tf_op jit(solution)/shard_map/ppermute | solution.py:759
  40.3 3.7 %collective-permute-done.11.second_ref = bf16[1,16,3072]{2,1,0:T(8,128)(2,1)S(1)} collective-permute-done((bf16[1,16,3072]{2,1,0:T(8,128)(2,1)S(1)}, bf16[1,16,3072]{2,1,0:T(8,128)(2,1)S(1)}, u32[]{:S(2)}, u32[]{:S(2)}) %collective-permute-start.11) | collective-permute-done | bytes 98336 | tf_op jit(solution)/shard_map/ppermute | solution.py:759
  44.7 1.6 %collective-permute-start.12 = (bf16[2,16,3072]{2,1,0:T(8,128)(2,1)S(1)}, bf16[2,16,3072]{2,1,0:T(8,128)(2,1)S(1)}, u32[]{:S(2)}, u32[]{:S(2)}) collective-permute-start(bf16[2,16,3072]{2,1,0:T(8,128)(2,1)S(1)} %merge.1.refs_4_), channel_id=1, source_target_pairs={{0,16},{1,9},{8,24},{9,1},{16,0},{17,25},{24,8},{25,17},{2,18},{3,... | collective-permute-start | bytes 589832 | tf_op jit(solution)/shard_map/ppermute | solution.py:759
  46.5 5.0 %collective-permute-done.10.refs_1_.refs_3_ = bf16[128,640]{1,0:T(8,128)(2,1)S(1)} collective-permute-done((bf16[128,640]{1,0:T(8,128)(2,1)S(1)}, bf16[128,640]{1,0:T(8,128)(2,1)S(1)}, u32[]{:S(2)}, u32[]{:S(2)}) %collective-permute-start.10) | collective-permute-done | bytes 163872 | tf_op jit(solution)/shard_map/ppermute | solution.py:843
  54.3 9.0 %serial.1 = (bf16[128,512]{1,0:T(8,128)(2,1)S(1)}, f32[128,1]{1,0:T(8,128)S(1)}, bf16[128,384]{1,0:T(8,128)(2,1)S(1)}, bf16[128,512]{1,0:T(8,128)(2,1)}, bf16[128,512]{1,0:T(8,128)(2,1)}) custom-call(s32[1]{0:T(128)} %bitcast.6.s_ref, s32[8]{0:T(128)S(1)} %pad_add_fusion.refs_8_.p_ref, bf16[128,640]{1,0:T(8,128)(2,1)S(1)} %hold.4.refs_0_, ...), custom_call_target="tpu_custom_call" | custom-call | tf_op jit(solution)/shard_map/serial/pallas_call | solution.py:453
  65.2 1.3 %collective-permute-start.17 = (bf16[128,512]{1,0:T(8,128)(2,1)}, bf16[128,512]{1,0:T(8,128)(2,1)S(1)}, u32[]{:S(2)}, u32[]{:S(2)}) collective-permute-start(bf16[128,512]{1,0:T(8,128)(2,1)} %get-tuple-element.49), channel_id=1, source_target_pairs={{2,0},{4,2},{6,4},{3,1},{5,3},{7,5},{10,8},{12,10},{14,12},{11,9},... | collective-permute-start | bytes 393224 | tf_op jit(solution)/shard_map/ppermute | solution.py:878
  66.5 3.8 %widen.1 = (bf16[128,4096]{1,0:T(8,128)(2,1)}, bf16[2,4,128,1024]{3,2,1,0:T(8,128)(2,1)S(1)}) custom-call(bf16[128,512]{1,0:T(8,128)(2,1)S(1)} %get-tuple-element.46.v_ref, f32[1,4096]{1,0:T(1,128)S(1)} %copy-done.5, bf16[4096,384]{1,0:T(8,128)(2,1)} %bitcast.37, bf16[128,4096]{1,0:T(8,128)(2,1)} %bitcast.42), custom_call_target="tpu_custom_call" | custom-call | tf_op jit(solution)/shard_map/widen/pallas_call | solution.py:550
  70.3 2.0 %collective-permute-done.15.r_ref = bf16[128,512]{1,0:T(8,128)(2,1)S(1)} collective-permute-done((bf16[128,512]{1,0:T(8,128)(2,1)}, bf16[128,512]{1,0:T(8,128)(2,1)S(1)}, u32[]{:S(2)}, u32[]{:S(2)}) %collective-permute-start.15) | collective-permute-done | bytes 131104 | tf_op jit(solution)/shard_map/ppermute | solution.py:878
  72.4 2.1 %collective-permute-done.17.r_ref = bf16[128,512]{1,0:T(8,128)(2,1)S(1)} collective-permute-done((bf16[128,512]{1,0:T(8,128)(2,1)}, bf16[128,512]{1,0:T(8,128)(2,1)S(1)}, u32[]{:S(2)}, u32[]{:S(2)}) %collective-permute-start.17) | collective-permute-done | bytes 131104 | tf_op jit(solution)/shard_map/ppermute | solution.py:878
  76.4 1.3 %collective-permute-start.23 = (bf16[128,512]{1,0:T(8,128)(2,1)S(1)}, bf16[128,512]{1,0:T(8,128)(2,1)S(1)}, u32[]{:S(2)}, u32[]{:S(2)}) collective-permute-start(bf16[128,512]{1,0:T(8,128)(2,1)S(1)} %get-tuple-element.57.refs_2_), channel_id=1, source_target_pairs={{2,0},{4,2},{6,4},{3,1},{5,3},{7,5},{10,8},{12,10},{14,12},{11,9},... | collective-permute-start | bytes 393224 | tf_op jit(solution)/shard_map/ppermute | solution.py:878
  79.0 4.5 %settle.1 = (bf16[4,128,1024]{2,1,0:T(8,128)(2,1)S(1)}, f32[32,128]{1,0:T(8,128)S(1)}) custom-call(s32[8]{0:T(128)S(1)} %pad_add_fusion.refs_8_.p_ref, f32[128,1]{1,0:T(8,128)S(1)} %copy-done.8, bf16[128,384]{1,0:T(8,128)(2,1)S(1)} %get-tuple-element.53.a_ref, bf16[128,4096]{1,0:T(8,128)(2,1)} %get-tuple-element.54.x_ref, bf16[128,4096]{1,0:T(8,128)(2,1)} %c_ref.1, ...), custom_call_target="tpu_custom_call" | custom-call | tf_op jit(solution)/shard_map/settle/pallas_call | solution.py:610
  83.5 1.3 %collective-permute-start.22 = (bf16[128,512]{1,0:T(8,128)(2,1)S(1)}, bf16[128,512]{1,0:T(8,128)(2,1)S(1)}, u32[]{:S(2)}, u32[]{:S(2)}) collective-permute-start(bf16[128,512]{1,0:T(8,128)(2,1)S(1)} %get-tuple-element.59), channel_id=1, source_target_pairs={{2,0},{4,2},{6,4},{3,1},{5,3},{7,5},{10,8},{12,10},{14,12},{11,9},... | collective-permute-start | bytes 393224 | tf_op jit(solution)/shard_map/ppermute | solution.py:878
  85.3 1.3 %collective-permute-start.26 = (bf16[128,512]{1,0:T(8,128)(2,1)S(1)}, bf16[128,512]{1,0:T(8,128)(2,1)S(1)}, u32[]{:S(2)}, u32[]{:S(2)}) collective-permute-start(bf16[128,512]{1,0:T(8,128)(2,1)S(1)} %get-tuple-element.63), channel_id=1, source_target_pairs={{2,0},{4,2},{6,4},{3,1},{5,3},{7,5},{10,8},{12,10},{14,12},{11,9},... | collective-permute-start | bytes 393224 | tf_op jit(solution)/shard_map/ppermute | solution.py:878
  86.6 1.6 %collective-permute-start.24 = (f32[32,128]{1,0:T(8,128)S(1)}, f32[32,128]{1,0:T(8,128)S(1)}, u32[]{:S(2)}, u32[]{:S(2)}) collective-permute-start(f32[32,128]{1,0:T(8,128)S(1)} %stacked.1.refs_0_), channel_id=1, source_target_pairs={{0,8},{1,17},{8,0},{9,25},{16,24},{17,1},{24,16},{25,9},{2,10},{3,... | collective-permute-start | bytes 49160 | tf_op jit(solution)/shard_map/ppermute | solution.py:759
  88.2 2.2 %collective-permute-done.24.refs_1_ = f32[32,128]{1,0:T(8,128)S(1)} collective-permute-done((f32[32,128]{1,0:T(8,128)S(1)}, f32[32,128]{1,0:T(8,128)S(1)}, u32[]{:S(2)}, u32[]{:S(2)}) %collective-permute-start.24) | collective-permute-done | bytes 16416 | tf_op jit(solution)/shard_map/ppermute | solution.py:759
  90.4 2.1 %collective-permute-done.22.r_ref = bf16[128,512]{1,0:T(8,128)(2,1)S(1)} collective-permute-done((bf16[128,512]{1,0:T(8,128)(2,1)S(1)}, bf16[128,512]{1,0:T(8,128)(2,1)S(1)}, u32[]{:S(2)}, u32[]{:S(2)}) %collective-permute-start.22) | collective-permute-done | bytes 131104 | tf_op jit(solution)/shard_map/ppermute | solution.py:878
  95.9 1.6 %collective-permute-start.27 = (f32[32,128]{1,0:T(8,128)S(1)}, f32[32,128]{1,0:T(8,128)S(1)}, u32[]{:S(2)}, u32[]{:S(2)}) collective-permute-start(f32[32,128]{1,0:T(8,128)S(1)} %added.3.refs_0_), channel_id=1, source_target_pairs={{0,16},{1,9},{8,24},{9,1},{16,0},{17,25},{24,8},{25,17},{2,18},{3,... | collective-permute-start | bytes 49160 | tf_op jit(solution)/shard_map/ppermute | solution.py:759
  97.5 2.2 %collective-permute-done.27.refs_1_ = f32[32,128]{1,0:T(8,128)S(1)} collective-permute-done((f32[32,128]{1,0:T(8,128)S(1)}, f32[32,128]{1,0:T(8,128)S(1)}, u32[]{:S(2)}, u32[]{:S(2)}) %collective-permute-start.27) | collective-permute-done | bytes 16416 | tf_op jit(solution)/shard_map/ppermute | solution.py:759
  105.5 2.9 %collective-permute-done.28.r_ref = bf16[128,512]{1,0:T(8,128)(2,1)S(1)} collective-permute-done((bf16[128,512]{1,0:T(8,128)(2,1)S(1)}, bf16[128,512]{1,0:T(8,128)(2,1)S(1)}, u32[]{:S(2)}, u32[]{:S(2)}) %collective-permute-start.28) | collective-permute-done | bytes 131104 | tf_op jit(solution)/shard_map/ppermute | solution.py:878
  114.2 4.7 %collective-permute-done.33.refs_1_ = bf16[128,512]{1,0:T(8,128)(2,1)S(1)} collective-permute-done((bf16[128,512]{1,0:T(8,128)(2,1)}, bf16[128,512]{1,0:T(8,128)(2,1)S(1)}, u32[]{:S(2)}, u32[]{:S(2)}) %collective-permute-start.33) | collective-permute-done | bytes 131104 | tf_op jit(solution)/shard_map/ppermute | solution.py:878
  118.9 1.4 %collective-permute-done.30.refs_0_ = bf16[128,512]{1,0:T(8,128)(2,1)S(1)} collective-permute-done((bf16[128,512]{1,0:T(8,128)(2,1)}, bf16[128,512]{1,0:T(8,128)(2,1)S(1)}, u32[]{:S(2)}, u32[]{:S(2)}) %collective-permute-start.30) | collective-permute-done | bytes 131104 | tf_op jit(solution)/shard_map/ppermute | solution.py:878
  (102 shorter events, 30.0 us)
Async XLA Ops:
  4.1 17.5 %collective-permute-start.1 = (bf16[16,4096]{1,0:T(8,128)(2,1)}, bf16[16,4096]{1,0:T(8,128)(2,1)S(1)}, u32[]{:S(2)}, u32[]{:S(2)}) collective-permute-start(bf16[16,4096]{1,0:T(8,128)(2,1)} %get-tuple-element.42.refs_3_), channel_id=1, source_target_pairs={{0,6},{1,7},{8,14},{9,15},{16,22},{17,23},{24,30},{25,31}} | collective-permute-start | bytes 393224 | tf_op jit(solution)/shard_map/ppermute | solution.py:748
  11.1 10.6 %collective-permute-start.2 = (bf16[16,4096]{1,0:T(8,128)(2,1)}, bf16[16,4096]{1,0:T(8,128)(2,1)S(1)}, u32[]{:S(2)}, u32[]{:S(2)}) collective-permute-start(bf16[16,4096]{1,0:T(8,128)(2,1)} %get-tuple-element.42.refs_3_), channel_id=1, source_target_pairs={{0,4},{2,6},{1,5},{3,7},{8,12},{10,14},{9,13},{11,15},{16,20},{18,... | collective-permute-start | bytes 393224 | tf_op jit(solution)/shard_map/ppermute | solution.py:748
  12.4 9.3 %collective-permute-start.3 = (bf16[16,4096]{1,0:T(8,128)(2,1)}, bf16[16,4096]{1,0:T(8,128)(2,1)S(1)}, u32[]{:S(2)}, u32[]{:S(2)}) collective-permute-start(bf16[16,4096]{1,0:T(8,128)(2,1)} %get-tuple-element.42.refs_3_), channel_id=1, source_target_pairs={{0,2},{2,4},{4,6},{1,3},{3,5},{5,7},{8,10},{10,12},{12,14},{9,11},... | collective-permute-start | bytes 393224 | tf_op jit(solution)/shard_map/ppermute | solution.py:748
  15.6 2.2 %collective-permute-start = (bf16[4,16,4096]{2,1,0:T(8,128)(2,1)}, bf16[4,16,4096]{2,1,0:T(8,128)(2,1)S(1)}, u32[]{:S(2)}, u32[]{:S(2)}) collective-permute-start(bf16[4,16,4096]{2,1,0:T(8,128)(2,1)} %get-tuple-element.40), channel_id=1, source_target_pairs={{0,1},{1,0},{2,3},{3,2},{4,5},{5,4},{6,7},{7,6},{8,9},{9,8},{10,11... | collective-permute-start | bytes 1572872 | tf_op jit(solution)/shard_map/ppermute | solution.py:764
  25.1 8.6 %collective-permute-start.5 = (bf16[16,1152]{1,0:T(8,128)(2,1)S(1)}, bf16[16,1152]{1,0:T(8,128)(2,1)S(1)}, u32[]{:S(2)}, u32[]{:S(2)}) collective-permute-start(bf16[16,1152]{1,0:T(8,128)(2,1)S(1)} %get-tuple-element.43.refs_0_), channel_id=1, source_target_pairs={{0,2},{2,4},{4,6},{6,0},{1,3},{3,5},{5,7},{7,1},{8,10},{10,12},{12... | collective-permute-start | bytes 110600 | tf_op jit(solution)/shard_map/ppermute | solution.py:743
  27.5 6.2 %collective-permute-start.6 = (bf16[16,1152]{1,0:T(8,128)(2,1)S(1)}, bf16[16,1152]{1,0:T(8,128)(2,1)S(1)}, u32[]{:S(2)}, u32[]{:S(2)}) collective-permute-start(bf16[16,1152]{1,0:T(8,128)(2,1)S(1)} %get-tuple-element.43.refs_0_), channel_id=1, source_target_pairs={{0,4},{2,6},{4,0},{6,2},{1,5},{3,7},{5,1},{7,3},{8,12},{10,14},{12... | collective-permute-start | bytes 110600 | tf_op jit(solution)/shard_map/ppermute | solution.py:743
  29.4 4.5 %collective-permute-start.7 = (bf16[16,1152]{1,0:T(8,128)(2,1)S(1)}, bf16[16,1152]{1,0:T(8,128)(2,1)S(1)}, u32[]{:S(2)}, u32[]{:S(2)}) collective-permute-start(bf16[16,1152]{1,0:T(8,128)(2,1)S(1)} %get-tuple-element.43.refs_0_), channel_id=1, source_target_pairs={{0,6},{2,0},{4,2},{6,4},{1,7},{3,1},{5,3},{7,5},{8,14},{10,8},{12,... | collective-permute-start | bytes 110600 | tf_op jit(solution)/shard_map/ppermute | solution.py:743
  32.2 19.4 %collective-permute-start.18 = (bf16[1,3,16,4096]{3,2,1,0:T(8,128)(2,1)}, bf16[1,3,16,4096]{3,2,1,0:T(8,128)(2,1)S(1)}, u32[]{:S(2)}, u32[]{:S(2)}) collective-permute-start(bf16[1,3,16,4096]{3,2,1,0:T(8,128)(2,1)} %bitcast.31), channel_id=1, source_target_pairs={{0,8},{1,17},{8,0},{9,25},{16,24},{17,1},{24,16},{25,9},{2,10},{3,... | collective-permute-start | bytes 1179656 | tf_op jit(solution)/shard_map/ppermute | solution.py:759
  33.9 10.1 %collective-permute-start.8 = (bf16[128,640]{1,0:T(8,128)(2,1)S(1)}, bf16[128,640]{1,0:T(8,128)(2,1)S(1)}, u32[]{:S(2)}, u32[]{:S(2)}) collective-permute-start(bf16[128,640]{1,0:T(8,128)(2,1)S(1)} %hold.4.refs_0_), channel_id=1, source_target_pairs={{0,2},{2,0},{4,6},{6,4},{1,3},{3,1},{5,7},{7,5},{8,10},{10,8},{12,... | collective-permute-start | bytes 491528 | tf_op jit(solution)/shard_map/ppermute | solution.py:843
  34.8 9.8 %collective-permute-start.9 = (bf16[128,640]{1,0:T(8,128)(2,1)S(1)}, bf16[128,640]{1,0:T(8,128)(2,1)S(1)}, u32[]{:S(2)}, u32[]{:S(2)}) collective-permute-start(bf16[128,640]{1,0:T(8,128)(2,1)S(1)} %hold.4.refs_0_), channel_id=1, source_target_pairs={{0,4},{2,6},{4,0},{6,2},{1,5},{3,7},{5,1},{7,3},{8,12},{10,14},{12... | collective-permute-start | bytes 491528 | tf_op jit(solution)/shard_map/ppermute | solution.py:843
  38.8 5.2 %collective-permute-start.11 = (bf16[1,16,3072]{2,1,0:T(8,128)(2,1)S(1)}, bf16[1,16,3072]{2,1,0:T(8,128)(2,1)S(1)}, u32[]{:S(2)}, u32[]{:S(2)}) collective-permute-start(bf16[1,16,3072]{2,1,0:T(8,128)(2,1)S(1)} %compact.1.first_ref), channel_id=1, source_target_pairs={{0,8},{1,17},{8,0},{9,25},{16,24},{17,1},{24,16},{25,9},{2,10},{3,... | collective-permute-start | bytes 294920 | tf_op jit(solution)/shard_map/ppermute | solution.py:759
  44.7 6.9 %collective-permute-start.12 = (bf16[2,16,3072]{2,1,0:T(8,128)(2,1)S(1)}, bf16[2,16,3072]{2,1,0:T(8,128)(2,1)S(1)}, u32[]{:S(2)}, u32[]{:S(2)}) collective-permute-start(bf16[2,16,3072]{2,1,0:T(8,128)(2,1)S(1)} %merge.1.refs_4_), channel_id=1, source_target_pairs={{0,16},{1,9},{8,24},{9,1},{16,0},{17,25},{24,8},{25,17},{2,18},{3,... | collective-permute-start | bytes 589832 | tf_op jit(solution)/shard_map/ppermute | solution.py:759
  46.3 5.3 %collective-permute-start.10 = (bf16[128,640]{1,0:T(8,128)(2,1)S(1)}, bf16[128,640]{1,0:T(8,128)(2,1)S(1)}, u32[]{:S(2)}, u32[]{:S(2)}) collective-permute-start(bf16[128,640]{1,0:T(8,128)(2,1)S(1)} %collective-permute-done.9.refs_1_.refs_2_), channel_id=1, source_target_pairs={{0,2},{2,0},{4,6},{6,4},{1,3},{3,1},{5,7},{7,5},{8,10},{10,8},{12,... | collective-permute-start | bytes 491528 | tf_op jit(solution)/shard_map/ppermute | solution.py:843
  52.0 22.5 %collective-permute-start.19 = (bf16[2,3,16,4096]{3,2,1,0:T(8,128)(2,1)S(1)}, bf16[2,3,16,4096]{3,2,1,0:T(8,128)(2,1)}, u32[]{:S(2)}, u32[]{:S(2)}) collective-permute-start(bf16[2,3,16,4096]{3,2,1,0:T(8,128)(2,1)S(1)} %gather_two.1.refs_0_), channel_id=1, source_target_pairs={{0,16},{1,9},{8,24},{9,1},{16,0},{17,25},{24,8},{25,17},{2,18},{3,... | collective-permute-start | bytes 2359304 | tf_op jit(solution)/shard_map/ppermute | solution.py:759
  52.6 1.4 %collective-permute-start.13 = (bf16[2,16,3072]{2,1,0:T(8,128)(2,1)S(1)}, bf16[2,16,3072]{2,1,0:T(8,128)(2,1)S(1)}, u32[]{:S(2)}, u32[]{:S(2)}) collective-permute-start(bf16[2,16,3072]{2,1,0:T(8,128)(2,1)S(1)} %merge.1.refs_4_), channel_id=1, source_target_pairs={{0,1},{1,0},{2,3},{3,2},{4,5},{5,4},{6,7},{7,6},{8,9},{9,8},{10,11... | collective-permute-start | bytes 589832 | tf_op jit(solution)/shard_map/ppermute | solution.py:764
  52.6 1.7 %collective-permute-start.14 = (bf16[2,16,3072]{2,1,0:T(8,128)(2,1)S(1)}, bf16[2,16,3072]{2,1,0:T(8,128)(2,1)S(1)}, u32[]{:S(2)}, u32[]{:S(2)}) collective-permute-start(bf16[2,16,3072]{2,1,0:T(8,128)(2,1)S(1)} %hold.5.refs_5_.refs_0_), channel_id=1, source_target_pairs={{0,1},{1,0},{2,3},{3,2},{4,5},{5,4},{6,7},{7,6},{8,9},{9,8},{10,11... | collective-permute-start | bytes 589832 | tf_op jit(solution)/shard_map/ppermute | solution.py:764
  63.9 8.4 %collective-permute-start.15 = (bf16[128,512]{1,0:T(8,128)(2,1)}, bf16[128,512]{1,0:T(8,128)(2,1)S(1)}, u32[]{:S(2)}, u32[]{:S(2)}) collective-permute-start(bf16[128,512]{1,0:T(8,128)(2,1)} %get-tuple-element.45), channel_id=1, source_target_pairs={{2,0},{4,2},{6,4},{3,1},{5,3},{7,5},{10,8},{12,10},{14,12},{11,9},... | collective-permute-start | bytes 393224 | tf_op jit(solution)/shard_map/ppermute | solution.py:878
  65.2 9.2 %collective-permute-start.17 = (bf16[128,512]{1,0:T(8,128)(2,1)}, bf16[128,512]{1,0:T(8,128)(2,1)S(1)}, u32[]{:S(2)}, u32[]{:S(2)}) collective-permute-start(bf16[128,512]{1,0:T(8,128)(2,1)} %get-tuple-element.49), channel_id=1, source_target_pairs={{2,0},{4,2},{6,4},{3,1},{5,3},{7,5},{10,8},{12,10},{14,12},{11,9},... | collective-permute-start | bytes 393224 | tf_op jit(solution)/shard_map/ppermute | solution.py:878
  74.5 3.2 %collective-permute-start.21 = (bf16[2,3,16,4096]{3,2,1,0:T(8,128)(2,1)}, bf16[2,3,16,4096]{3,2,1,0:T(8,128)(2,1)}, u32[]{:S(2)}, u32[]{:S(2)}) collective-permute-start(bf16[2,3,16,4096]{3,2,1,0:T(8,128)(2,1)} %hold.7.refs_1_), channel_id=1, source_target_pairs={{0,1},{1,0},{2,3},{3,2},{4,5},{5,4},{6,7},{7,6},{8,9},{9,8},{10,11... | collective-permute-start | bytes 2359304 | tf_op jit(solution)/shard_map/ppermute | solution.py:764
  74.6 3.5 %collective-permute-start.20 = (bf16[2,3,16,4096]{3,2,1,0:T(8,128)(2,1)S(1)}, bf16[2,3,16,4096]{3,2,1,0:T(8,128)(2,1)}, u32[]{:S(2)}, u32[]{:S(2)}) collective-permute-start(bf16[2,3,16,4096]{3,2,1,0:T(8,128)(2,1)S(1)} %hold.6.refs_0_), channel_id=1, source_target_pairs={{0,1},{1,0},{2,3},{3,2},{4,5},{5,4},{6,7},{7,6},{8,9},{9,8},{10,11... | collective-permute-start | bytes 2359304 | tf_op jit(solution)/shard_map/ppermute | solution.py:764
  75.1 8.4 %collective-permute-start.16 = (bf16[128,512]{1,0:T(8,128)(2,1)S(1)}, bf16[128,512]{1,0:T(8,128)(2,1)S(1)}, u32[]{:S(2)}, u32[]{:S(2)}) collective-permute-start(bf16[128,512]{1,0:T(8,128)(2,1)S(1)} %get-tuple-element.48.refs_1_), channel_id=1, source_target_pairs={{2,0},{4,2},{6,4},{3,1},{5,3},{7,5},{10,8},{12,10},{14,12},{11,9},... | collective-permute-start | bytes 393224 | tf_op jit(solution)/shard_map/ppermute | solution.py:878
  76.4 8.9 %collective-permute-start.23 = (bf16[128,512]{1,0:T(8,128)(2,1)S(1)}, bf16[128,512]{1,0:T(8,128)(2,1)S(1)}, u32[]{:S(2)}, u32[]{:S(2)}) collective-permute-start(bf16[128,512]{1,0:T(8,128)(2,1)S(1)} %get-tuple-element.57.refs_2_), channel_id=1, source_target_pairs={{2,0},{4,2},{6,4},{3,1},{5,3},{7,5},{10,8},{12,10},{14,12},{11,9},... | collective-permute-start | bytes 393224 | tf_op jit(solution)/shard_map/ppermute | solution.py:878
  83.5 9.0 %collective-permute-start.22 = (bf16[128,512]{1,0:T(8,128)(2,1)S(1)}, bf16[128,512]{1,0:T(8,128)(2,1)S(1)}, u32[]{:S(2)}, u32[]{:S(2)}) collective-permute-start(bf16[128,512]{1,0:T(8,128)(2,1)S(1)} %get-tuple-element.59), channel_id=1, source_target_pairs={{2,0},{4,2},{6,4},{3,1},{5,3},{7,5},{10,8},{12,10},{14,12},{11,9},... | collective-permute-start | bytes 393224 | tf_op jit(solution)/shard_map/ppermute | solution.py:878
  85.3 9.3 %collective-permute-start.26 = (bf16[128,512]{1,0:T(8,128)(2,1)S(1)}, bf16[128,512]{1,0:T(8,128)(2,1)S(1)}, u32[]{:S(2)}, u32[]{:S(2)}) collective-permute-start(bf16[128,512]{1,0:T(8,128)(2,1)S(1)} %get-tuple-element.63), channel_id=1, source_target_pairs={{2,0},{4,2},{6,4},{3,1},{5,3},{7,5},{10,8},{12,10},{14,12},{11,9},... | collective-permute-start | bytes 393224 | tf_op jit(solution)/shard_map/ppermute | solution.py:878
  86.6 3.8 %collective-permute-start.24 = (f32[32,128]{1,0:T(8,128)S(1)}, f32[32,128]{1,0:T(8,128)S(1)}, u32[]{:S(2)}, u32[]{:S(2)}) collective-permute-start(f32[32,128]{1,0:T(8,128)S(1)} %stacked.1.refs_0_), channel_id=1, source_target_pairs={{0,8},{1,17},{8,0},{9,25},{16,24},{17,1},{24,16},{25,9},{2,10},{3,... | collective-permute-start | bytes 49160 | tf_op jit(solution)/shard_map/ppermute | solution.py:759
  92.6 8.0 %collective-permute-start.25 = (bf16[128,512]{1,0:T(8,128)(2,1)S(1)}, bf16[128,512]{1,0:T(8,128)(2,1)S(1)}, u32[]{:S(2)}, u32[]{:S(2)}) collective-permute-start(bf16[128,512]{1,0:T(8,128)(2,1)S(1)} %get-tuple-element.62), channel_id=1, source_target_pairs={{2,0},{4,2},{6,4},{3,1},{5,3},{7,5},{10,8},{12,10},{14,12},{11,9},... | collective-permute-start | bytes 393224 | tf_op jit(solution)/shard_map/ppermute | solution.py:878
  94.6 7.7 %collective-permute-start.29 = (bf16[128,512]{1,0:T(8,128)(2,1)S(1)}, bf16[128,512]{1,0:T(8,128)(2,1)S(1)}, u32[]{:S(2)}, u32[]{:S(2)}) collective-permute-start(bf16[128,512]{1,0:T(8,128)(2,1)S(1)} %get-tuple-element.67), channel_id=1, source_target_pairs={{2,0},{4,2},{6,4},{3,1},{5,3},{7,5},{10,8},{12,10},{14,12},{11,9},... | collective-permute-start | bytes 393224 | tf_op jit(solution)/shard_map/ppermute | solution.py:878
  95.9 3.8 %collective-permute-start.27 = (f32[32,128]{1,0:T(8,128)S(1)}, f32[32,128]{1,0:T(8,128)S(1)}, u32[]{:S(2)}, u32[]{:S(2)}) collective-permute-start(f32[32,128]{1,0:T(8,128)S(1)} %added.3.refs_0_), channel_id=1, source_target_pairs={{0,16},{1,9},{8,24},{9,1},{16,0},{17,25},{24,8},{25,17},{2,18},{3,... | collective-permute-start | bytes 49160 | tf_op jit(solution)/shard_map/ppermute | solution.py:759
  100.6 7.8 %collective-permute-start.28 = (bf16[128,512]{1,0:T(8,128)(2,1)S(1)}, bf16[128,512]{1,0:T(8,128)(2,1)S(1)}, u32[]{:S(2)}, u32[]{:S(2)}) collective-permute-start(bf16[128,512]{1,0:T(8,128)(2,1)S(1)} %get-tuple-element.66), channel_id=1, source_target_pairs={{2,0},{4,2},{6,4},{3,1},{5,3},{7,5},{10,8},{12,10},{14,12},{11,9},... | collective-permute-start | bytes 393224 | tf_op jit(solution)/shard_map/ppermute | solution.py:878
  103.0 7.4 %collective-permute-start.31 = (bf16[128,512]{1,0:T(8,128)(2,1)}, bf16[128,512]{1,0:T(8,128)(2,1)S(1)}, u32[]{:S(2)}, u32[]{:S(2)}) collective-permute-start(bf16[128,512]{1,0:T(8,128)(2,1)} %get-tuple-element.71), channel_id=1, source_target_pairs={{2,0},{4,2},{6,4},{3,1},{5,3},{7,5},{10,8},{12,10},{14,12},{11,9},... | collective-permute-start | bytes 393224 | tf_op jit(solution)/shard_map/ppermute | solution.py:878
  111.0 7.9 %collective-permute-start.33 = (bf16[128,512]{1,0:T(8,128)(2,1)}, bf16[128,512]{1,0:T(8,128)(2,1)S(1)}, u32[]{:S(2)}, u32[]{:S(2)}) collective-permute-start(bf16[128,512]{1,0:T(8,128)(2,1)} %get-tuple-element.73), channel_id=1, source_target_pairs={{2,0},{4,2},{6,4},{3,1},{5,3},{7,5},{10,8},{12,10},{14,12},{11,9},... | collective-permute-start | bytes 393224 | tf_op jit(solution)/shard_map/ppermute | solution.py:878
  112.3 8.0 %collective-permute-start.30 = (bf16[128,512]{1,0:T(8,128)(2,1)}, bf16[128,512]{1,0:T(8,128)(2,1)S(1)}, u32[]{:S(2)}, u32[]{:S(2)}) collective-permute-start(bf16[128,512]{1,0:T(8,128)(2,1)} %get-tuple-element.70), channel_id=1, source_target_pairs={{2,0},{4,2},{6,4},{3,1},{5,3},{7,5},{10,8},{12,10},{14,12},{11,9},... | collective-permute-start | bytes 393224 | tf_op jit(solution)/shard_map/ppermute | solution.py:878
  (14 other events, 113.3 us)
